TPU v7x, 512 devices: a whole 4x8x8 slice. The times are simulated.
512 devices in a mesh: gx: 32 (over y, z_lo, core), gy: 16 (over x, z_hi).
Axes of the slice: x: 4, y: 8, z: 8 (z_hi: 4, z_lo: 2; z = z_hi * 2 + z_lo), core: 2. Of those that a mesh axis runs over, the one named last changes fastest.
Arguments:
- checkpoint: float32 [512, 512, 256], P('gx', 'gy'), may hold values from -4 to 4
- terminal_adjoint: float32 [512, 512, 256], P('gx', 'gy'), may hold values from -6 to 6
- diffusivity: float32 [512, 512, 256], P('gx', 'gy'), may hold values from 0.3 to 2
- controls: float32 [4, 4096], P(None, ('gx', 'gy')), may hold values from -5 to 5
- owner_map: int32 [4096], replicated, may hold values from 0 to 4095, each once
- act_ids: int32 [8192], P(('gx', 'gy')), may hold values from 0 to 4095, as said below
- slot_tiles: int32 [8192], P(('gx', 'gy')), may hold values from 0 to 1023
- slot_count: int32 [512], P(('gx', 'gy')), may hold values from 0 to 16, as said below
- free_list: int32 [4, 2048], replicated, may hold values from 0 to 4095, as said below
Outputs:
- start_adjoint: float32 [512, 512, 256], P('gx', 'gy')
- gradient: float32 [4, 4096], P(None, ('gx', 'gy'))
Inputs may be any that keep to these rules, and one draw needn't show every extreme that they name: `act_ids`: over all devices the live slots name every actuator exactly once; entries of slots that are not live are arbitrary actuators. `slot_count`: counts sum to 4096; some device has 16 live slots. `free_list`: each row names distinct actuators.
All inputs are finite; a program needn't handle non-finite values.
Results may differ from a plain program's by a relative error of at most 0.0001.
Values sent between devices are 32-bit elements; how exact they have to be, the bound alone decides.
No kernel may reach another device: no remote copies, remote signals or barrier semaphores. Data moves between devices by JAX's collectives and lax.ppermute only.
A program may use at most 64 MiB of HBM per device.

v0:
```python
import jax
import jax.numpy as jnp
from jax import lax
from jax.sharding import PartitionSpec as P

TZ = 128


time_step = 0.05
velocity = (1.0, 0.7, 0.4)


def extended(shard, sides, width):
    for axis, dim in sides:
        size, length = (lax.axis_size(axis), shard.shape[dim])
        up = [(i, (i + 1) % size) for i in range(size - 1)]
        down = [(j, i) for i, j in up]
        last = lax.slice_in_dim(shard, length - width, length, axis=dim)
        leading = lax.slice_in_dim(shard, 0, width, axis=dim)
        before = lax.ppermute(last, axis, up)
        after = lax.ppermute(leading, axis, down)
        shard = jnp.concatenate([before, shard, after], axis=dim)
    return shard


def interior(padded, axis, offset):
    window = [slice(1, -1), slice(1, -1), slice(1, -1)]
    window[axis] = slice(1 + offset, padded.shape[axis] - 1 + offset)
    return padded[tuple(window)]


def evolve(padded, field, kappa, source):
    laplace = -6.0 * field
    advection = jnp.zeros_like(field)
    flux = 0.5 * padded * padded
    for axis in range(3):
        laplace = laplace + interior(padded, axis, 1) + interior(padded, axis, -1)
        advection = advection + velocity[axis] * 0.5 * (
            interior(flux, axis, 1) - interior(flux, axis, -1)
        )
    return field + time_step * (kappa * laplace - advection + source)


def pad_depth(padded):
    return jnp.pad(padded, ((0, 0), (0, 0), (1, 1)))


def advance(field, kappa, source):
    padded = extended(field, (("gx", 0), ("gy", 1)), 1)
    return evolve(pad_depth(padded), field, kappa, source)


def transpose_step(adjoint, state, adj_padded, coef_padded):
    laplace = -6.0 * interior(coef_padded, 0, 0)
    drift = jnp.zeros_like(adjoint)
    for axis in range(3):
        laplace = laplace + interior(coef_padded, axis, 1) + interior(coef_padded, axis, -1)
        drift = drift + velocity[axis] * 0.5 * (
            interior(adj_padded, axis, 1) - interior(adj_padded, axis, -1)
        )
    return adjoint + time_step * (laplace + state * drift)


def shards(
    checkpoint,
    terminal_adjoint,
    diffusivity,
    controls,
    owner_map,
    act_ids,
    slot_tiles,
    slot_count,
    free_list,
):
    size_x, size_y, size_z = checkpoint.shape
    slot_total = act_ids.shape[0]
    tile_total = size_x * size_y * (size_z // TZ)
    step_total = controls.shape[0]
    act_total = owner_map.shape[0]
    alive_mask = (jnp.arange(slot_total) < slot_count[0]).astype(jnp.float32)
    owner_slot = owner_map[act_ids]
    all_controls = lax.all_gather(controls, ("gx", "gy"), axis=1, tiled=True)
    slot_values = all_controls[:, owner_slot] * alive_mask[None, :]
    tile_onehot = (slot_tiles[:, None] == jnp.arange(tile_total)[None, :]).astype(jnp.float32)
    tile_source = jnp.dot(slot_values, tile_onehot, precision=lax.Precision.HIGHEST)
    sources = jnp.broadcast_to(
        tile_source.reshape(step_total, size_x, size_y, size_z // TZ, 1),
        (step_total, size_x, size_y, size_z // TZ, TZ),
    )
    sources = sources.reshape(step_total, size_x, size_y, size_z)
    states = []
    state = checkpoint
    for step in range(step_total):
        states.append(state)
        state = advance(state, diffusivity, sources[step])
    adjoint = terminal_adjoint
    rows = [None] * step_total
    for step in range(step_total - 1, -1, -1):
        tile_sums = jnp.sum(adjoint.reshape(tile_total, TZ), axis=-1)
        values = time_step * tile_sums[slot_tiles] * alive_mask
        dense_grad = jnp.zeros((act_total,), jnp.float32).at[owner_slot].add(values)
        rows[step] = dense_grad[None, :]
        stacked = jnp.stack([adjoint, diffusivity * adjoint])
        both_rims = extended(stacked, (("gx", 1), ("gy", 2)), 1)
        adj_padded = pad_depth(both_rims[0])
        coef_padded = pad_depth(both_rims[1])
        adjoint = transpose_step(adjoint, states[step], adj_padded, coef_padded)
    shares = lax.psum_scatter(
        jnp.concatenate(rows, axis=0), ("gx", "gy"), scatter_dimension=1, tiled=True
    )
    owned = shares.shape[1]
    flags = (
        jnp.zeros((step_total, act_total), jnp.float32)
        .at[jnp.arange(step_total)[:, None], owner_map[free_list]]
        .set(1.0)
    )
    mine = lax.dynamic_slice_in_dim(flags, lax.axis_index(("gx", "gy")) * owned, owned, 1)
    return (adjoint, shares * mine)


def solution(mesh):
    placed = (
        P("gx", "gy", None),
        P("gx", "gy", None),
        P("gx", "gy", None),
        P(None, ("gx", "gy")),
        P(),
        P(("gx", "gy")),
        P(("gx", "gy")),
        P(("gx", "gy")),
        P(),
    )
    return jax.shard_map(
        shards,
        mesh=mesh,
        in_specs=placed,
        out_specs=(P("gx", "gy", None), P(None, ("gx", "gy"))),
        check_vma=False,
    )
```

profile of v0, /device:TPU:1, one launch (start us, length us, event | category | flops | bytes accessed | tf_op | source)
XLA Modules:
  0.0 1746.2 jit_solution(12804396459599570706)
XLA Ops:
  7.3 1.3 multiply_bitcast_fusion.3
  9.3 8.8 collective-permute-start.1
  18.1 1.9 collective-permute-start
  20.0 1.9 collective-permute-start.5
  21.9 2.4 collective-permute-start.4
  24.4 1229.1 %all-gather = f32[512,8,4]{1,2,0:T(4,128)S(1)} all-gather(f32[1,8,4]{1,2,0:T(4,128)S(1)} %bitcast.75), channel_id=1, replica_groups=mesh['gx'=32,'gy'=16] {'gx','gy'}, dimensions={0}, use_global_device_ids=true | all-gather | bytes 65664 | tf_op jit(solution)/shard_map/all_gather | solution.py:82
  1253.5 4.2 copy.13
  1259.7 45.5 %gather_fusion.6 = s32[8192]{0:T(1024)S(1)} fusion(s32[4096]{0:T(1024)S(1)} %copy-done, s32[8192]{0:T(1024)S(1)} %broadcast_clamp_fusion), kind=kCustom, calls=%fused_computation.6 | custom fusion | bytes 98304 | tf_op jit(solution)/shard_map/gather | solution.py:114
  1305.2 2.2 gather_fusion.1
  1308.5 1.3 collective-permute-start.6
  1309.8 4.9 collective-permute-start.7
  1316.1 1.2 broadcast_in_dim.62
  1318.5 1.0 fusion.82
  1320.2 25.2 %collective-permute-start.8 = (f32[1,32,256]{2,1,0:T(8,128)}, f32[1,32,256]{2,1,0:T(8,128)S(1)}, u32[]{:S(2)}, u32[]{:S(2)}) collective-permute-start(f32[1,32,256]{2,1,0:T(8,128)} %get-tuple-element.50), channel_id=1, source_target_pairs={{16,0},{32,16},{48,32},{64,48},{80,64},{96,80},{112,96},{128,112},... | collective-permute-start | bytes 98312 | tf_op jit(solution)/shard_map/ppermute | solution.py:21
  1345.4 1.9 collective-permute-start.9
  1349.2 0.9 slice.527
  1350.7 1.2 broadcast_in_dim.66
  1352.0 1.3 collective-permute-start.10
  1353.3 4.9 collective-permute-start.11
  1359.0 1.3 collective-permute-start.3
  1360.3 4.9 collective-permute-start.2
  1365.7 1.0 fusion.68
  1366.8 3.5 collective-permute-start.12
  1370.3 2.0 collective-permute-start.13
  1372.4 1.1 pad_maximum_fusion
  1373.5 1.3 collective-permute-start.14
  1374.8 6.2 collective-permute-start.15
  1382.2 3.3 multiply_bitcast_fusion.2
  1385.5 3.1 collective-permute-start.17
  1388.7 3.8 collective-permute-start.16
  1393.3 1.2 reduce_sum.39
  1395.3 1.3 collective-permute-start.19
  1396.6 6.4 collective-permute-start.18
  1403.8 30.5 %scatter_custom_fusion.4 = f32[16384]{0:T(1024)S(1)} fusion(s32[8192]{0:T(1024)S(1)} %bitcast.74, f32[8192]{0:T(1024)S(1)} %broadcast.149, f32[]{:T(128)} %constant.16.clone.1), kind=kCustom, calls=%fused_computation.246 | custom fusion | bytes 65540
  1435.2 1.2 reduce_sum.38
  1437.5 0.9 multiply_bitcast_fusion.1
  1438.3 1.9 collective-permute-start.21
  1440.3 3.6 collective-permute-start.20
  1445.9 1.3 collective-permute-start.23
  1447.2 6.7 collective-permute-start.22
  1456.2 1.9 collective-permute-start.25
  1458.1 4.5 collective-permute-start.24
  1465.1 1.3 collective-permute-start.27
  1466.4 6.4 collective-permute-start.26
  1472.8 262.4 %all-reduce.14.cloned.1.call-done = f32[4,4096]{1,0:T(4,128)} async-done(((f32[4,4096]{1,0:T(4,128)}), f32[4,4096]{1,0:T(4,128)}) %all-reduce.14.cloned.1.call-update) | async-done | bytes 65552
  1735.2 1.3 dynamic-slice_multiply_fusion
  1736.9 0.9 copy-done.6
  1737.8 1.6 fusion.32
  (143 shorter events, 22.5 us)
Async XLA Ops:
  7.2 1251.1 %copy-start = (s32[4096]{0:T(1024)S(1)}, s32[4096]{0:T(1024)}, u32[]{:S(2)}) copy-start(s32[4096]{0:T(1024)} %param.13) | copy-start | bytes 49156
  7.2 1.4 copy-start.1
  7.2 12.8 copy-start.5
  7.2 17.1 copy-start.14
  7.2 1728.0 %all-reduce.14.cloned.1.call-start = ((), (), s32[]{:S(2)}) async-start(), calls=%async_computation | async-start | bytes 131072
  9.3 1348.9 %collective-permute-start.1 = (f32[2,1,32,256]{3,2,1,0:T(8,128)}, f32[2,1,32,256]{3,2,1,0:T(8,128)S(1)}, u32[]{:S(2)}, u32[]{:S(2)}) collective-permute-start(f32[2,1,32,256]{3,2,1,0:T(8,128)} %get-tuple-element.34), channel_id=1, source_target_pairs={{16,0},{32,16},{48,32},{64,48},{80,64},{96,80},{112,96},{128,112},... | collective-permute-start | bytes 196616 | tf_op jit(solution)/shard_map/ppermute | solution.py:21
  18.1 1340.2 %collective-permute-start = (f32[2,1,32,256]{3,2,1,0:T(8,128)}, f32[2,1,32,256]{3,2,1,0:T(8,128)}, u32[]{:S(2)}, u32[]{:S(2)}) collective-permute-start(f32[2,1,32,256]{3,2,1,0:T(8,128)} %get-tuple-element.33), channel_id=1, source_target_pairs={{0,16},{16,32},{32,48},{48,64},{64,80},{80,96},{96,112},{112,128},... | collective-permute-start | bytes 196616 | tf_op jit(solution)/shard_map/ppermute | solution.py:20
  20.0 1288.4 %collective-permute-start.5 = (f32[1,32,256]{2,1,0:T(8,128)S(1)}, f32[1,32,256]{2,1,0:T(8,128)S(1)}, u32[]{:S(2)}, u32[]{:S(2)}) collective-permute-start(f32[1,32,256]{2,1,0:T(8,128)S(1)} %get-tuple-element.52), channel_id=1, source_target_pairs={{0,16},{16,32},{32,48},{48,64},{64,80},{80,96},{96,112},{112,128},... | collective-permute-start | bytes 98312 | tf_op jit(solution)/shard_map/ppermute | solution.py:20
  21.9 1286.5 %collective-permute-start.4 = (f32[1,32,256]{2,1,0:T(8,128)S(1)}, f32[1,32,256]{2,1,0:T(8,128)S(1)}, u32[]{:S(2)}, u32[]{:S(2)}) collective-permute-start(f32[1,32,256]{2,1,0:T(8,128)S(1)} %get-tuple-element.51), channel_id=1, source_target_pairs={{16,0},{32,16},{48,32},{64,48},{80,64},{96,80},{112,96},{128,112},... | collective-permute-start | bytes 98312 | tf_op jit(solution)/shard_map/ppermute | solution.py:21
  1253.4 4.2 copy-start.19
  1253.4 4.2 copy-start.18
  1253.5 6.1 copy-start.11
  1259.6 48.0 %copy-start.16 = (s32[2]{0:T(128)S(1)}, s32[2]{0:T(128)}, u32[]{:S(2)}) copy-start(s32[2]{0:T(128)} %constant.81) | copy-start | bytes 28
  1308.5 8.8 collective-permute-start.6
  1309.8 7.5 collective-permute-start.7
  1317.3 1.0 copy-start.2
  1317.3 1.2 copy-start.8
  1318.5 28.8 %copy-start.15 = (s32[2]{0:T(128)S(1)}, s32[2]{0:T(128)}, u32[]{:S(2)}) copy-start(s32[2]{0:T(128)} %constant.78) | copy-start | bytes 28
  1318.5 29.5 %copy-start.12 = (f32[1024]{0:T(1024)S(1)}, f32[1024]{0:T(1024)}, u32[]{:S(2)}) copy-start(f32[1024]{0:T(1024)} %get-tuple-element.3) | copy-start | bytes 12292
  1320.2 31.8 %collective-permute-start.8 = (f32[1,32,256]{2,1,0:T(8,128)}, f32[1,32,256]{2,1,0:T(8,128)S(1)}, u32[]{:S(2)}, u32[]{:S(2)}) collective-permute-start(f32[1,32,256]{2,1,0:T(8,128)} %get-tuple-element.50), channel_id=1, source_target_pairs={{16,0},{32,16},{48,32},{64,48},{80,64},{96,80},{112,96},{128,112},... | collective-permute-start | bytes 98312 | tf_op jit(solution)/shard_map/ppermute | solution.py:21
  1345.4 6.6 collective-permute-start.9
  1352.0 13.2 collective-permute-start.10
  1353.3 11.9 collective-permute-start.11
  1359.0 13.3 collective-permute-start.3
  1360.3 12.0 collective-permute-start.2
  1366.8 6.7 collective-permute-start.12
  1370.3 3.1 collective-permute-start.13
  1373.5 7.6 collective-permute-start.14
  1374.8 6.9 collective-permute-start.15
  1381.1 1.1 copy-start.7
  1385.5 7.0 copy-start.9
  1385.5 7.0 copy-start.10
  1385.5 9.0 copy-start.13
  1385.5 9.7 collective-permute-start.17
  1388.7 6.5 collective-permute-start.16
  1395.3 41.8 %collective-permute-start.19 = (f32[2,18,1,256]{3,2,1,0:T(1,128)S(1)}, f32[2,18,1,256]{3,2,1,0:T(1,128)S(1)}, u32[]{:S(2)}, u32[]{:S(2)}) collective-permute-start(f32[2,18,1,256]{3,2,1,0:T(1,128)S(1)} %get-tuple-element.24), channel_id=1, source_target_pairs={{1,0},{2,1},{3,2},{4,3},{5,4},{6,5},{7,6},{8,7},{9,8},{10,9},{11,1... | collective-permute-start | bytes 110600 | tf_op jit(solution)/shard_map/ppermute | solution.py:21
  1396.6 40.5 %collective-permute-start.18 = (f32[2,18,1,256]{3,2,1,0:T(1,128)S(1)}, f32[2,18,1,256]{3,2,1,0:T(1,128)S(1)}, u32[]{:S(2)}, u32[]{:S(2)}) collective-permute-start(f32[2,18,1,256]{3,2,1,0:T(1,128)S(1)} %get-tuple-element.23), channel_id=1, source_target_pairs={{0,1},{1,2},{2,3},{3,4},{4,5},{5,6},{6,7},{7,8},{8,9},{9,10},{10,1... | collective-permute-start | bytes 110600 | tf_op jit(solution)/shard_map/ppermute | solution.py:20
  1438.3 6.4 copy-start.3
  1438.3 7.3 collective-permute-start.21
  1440.3 5.4 collective-permute-start.20
  1444.8 1.0 copy-start.4
  1445.9 8.8 collective-permute-start.23
  1447.2 7.7 collective-permute-start.22
  1456.2 8.9 collective-permute-start.25
  1458.1 6.9 collective-permute-start.24
  1465.1 271.5 %collective-permute-start.27 = (f32[2,18,1,256]{3,2,1,0:T(1,128)S(1)}, f32[2,18,1,256]{3,2,1,0:T(1,128)S(1)}, u32[]{:S(2)}, u32[]{:S(2)}) collective-permute-start(f32[2,18,1,256]{3,2,1,0:T(1,128)S(1)} %get-tuple-element.20), channel_id=1, source_target_pairs={{1,0},{2,1},{3,2},{4,3},{5,4},{6,5},{7,6},{8,7},{9,8},{10,9},{11,1... | collective-permute-start | bytes 110600 | tf_op jit(solution)/shard_map/ppermute | solution.py:21
  1466.4 270.2 %collective-permute-start.26 = (f32[2,18,1,256]{3,2,1,0:T(1,128)S(1)}, f32[2,18,1,256]{3,2,1,0:T(1,128)S(1)}, u32[]{:S(2)}, u32[]{:S(2)}) collective-permute-start(f32[2,18,1,256]{3,2,1,0:T(1,128)S(1)} %get-tuple-element.19), channel_id=1, source_target_pairs={{0,1},{1,2},{2,3},{3,4},{4,5},{5,6},{6,7},{7,8},{8,9},{9,10},{10,1... | collective-permute-start | bytes 110600 | tf_op jit(solution)/shard_map/ppermute | solution.py:20
  1736.8 1.0 copy-start.6
  (1 other events, 0.7 us)
Sparse Core Ops, SparseCore 0:
  1465.1 270.0 all-reduce.13
where the time goes:
time: 1750 us
  blocking collectives  1230 us (70%)
  waiting for transfers between devices  263 us (15%)
  starting transfers between devices  116 us (7%)
  local copies, waits for them, and re-layouts  96.9 us (6%)
  other arithmetic  25 us (1%)
    all_gather x1, blocking collectives, shards(): all_controls = lax.all_gather(controls, ('gx', 'gy'), axis=1, tiled=True)  1230 us
    unnamed x2, waiting for transfers between devices  262 us
    ppermute x14, starting transfers between devices, extended(): before = lax.ppermute(last, axis, up)  60 us
    ppermute x14, starting transfers between devices, extended(): after = lax.ppermute(leading, axis, down)  55.9 us
    gather x2, local copies, waits for them, and re-layouts, shards(): owner_map[free_list]  45.6 us
  transfers between devices with their start and end apart: 29, of which 3 were waited for; matrix products, arithmetic and copies ran while one was open for 6% of the time, Pallas kernels for 0%

commit v1 on v0

v1 whole, which is shorter than its diff:
```python
import functools

import jax
import jax.numpy as jnp
from jax import lax
from jax.experimental import pallas as pl
from jax.experimental.pallas import tpu as pltpu
from jax.sharding import PartitionSpec as P

TZ = 128
DT = 0.05
VEL = (1.0, 0.7, 0.4)
AXES = ("gx", "gy")

WIDE = (6, 5, 4)
LAYERS = sum(WIDE)
XO = 6
YO = 12
YR = 56
LANES = 128
POS, TIL = 32, 48


def corner_pieces():
    pieces, row = [], 0
    for field, wide in enumerate(WIDE):
        for layer in range(1, wide):
            pieces.append((field, layer, wide - layer, row))
            row += wide - layer
    return pieces, -(-row // 8) * 8


CORNER, CORNER_ROWS = corner_pieces()


def pack_kernel(
    cx, cy, ck_ref, kp_ref, ta_ref, ctl_ref, own_ref, act_ref, til_ref, cnt_ref,
    yup_ref, ydn_ref, xup_ref, xdn_ref, uu_ref, ud_ref, du_ref, dd_ref, row_ref,
):
    fields = (ck_ref, kp_ref, ta_ref)
    lane = lax.broadcasted_iota(jnp.int32, (1, LANES), 1)
    row = jnp.zeros((1, LANES), jnp.float32)
    steps, owned = ctl_ref.shape
    for n in range(steps):
        for k in range(owned):
            row = jnp.where(lane == n * owned + k, ctl_ref[n, k], row)
    for j in range(act_ref.shape[0]):
        place = jnp.where(j < cnt_ref[0], own_ref[act_ref[j]], -1)
        row = jnp.where(lane == POS + j, place.astype(jnp.float32), row)
        row = jnp.where(lane == TIL + j, til_ref[j].astype(jnp.float32), row)
    row_ref[...] = jnp.broadcast_to(row, row_ref.shape)
    halves = (slice(0, LANES), slice(LANES, 2 * LANES))
    at = 0
    for field, wide in zip(fields, WIDE):
        for i in range(wide):
            for h in range(2):
                xup_ref[at + i, h] = field[cx - wide + i, :, halves[h]]
                xdn_ref[at + i, h] = field[i, :, halves[h]]
        at += wide

    def rows(x, carry):
        at = 0
        for field, wide in zip(fields, WIDE):
            for h in range(2):
                yup_ref[x, h, at : at + wide, :] = field[x, cy - wide : cy, halves[h]]
                ydn_ref[x, h, at : at + wide, :] = field[x, 0:wide, halves[h]]
            at += wide
        return carry

    lax.fori_loop(0, cx, rows, 0)
    for f, layer, count, start in CORNER:
        for h in range(2):
            for up_x, up_y, ref in ((1, 1, uu_ref), (1, 0, ud_ref), (0, 1, du_ref), (0, 0, dd_ref)):
                x = cx - layer if up_x else layer - 1
                y = cy - count if up_y else 0
                ref[h, start : start + count, :] = fields[f][x, y : y + count, halves[h]]


def window_kernel(
    cx, cy, nx, ny, ck_ref, kp_ref, ta_ref,
    yup_ref, ydn_ref, xup_ref, xdn_ref, uu_ref, ud_ref, du_ref, dd_ref, tab_ref,
    out_ref, msg_ref,
    s0, s1, s2, s3, kap, a4, a3, a2, a1, qa, qb,
    near_v, near_s, list_s, pick_v, which_v, amp_v, sum_v, sem,
):
    gx = lax.axis_index("gx")
    gy = lax.axis_index("gy")
    me = gx * ny + gy
    halves = (slice(0, LANES), slice(LANES, 2 * LANES))
    lane = lax.broadcasted_iota(jnp.int32, (1, LANES), 1)

    order = [(0, 0)] + [(a, b) for a in (-1, 0, 1) for b in (-1, 0, 1) if (a, b) != (0, 0)]
    for i, (a, b) in enumerate(order):
        there = (gx + a >= 0) & (gx + a < nx) & (gy + b >= 0) & (gy + b < ny)
        source = jnp.where(there, me + a * ny + b, me)
        seen = tab_ref[pl.ds(source, 1), :]
        near_v[i : i + 1, :] = jnp.where(there, seen, -1.0).astype(jnp.int32)
    ids = pltpu.make_async_copy(near_v, near_s, sem)
    ids.start()

    fields = ((ck_ref, s0), (kp_ref, kap), (ta_ref, a4))
    for f, (own, ext) in enumerate(fields):
        wide, at = WIDE[f], sum(WIDE[:f])

        def assemble(x, carry, own=own, ext=ext, wide=wide, at=at):
            for h in range(2):
                ext[XO + x, h, YO : YO + cy, :] = own[x, :, halves[h]]
                ext[XO + x, h, YO - wide : YO, :] = yup_ref[x, h, at : at + wide, :]
                ext[XO + x, h, YO + cy : YO + cy + wide, :] = ydn_ref[x, h, at : at + wide, :]
            return carry

        lax.fori_loop(0, cx, assemble, 0)
        for i in range(wide):
            for h in range(2):
                ext[XO - wide + i, h, YO : YO + cy, :] = xup_ref[at + i, h]
                ext[XO + cx + i, h, YO : YO + cy, :] = xdn_ref[at + i, h]
    for f, layer, count, start in CORNER:
        ext = fields[f][1]
        for h in range(2):
            for up_x, up_y, ref in ((1, 1, uu_ref), (1, 0, ud_ref), (0, 1, du_ref), (0, 0, dd_ref)):
                x = XO - layer if up_x else XO + cx + layer - 1
                y = YO - count if up_y else YO + cy
                ext[x, h, y : y + count, :] = ref[h, start : start + count, :]

    ids.wait()
    total = jnp.int32(0)
    own_total = jnp.int32(0)
    for i, (a, b) in enumerate(order):
        for j in range(16):
            place = near_s[i, POS + j]
            tile = near_s[i, TIL + j]
            x = lax.shift_right_logical(tile, 6) + (XO + a * cx)
            y = (lax.shift_right_logical(tile, 1) & (cy - 1)) + (YO + b * cy)
            keep = place >= 0
            if a != 0:
                keep &= (x >= XO - 5) & (x < XO + cx + 5)
            if b != 0:
                keep &= (y >= YO - 5) & (y < YO + cy + 5)
            list_s[0, total] = x
            list_s[1, total] = tile & 1
            list_s[2, total] = y
            list_s[3, total] = place
            total = total + keep.astype(jnp.int32)
        if i == 0:
            own_total = total

    def pick(e, carry):
        place = list_s[3, e]
        pick_v[pl.ds(e, 1), :] = tab_ref[pl.ds(lax.shift_right_logical(place, 3), 1), :]
        which_v[pl.ds(e, 1), :] = jnp.broadcast_to(place & 7, (1, LANES))
        return carry

    lax.fori_loop(0, total, pick, 0)
    lanes = lax.broadcasted_iota(jnp.int32, pick_v.shape, 1)
    for n in range(3):
        chosen = jnp.where(lanes - 8 * n == which_v[...], pick_v[...], 0.0)
        amp_v[n] = jnp.broadcast_to(DT * jnp.sum(chosen, axis=1, keepdims=True), pick_v.shape)

    lo_x, hi_x, lo_y, hi_y = gx == 0, gx == nx - 1, gy == 0, gy == ny - 1

    def clear_outside(ref):
        @pl.when(lo_x)
        def _():
            ref[XO - 1] = jnp.zeros(ref.shape[1:], jnp.float32)

        @pl.when(hi_x)
        def _():
            ref[XO + cx] = jnp.zeros(ref.shape[1:], jnp.float32)

        @pl.when(lo_y)
        def _():
            ref[:, :, YO - 1 : YO, :] = jnp.zeros((ref.shape[0], 2, 1, LANES), jnp.float32)

        @pl.when(hi_y)
        def _():
            ref[:, :, YO + cy : YO + cy + 1, :] = jnp.zeros((ref.shape[0], 2, 1, LANES), jnp.float32)

    def depth(v0, v1):
        first = lax.broadcasted_iota(jnp.int32, v0.shape, 1) == 0
        last = lax.broadcasted_iota(jnp.int32, v0.shape, 1) == LANES - 1
        f0, f1 = pltpu.roll(v0, 1, 1), pltpu.roll(v1, 1, 1)
        b0, b1 = pltpu.roll(v0, LANES - 1, 1), pltpu.roll(v1, LANES - 1, 1)
        before = (jnp.where(first, 0.0, f0), jnp.where(first, f0, f1))
        after = (jnp.where(last, b1, b0), jnp.where(last, 0.0, b1))
        return before, after

    def forward(src, dst, lo, hi, y0, rows):
        def plane(x, carry):
            mid = [src[x, h, pl.ds(y0, rows), :] for h in range(2)]
            before, after = depth(*mid)
            for h in range(2):
                f = mid[h]
                pairs = (
                    (src[x + 1, h, pl.ds(y0, rows), :], src[x - 1, h, pl.ds(y0, rows), :]),
                    (src[x, h, pl.ds(y0 + 1, rows), :], src[x, h, pl.ds(y0 - 1, rows), :]),
                    (after[h], before[h]),
                )
                lap, adv = -6.0 * f, 0.0
                for v, (p, m) in zip(VEL, pairs):
                    both = p + m
                    lap = lap + both
                    adv = adv + (0.25 * v) * (both * (p - m))
                kappa = kap[x, h, pl.ds(y0, rows), :]
                dst[x, h, pl.ds(y0, rows), :] = f + DT * (kappa * lap - adv)
            return carry

        lax.fori_loop(lo, hi, plane, 0)

    def actuate(n, dst):
        def one(e, carry):
            x, h, y = list_s[0, e], list_s[1, e], list_s[2, e]
            dst[x, h, pl.ds(y, 1), :] += amp_v[n, pl.ds(e, 1), :]
            return carry

        lax.fori_loop(0, total, one, 0)
        clear_outside(dst)

    forward(s0, s1, XO - 5, XO, 8, 40)
    forward(s0, s1, XO, XO + cx, 4, 48)
    forward(s0, s1, XO + cx, XO + cx + 5, 8, 40)
    actuate(0, s1)
    forward(s1, s2, XO - 4, XO + cx + 4, 8, 40)
    actuate(1, s2)
    forward(s2, s3, XO - 3, XO + cx + 3, 8, 40)
    actuate(2, s3)

    def scale(x, carry):
        for h in range(2):
            qa[x, h] = kap[x, h] * a4[x, h]
        return carry

    lax.fori_loop(XO - 4, XO + cx + 4, scale, 0)

    def step(adj, q, state, x, y0, rows):
        mid = [adj[x, h, pl.ds(y0, rows), :] for h in range(2)]
        qmid = [q[x, h, pl.ds(y0, rows), :] for h in range(2)]
        before, after = depth(*mid)
        qbefore, qafter = depth(*qmid)
        result = []
        for h in range(2):
            lap = (
                (q[x + 1, h, pl.ds(y0, rows), :] + q[x - 1, h, pl.ds(y0, rows), :])
                + (q[x, h, pl.ds(y0 + 1, rows), :] + q[x, h, pl.ds(y0 - 1, rows), :])
                + (qafter[h] + qbefore[h])
            ) - 6.0 * qmid[h]
            drift = (
                (0.5 * VEL[0]) * (adj[x + 1, h, pl.ds(y0, rows), :] - adj[x - 1, h, pl.ds(y0, rows), :])
                + (0.5 * VEL[1]) * (adj[x, h, pl.ds(y0 + 1, rows), :] - adj[x, h, pl.ds(y0 - 1, rows), :])
                + (0.5 * VEL[2]) * (after[h] - before[h])
            )
            result.append(mid[h] + DT * (lap + state[x, h, pl.ds(y0, rows), :] * drift))
        return result

    def backward(adj, q, state, dst, qdst, wide):
        def plane(x, carry):
            for h, value in enumerate(step(adj, q, state, x, 8, 40)):
                dst[x, h, pl.ds(8, 40), :] = value
                qdst[x, h, pl.ds(8, 40), :] = kap[x, h, pl.ds(8, 40), :] * value
            return carry

        lax.fori_loop(XO - wide, XO + cx + wide, plane, 0)
        clear_outside(dst)

    backward(a4, qa, s3, a3, qb, 3)
    backward(a3, qb, s2, a2, qa, 2)
    backward(a2, qa, s1, a1, qb, 1)

    def final(x, carry):
        for h, value in enumerate(step(a1, qb, s0, XO + x, YO, cy)):
            out_ref[x, :, halves[h]] = value
        return carry

    lax.fori_loop(0, cx, final, 0)

    msg_ref[...] = jnp.zeros(msg_ref.shape, jnp.float32)

    def foot(e, carry):
        x, h, y = list_s[0, e], list_s[1, e], list_s[2, e]
        for n, adj in enumerate((a1, a2, a3, a4)):
            sum_v[n, pl.ds(e, 1), :] = adj[x, h, pl.ds(y, 1), :]
        return carry

    lax.fori_loop(0, own_total, foot, 0)
    part = jnp.zeros((16, LANES), jnp.float32)
    for n in range(4):
        sums = DT * jnp.sum(sum_v[n], axis=1, keepdims=True)
        part = jnp.where(lanes[:16] - 8 * n == which_v[0:16, :], sums, part)
    sum_v[0] = part

    def post(e, carry):
        at = pl.ds(lax.shift_right_logical(list_s[3, e], 3), 1)
        msg_ref[at, :] += sum_v[0, pl.ds(e, 1), :]
        return carry

    lax.fori_loop(0, own_total, post, 0)


def gradient_kernel(ny, got_ref, own_ref, free_ref, out_ref):
    me = lax.axis_index("gx") * ny + lax.axis_index("gy")
    steps, owned = out_ref.shape
    total = jnp.sum(got_ref[...], axis=0, keepdims=True)
    flat = lax.broadcasted_iota(jnp.int32, own_ref.shape, 0) * LANES + lax.broadcasted_iota(
        jnp.int32, own_ref.shape, 1
    )
    listed = free_ref[...]
    column = lax.broadcasted_iota(jnp.int32, (steps, owned), 1)
    flags = jnp.zeros((steps, owned), jnp.float32)
    for k in range(owned):
        actuator = jnp.sum(jnp.where(own_ref[...] == me * owned + k, flat, 0))
        hit = jnp.max(jnp.where(listed == actuator, 1.0, 0.0), axis=1, keepdims=True)
        flags = jnp.where(column == k, hit, flags)
    for n in range(steps):
        out_ref[n : n + 1, :] = total[:, n * owned : (n + 1) * owned] * flags[n : n + 1, :]


VM = pl.BlockSpec(memory_space=pltpu.VMEM)
SM = pl.BlockSpec(memory_space=pltpu.SMEM)


def shards(
    checkpoint, terminal_adjoint, diffusivity, controls, owner_map, act_ids, slot_tiles, slot_count, free_list,
):
    cx, cy, cz = checkpoint.shape
    nx, ny = lax.axis_size("gx"), lax.axis_size("gy")
    ndev = nx * ny
    f32 = jnp.float32

    def shape(*dims):
        return jax.ShapeDtypeStruct(dims, f32)

    packed = pl.pallas_call(
        functools.partial(pack_kernel, cx, cy),
        out_shape=[shape(cx, 2, 16, LANES)] * 2
        + [shape(LAYERS, 2, cy, LANES)] * 2
        + [shape(2, CORNER_ROWS, LANES)] * 4
        + [shape(ndev, LANES)],
        in_specs=[VM] * 3 + [SM] * 5,
        out_specs=[VM] * 9,
        compiler_params=pltpu.CompilerParams(vmem_limit_bytes=32 << 20),
        name="pack",
    )(checkpoint, diffusivity, terminal_adjoint, controls, owner_map, act_ids, slot_tiles, slot_count)
    yup, ydn, xup, xdn, uu, ud, du, dd, row = packed

    def shift(value, a, b):
        pairs = [
            (i * ny + j, (i + a) * ny + j + b)
            for i in range(nx)
            for j in range(ny)
            if 0 <= i + a < nx and 0 <= j + b < ny
        ]
        return lax.ppermute(value, AXES, pairs)

    xup, xdn = shift(xup, 1, 0), shift(xdn, -1, 0)
    yup, ydn = shift(yup, 0, 1), shift(ydn, 0, -1)
    uu, ud, du, dd = shift(uu, 1, 1), shift(ud, 1, -1), shift(du, -1, 1), shift(dd, -1, -1)
    table = lax.all_to_all(row, AXES, 0, 0, tiled=True)

    ext = pltpu.VMEM((cx + 2 * XO, 2, YR, LANES), f32)
    start_adjoint, message = pl.pallas_call(
        functools.partial(window_kernel, cx, cy, nx, ny),
        out_shape=[shape(cx, cy, cz), shape(ndev, LANES)],
        in_specs=[VM] * 12,
        out_specs=[VM] * 2,
        scratch_shapes=[ext] * 11
        + [
            pltpu.VMEM((16, LANES), jnp.int32),
            pltpu.SMEM((16, LANES), jnp.int32),
            pltpu.SMEM((4, 160), jnp.int32),
            pltpu.VMEM((144, LANES), f32),
            pltpu.VMEM((144, LANES), jnp.int32),
            pltpu.VMEM((3, 144, LANES), f32),
            pltpu.VMEM((4, 16, LANES), f32),
            pltpu.SemaphoreType.DMA,
        ],
        compiler_params=pltpu.CompilerParams(vmem_limit_bytes=48 << 20),
        name="window",
    )(checkpoint, diffusivity, terminal_adjoint, yup, ydn, xup, xdn, uu, ud, du, dd, table)

    got = lax.all_to_all(message, AXES, 0, 0, tiled=True)
    gradient = pl.pallas_call(
        functools.partial(gradient_kernel, ny),
        out_shape=shape(*controls.shape),
        in_specs=[VM] * 3,
        out_specs=VM,
        name="gradient",
    )(got, owner_map.reshape(-1, LANES), free_list)
    return start_adjoint, gradient


def solution(mesh):
    placed = (
        P("gx", "gy", None),
        P("gx", "gy", None),
        P("gx", "gy", None),
        P(None, ("gx", "gy")),
        P(),
        P(("gx", "gy")),
        P(("gx", "gy")),
        P(("gx", "gy")),
        P(),
    )
    return jax.shard_map(
        shards,
        mesh=mesh,
        in_specs=placed,
        out_specs=(P("gx", "gy", None), P(None, ("gx", "gy"))),
        check_vma=False,
    )
```

time: 1750 us -> 144 us (0.08)
  blocking collectives: 1230 us -> 37.9 us
  waiting for transfers between devices: 263 us -> 26.3 us
  local copies, waits for them, and re-layouts: 96.9 us -> 5.25 us
  starting transfers between devices: 116 us -> 46.6 us
  Pallas kernels: 0 us -> 25.7 us
  other arithmetic: 25 us -> 0 us
    all_gather x1 -> x0, blocking collectives: 1230 us -> none  [shards(): all_controls = lax.all_gather(controls, ('gx', 'gy'), axis=1, tiled=True)]
    unnamed x2 -> x0, waiting for transfers between devices: 262 us -> none
    ppermute x28 -> x8, starting transfers between devices: 116 us -> 24.4 us  [shift(): return lax.ppermute(value, AXES, pairs)]
    gather x8 -> x0, local copies, waits for them, and re-layouts: 50.9 us -> none  [the longest x2 45.6 us: shards(): owner_map[free_list]]
    all_to_all x0 -> x1, blocking collectives: none -> 37.9 us  [shards(): got = lax.all_to_all(message, AXES, 0, 0, tiled=True)]
    unnamed x46 -> x22, local copies, waits for them, and re-layouts: 32.4 us -> 5.25 us
    pallas_call x0 -> x3, Pallas kernels: none -> 25.7 us  [the longest x1 21.5 us: shards(): pl.pallas_call(functools.partial(window_kernel, cx, cy, nx, ny), out_shap...]
    ppermute x28 -> x8, waiting for transfers between devices: 0.85 us -> 26.3 us  [shift(): return lax.ppermute(value, AXES, pairs)]
  transfers between devices with their start and end apart: 29 -> 9, of which waited for: 3 -> 4; matrix products, arithmetic and copies ran while one was open for 6% -> 0% of each run, Pallas kernels for 0% -> 0%
where the time goes in v1:
time: 144 us; the launch traced here: 143 us
  starting transfers between devices  46.6 us (32%)
  blocking collectives  37.9 us (26%)
  waiting for transfers between devices  26.3 us (18%)
  Pallas kernels  25.7 us (18%)
  local copies, waits for them, and re-layouts  5.25 us (4%)
  between operations  1.47 us (1%)
    all_to_all x1, blocking collectives, shards(): got = lax.all_to_all(message, AXES, 0, 0, tiled=True)  37.9 us
    ppermute x8, waiting for transfers between devices, shift(): return lax.ppermute(value, AXES, pairs)  26.3 us
    ppermute x8, starting transfers between devices, shift(): return lax.ppermute(value, AXES, pairs)  24.4 us
    all_to_all x1, starting transfers between devices, shards(): table = lax.all_to_all(row, AXES, 0, 0, tiled=True)  22.2 us
    pallas_call x1, Pallas kernels, shards(): pl.pallas_call(functools.partial(window_kernel, cx, cy, nx, ny), out_shap...  21.5 us
    unnamed x22, local copies, waits for them, and re-layouts  5.25 us
  transfers between devices with their start and end apart: 9, of which 4 were waited for; matrix products, arithmetic and copies ran while one was open for 0% of the time, Pallas kernels for 0%

profile of v1, /device:TPU:1, one launch (start us, length us, event | category | flops | bytes accessed | tf_op | source)
XLA Modules:
  0.0 143.2 jit_solution(1833448570298262432)
XLA Ops:
  0.6 0.0 copy-start.9
  0.6 0.0 copy-start.8
  1.3 0.0 copy-done.9
  1.3 0.0 copy-done.8
  1.3 0.0 copy-start
  1.3 1.0 copy-done
  2.4 0.0 copy-start.2
  2.4 1.0 copy-done.2
  3.4 0.0 copy-start.4
  3.4 1.0 copy-done.4
  4.5 0.0 copy-start.6
  4.5 0.7 copy-done.6
  5.2 0.0 copy-start.7
  5.2 0.7 copy-done.7
  5.9 0.0 copy-start.3
  5.9 0.0 copy-start.5
  5.9 2.2 %pack.1 = (f32[16,2,16,128]{3,2,1,0:T(8,128)}, f32[16,2,16,128]{3,2,1,0:T(8,128)S(1)}, f32[15,2,32,128]{3,2,1,0:T(8,128)}, f32[15,2,32,128]{3,2,1,0:T(8,128)}, f...) custom-call(f32[16,32,256]{2,1,0:T(8,128)S(1)} %copy-done, ...), custom_call_target="tpu_custom_call" | custom-call | tf_op jit(solution)/shard_map/pack/pallas_call | solution.py:331
  8.1 0.0 copy-start.10
  8.1 0.7 copy-done.10
  8.8 0.0 copy-start.1
  8.8 22.2 %all-to-all-start = ((f32[512,1,128]{2,1,0:T(1,128)}), f32[512,1,128]{2,1,0:T(1,128)S(1)}, u32[]{:S(2)}, u32[]{:S(2)}) async-start(f32[512,1,128]{2,1,0:T(1,128)} %bitcast.1), calls=%async_computation | async-start | bytes 524288 | tf_op jit(solution)/shard_map/all_to_all | solution.py:356
  31.0 3.9 %collective-permute-start.2 = (f32[15,2,32,128]{3,2,1,0:T(8,128)}, f32[15,2,32,128]{3,2,1,0:T(8,128)S(1)}, u32[]{:S(2)}, u32[]{:S(2)}) collective-permute-start(f32[15,2,32,128]{3,2,1,0:T(8,128)} %get-tuple-element.15), channel_id=1, source_target_pairs={{0,16},{1,17},{2,18},{3,19},{4,20},{5,21},{6,22},{7,23},{8,24},{9,... | collective-permute-start | bytes 1474568 | tf_op jit(solution)/shard_map/ppermute | solution.py:351
  34.9 3.6 %collective-permute-start.3 = (f32[15,2,32,128]{3,2,1,0:T(8,128)}, f32[15,2,32,128]{3,2,1,0:T(8,128)S(1)}, u32[]{:S(2)}, u32[]{:S(2)}) collective-permute-start(f32[15,2,32,128]{3,2,1,0:T(8,128)} %get-tuple-element.16), channel_id=1, source_target_pairs={{16,0},{17,1},{18,2},{19,3},{20,4},{21,5},{22,6},{23,7},{24,8},{25... | collective-permute-start | bytes 1474568 | tf_op jit(solution)/shard_map/ppermute | solution.py:351
  38.5 3.4 %collective-permute-start = (f32[16,2,16,128]{3,2,1,0:T(8,128)}, f32[16,2,16,128]{3,2,1,0:T(8,128)S(1)}, u32[]{:S(2)}, u32[]{:S(2)}) collective-permute-start(f32[16,2,16,128]{3,2,1,0:T(8,128)} %get-tuple-element.13), channel_id=1, source_target_pairs={{0,1},{1,2},{2,3},{3,4},{4,5},{5,6},{6,7},{7,8},{8,9},{9,10},{10,1... | collective-permute-start | bytes 786440 | tf_op jit(solution)/shard_map/ppermute | solution.py:351
  41.9 1.3 collective-permute-start.1
  43.2 7.7 %collective-permute-start.4 = (f32[2,32,128]{2,1,0:T(8,128)S(1)}, f32[2,32,128]{2,1,0:T(8,128)S(1)}, u32[]{:S(2)}, u32[]{:S(2)}) collective-permute-start(f32[2,32,128]{2,1,0:T(8,128)S(1)} %get-tuple-element.17), channel_id=1, source_target_pairs={{0,17},{1,18},{2,19},{3,20},{4,21},{5,22},{6,23},{7,24},{8,25},{9,... | collective-permute-start | bytes 98312 | tf_op jit(solution)/shard_map/ppermute | solution.py:351
  50.9 10.5 %collective-permute-done.4.uu_ref = f32[2,32,128]{2,1,0:T(8,128)S(1)} collective-permute-done((f32[2,32,128]{2,1,0:T(8,128)S(1)}, f32[2,32,128]{2,1,0:T(8,128)S(1)}, u32[]{:S(2)}, u32[]{:S(2)}) %collective-permute-start.4) | collective-permute-done | bytes 32800 | tf_op jit(solution)/shard_map/ppermute | solution.py:351
  61.4 1.3 collective-permute-start.5
  62.7 4.8 %collective-permute-done.5.ud_ref = f32[2,32,128]{2,1,0:T(8,128)S(1)} collective-permute-done((f32[2,32,128]{2,1,0:T(8,128)S(1)}, f32[2,32,128]{2,1,0:T(8,128)S(1)}, u32[]{:S(2)}, u32[]{:S(2)}) %collective-permute-start.5) | collective-permute-done | bytes 32800 | tf_op jit(solution)/shard_map/ppermute | solution.py:351
  67.5 1.9 %collective-permute-start.6 = (f32[2,32,128]{2,1,0:T(8,128)S(1)}, f32[2,32,128]{2,1,0:T(8,128)S(1)}, u32[]{:S(2)}, u32[]{:S(2)}) collective-permute-start(f32[2,32,128]{2,1,0:T(8,128)S(1)} %get-tuple-element.19), channel_id=1, source_target_pairs={{16,1},{17,2},{18,3},{19,4},{20,5},{21,6},{22,7},{23,8},{24,9},{25... | collective-permute-start | bytes 98312 | tf_op jit(solution)/shard_map/ppermute | solution.py:351
  69.4 1.0 collective-permute-done.6.du_ref
  70.4 1.3 collective-permute-start.7
  71.7 10.0 %collective-permute-done.7.dd_ref = f32[2,32,128]{2,1,0:T(8,128)S(1)} collective-permute-done((f32[2,32,128]{2,1,0:T(8,128)S(1)}, f32[2,32,128]{2,1,0:T(8,128)S(1)}, u32[]{:S(2)}, u32[]{:S(2)}) %collective-permute-start.7) | collective-permute-done | bytes 32800 | tf_op jit(solution)/shard_map/ppermute | solution.py:351
  81.8 0.0 collective-permute-done.yup_ref
  81.8 0.0 collective-permute-done.1.ydn_ref
  81.8 0.0 collective-permute-done.2.xup_ref
  81.8 0.0 collective-permute-done.3.xdn_ref
  81.8 0.0 all-to-all-done
  81.8 0.0 copy-done.3
  81.8 0.0 copy-done.5
  81.8 0.0 copy-done.1
  81.8 21.5 %window.1 = (f32[16,32,256]{2,1,0:T(8,128)}, f32[512,128]{1,0:T(8,128)S(1)}) custom-call(f32[16,32,256]{2,1,0:T(8,128)S(1)} %copy-done.1, f32[16,32,256]{2,1,0:T(8,128)S(1)} %copy-done.3, f32[16,32,256]{2,1,0:T(8,128)S(1)} %copy-done.5, f32[16,2,16,128]{3,2,1,0:T(8,128)S(1)} %collective-permute-done.yup_ref, ...), custom_call_target="tpu_custom_call" | custom-call | tf_op jit(solution)/shard_map/window/pallas_call | solution.py:359
  103.4 37.9 %all_to_all.22 = f32[512,1,128]{2,1,0:T(1,128)} all-to-all(f32[512,1,128]{2,1,0:T(1,128)S(1)} %bitcast.10), channel_id=1, replica_groups=mesh['gx'=32,'gy'=16] {'gx','gy'}, dimensions={0} | all-to-all | bytes 524288 | tf_op jit(solution)/shard_map/all_to_all | solution.py:379
  141.3 2.0 %gradient.1 = f32[4,8]{1,0:T(4,128)} custom-call(f32[512,128]{1,0:T(8,128)} %bitcast.12, s32[32,128]{1,0:T(8,128)} %bitcast.11, s32[4,2048]{1,0:T(4,128)} %free_ref.1), custom_call_target="tpu_custom_call" | custom-call | tf_op jit(solution)/shard_map/gradient/pallas_call | solution.py:380
Async XLA Ops:
  0.6 0.7 copy-start.9
  0.6 0.7 copy-start.8
  1.3 1.0 copy-start
  2.4 1.0 copy-start.2
  3.4 1.0 copy-start.4
  4.5 0.7 copy-start.6
  5.2 0.7 copy-start.7
  5.9 75.9 %copy-start.3 = (f32[16,32,256]{2,1,0:T(8,128)S(1)}, f32[16,32,256]{2,1,0:T(8,128)}, u32[]{:S(2)}) copy-start(f32[16,32,256]{2,1,0:T(8,128)} %kp_ref.3) | copy-start | bytes 1572868
  5.9 75.9 %copy-start.5 = (f32[16,32,256]{2,1,0:T(8,128)S(1)}, f32[16,32,256]{2,1,0:T(8,128)}, u32[]{:S(2)}) copy-start(f32[16,32,256]{2,1,0:T(8,128)} %ta_ref.3) | copy-start | bytes 1572868
  8.1 0.7 copy-start.10
  8.8 73.0 %copy-start.1 = (f32[16,32,256]{2,1,0:T(8,128)S(1)}, f32[16,32,256]{2,1,0:T(8,128)}, u32[]{:S(2)}) copy-start(f32[16,32,256]{2,1,0:T(8,128)} %ck_ref.3) | copy-start | bytes 1572868
  8.8 73.0 %all-to-all-start = ((f32[512,1,128]{2,1,0:T(1,128)}), f32[512,1,128]{2,1,0:T(1,128)S(1)}, u32[]{:S(2)}, u32[]{:S(2)}) async-start(f32[512,1,128]{2,1,0:T(1,128)} %bitcast.1), calls=%async_computation | async-start | bytes 524288 | tf_op jit(solution)/shard_map/all_to_all | solution.py:356
  31.0 50.8 %collective-permute-start.2 = (f32[15,2,32,128]{3,2,1,0:T(8,128)}, f32[15,2,32,128]{3,2,1,0:T(8,128)S(1)}, u32[]{:S(2)}, u32[]{:S(2)}) collective-permute-start(f32[15,2,32,128]{3,2,1,0:T(8,128)} %get-tuple-element.15), channel_id=1, source_target_pairs={{0,16},{1,17},{2,18},{3,19},{4,20},{5,21},{6,22},{7,23},{8,24},{9,... | collective-permute-start | bytes 1474568 | tf_op jit(solution)/shard_map/ppermute | solution.py:351
  34.9 46.9 %collective-permute-start.3 = (f32[15,2,32,128]{3,2,1,0:T(8,128)}, f32[15,2,32,128]{3,2,1,0:T(8,128)S(1)}, u32[]{:S(2)}, u32[]{:S(2)}) collective-permute-start(f32[15,2,32,128]{3,2,1,0:T(8,128)} %get-tuple-element.16), channel_id=1, source_target_pairs={{16,0},{17,1},{18,2},{19,3},{20,4},{21,5},{22,6},{23,7},{24,8},{25... | collective-permute-start | bytes 1474568 | tf_op jit(solution)/shard_map/ppermute | solution.py:351
  38.5 43.3 %collective-permute-start = (f32[16,2,16,128]{3,2,1,0:T(8,128)}, f32[16,2,16,128]{3,2,1,0:T(8,128)S(1)}, u32[]{:S(2)}, u32[]{:S(2)}) collective-permute-start(f32[16,2,16,128]{3,2,1,0:T(8,128)} %get-tuple-element.13), channel_id=1, source_target_pairs={{0,1},{1,2},{2,3},{3,4},{4,5},{5,6},{6,7},{7,8},{8,9},{9,10},{10,1... | collective-permute-start | bytes 786440 | tf_op jit(solution)/shard_map/ppermute | solution.py:351
  41.9 39.9 %collective-permute-start.1 = (f32[16,2,16,128]{3,2,1,0:T(8,128)}, f32[16,2,16,128]{3,2,1,0:T(8,128)S(1)}, u32[]{:S(2)}, u32[]{:S(2)}) collective-permute-start(f32[16,2,16,128]{3,2,1,0:T(8,128)} %copy-done.10), channel_id=1, source_target_pairs={{1,0},{2,1},{3,2},{4,3},{5,4},{6,5},{7,6},{8,7},{9,8},{10,9},{11,1... | collective-permute-start | bytes 786440 | tf_op jit(solution)/shard_map/ppermute | solution.py:351
  43.2 18.2 %collective-permute-start.4 = (f32[2,32,128]{2,1,0:T(8,128)S(1)}, f32[2,32,128]{2,1,0:T(8,128)S(1)}, u32[]{:S(2)}, u32[]{:S(2)}) collective-permute-start(f32[2,32,128]{2,1,0:T(8,128)S(1)} %get-tuple-element.17), channel_id=1, source_target_pairs={{0,17},{1,18},{2,19},{3,20},{4,21},{5,22},{6,23},{7,24},{8,25},{9,... | collective-permute-start | bytes 98312 | tf_op jit(solution)/shard_map/ppermute | solution.py:351
  61.4 6.1 %collective-permute-start.5 = (f32[2,32,128]{2,1,0:T(8,128)S(1)}, f32[2,32,128]{2,1,0:T(8,128)S(1)}, u32[]{:S(2)}, u32[]{:S(2)}) collective-permute-start(f32[2,32,128]{2,1,0:T(8,128)S(1)} %get-tuple-element.18), channel_id=1, source_target_pairs={{1,16},{2,17},{3,18},{4,19},{5,20},{6,21},{7,22},{8,23},{9,24},{10... | collective-permute-start | bytes 98312 | tf_op jit(solution)/shard_map/ppermute | solution.py:351
  67.5 2.9 %collective-permute-start.6 = (f32[2,32,128]{2,1,0:T(8,128)S(1)}, f32[2,32,128]{2,1,0:T(8,128)S(1)}, u32[]{:S(2)}, u32[]{:S(2)}) collective-permute-start(f32[2,32,128]{2,1,0:T(8,128)S(1)} %get-tuple-element.19), channel_id=1, source_target_pairs={{16,1},{17,2},{18,3},{19,4},{20,5},{21,6},{22,7},{23,8},{24,9},{25... | collective-permute-start | bytes 98312 | tf_op jit(solution)/shard_map/ppermute | solution.py:351
  70.4 11.3 %collective-permute-start.7 = (f32[2,32,128]{2,1,0:T(8,128)S(1)}, f32[2,32,128]{2,1,0:T(8,128)S(1)}, u32[]{:S(2)}, u32[]{:S(2)}) collective-permute-start(f32[2,32,128]{2,1,0:T(8,128)S(1)} %get-tuple-element.20), channel_id=1, source_target_pairs={{17,0},{18,1},{19,2},{20,3},{21,4},{22,5},{23,6},{24,7},{25,8},{26... | collective-permute-start | bytes 98312 | tf_op jit(solution)/shard_map/ppermute | solution.py:351

commit v2 on v1

--- a/solution.py
+++ b/solution.py
@@ -18,7 +18,8 @@
 YO = 12
 YR = 56
 LANES = 128
-POS, TIL = 32, 48
+GROUP = 32
+CODE = 1024
 
 
 def corner_pieces():
@@ -33,68 +34,124 @@
 CORNER, CORNER_ROWS = corner_pieces()
 
 
-def pack_kernel(
-    cx, cy, ck_ref, kp_ref, ta_ref, ctl_ref, own_ref, act_ref, til_ref, cnt_ref,
-    yup_ref, ydn_ref, xup_ref, xdn_ref, uu_ref, ud_ref, du_ref, dd_ref, row_ref,
+def table_rows(nx):
+    return max(8, nx * GROUP // LANES)
+
+
+def first_kernel(
+    cx, cy, ck_ref, kp_ref, ta_ref, own_ref, ctl_ref, act_ref, til_ref, cnt_ref,
+    yup_ref, ydn_ref, ids_ref, row_ref, low, high, own_s, sems,
 ):
-    fields = (ck_ref, kp_ref, ta_ref)
+    copies = [pltpu.make_async_copy(own_ref, own_s, sems.at[6])]
+    for f, field in enumerate((ck_ref, kp_ref, ta_ref)):
+        copies.append(pltpu.make_async_copy(field.at[:, 0:8, :], low.at[f], sems.at[2 * f]))
+        copies.append(pltpu.make_async_copy(field.at[:, cy - 8 : cy, :], high.at[f], sems.at[2 * f + 1]))
+    for copy in copies:
+        copy.start()
     lane = lax.broadcasted_iota(jnp.int32, (1, LANES), 1)
     row = jnp.zeros((1, LANES), jnp.float32)
     steps, owned = ctl_ref.shape
     for n in range(steps):
         for k in range(owned):
             row = jnp.where(lane == n * owned + k, ctl_ref[n, k], row)
+    row_ref[...] = jnp.broadcast_to(row, row_ref.shape)
+    copies[0].wait()
+    ids = jnp.zeros((1, LANES), jnp.int32)
     for j in range(act_ref.shape[0]):
-        place = jnp.where(j < cnt_ref[0], own_ref[act_ref[j]], -1)
-        row = jnp.where(lane == POS + j, place.astype(jnp.float32), row)
-        row = jnp.where(lane == TIL + j, til_ref[j].astype(jnp.float32), row)
-    row_ref[...] = jnp.broadcast_to(row, row_ref.shape)
+        code = jnp.where(j < cnt_ref[0], own_s[act_ref[j]] * CODE + til_ref[j] + 1, 0)
+        ids = jnp.where(lane == j, code, ids)
+    ids = ids.astype(jnp.float32)
+    ids_ref[...] = jnp.broadcast_to(ids, ids_ref.shape)
+    for copy in copies[1:]:
+        copy.wait()
     halves = (slice(0, LANES), slice(LANES, 2 * LANES))
-    at = 0
-    for field, wide in zip(fields, WIDE):
-        for i in range(wide):
-            for h in range(2):
-                xup_ref[at + i, h] = field[cx - wide + i, :, halves[h]]
-                xdn_ref[at + i, h] = field[i, :, halves[h]]
-        at += wide
 
     def rows(x, carry):
         at = 0
-        for field, wide in zip(fields, WIDE):
-            for h in range(2):
-                yup_ref[x, h, at : at + wide, :] = field[x, cy - wide : cy, halves[h]]
-                ydn_ref[x, h, at : at + wide, :] = field[x, 0:wide, halves[h]]
+        for f, wide in enumerate(WIDE):
+            for h in range(2):
+                yup_ref[x, h, at : at + wide, :] = high[f, x, 8 - wide : 8, halves[h]]
+                ydn_ref[x, h, at : at + wide, :] = low[f, x, 0:wide, halves[h]]
             at += wide
         return carry
 
     lax.fori_loop(0, cx, rows, 0)
+    yup_ref[0, 0, LAYERS : LAYERS + 1, :] = ids
+    ydn_ref[0, 0, LAYERS : LAYERS + 1, :] = ids
+
+
+def second_kernel(
+    cx, cy, nx, ny, ck_ref, kp_ref, ta_ref, yup_ref, ydn_ref, ids_ref, got_ref,
+    xup_ref, xdn_ref, tab_ref, sems,
+):
+    copies = []
+    at = 0
+    for field, wide in zip((ck_ref, kp_ref, ta_ref), WIDE):
+        for h in range(2):
+            half = slice(h * LANES, (h + 1) * LANES)
+            for ref, x in ((xup_ref, cx - wide), (xdn_ref, 0)):
+                copies.append(
+                    pltpu.make_async_copy(
+                        field.at[x : x + wide, :, half], ref.at[at : at + wide, h], sems.at[len(copies)]
+                    )
+                )
+        at += wide
+    for copy in copies:
+        copy.start()
     for f, layer, count, start in CORNER:
-        for h in range(2):
-            for up_x, up_y, ref in ((1, 1, uu_ref), (1, 0, ud_ref), (0, 1, du_ref), (0, 0, dd_ref)):
-                x = cx - layer if up_x else layer - 1
-                y = cy - count if up_y else 0
-                ref[h, start : start + count, :] = fields[f][x, y : y + count, halves[h]]
+        top = sum(WIDE[: f + 1])
+        at = top - WIDE[f]
+        for ref, x in ((xup_ref, cx - layer), (xdn_ref, layer - 1)):
+            for h in range(2):
+                ref[LAYERS, h, start : start + count, :] = yup_ref[x, h, top - count : top, :]
+                ref[LAYERS + 1, h, start : start + count, :] = ydn_ref[x, h, at : at + count, :]
+    for ref in (xup_ref, xdn_ref):
+        ref[LAYERS, 0, cy - 1 : cy, :] = ids_ref[0:1, :]
+        ref[LAYERS, 1, cy - 1 : cy, :] = yup_ref[0, 0, LAYERS : LAYERS + 1, :]
+        ref[LAYERS + 1, 0, cy - 1 : cy, :] = ydn_ref[0, 0, LAYERS : LAYERS + 1, :]
+    rows = table_rows(nx)
+    if nx < rows:
+        for j in range(ny):
+            tab_ref[j, 0:nx, :] = got_ref[...]
+            tab_ref[j, nx:rows, :] = jnp.zeros((rows - nx, LANES), jnp.float32)
+    else:
+        lane = lax.broadcasted_iota(jnp.int32, (rows, LANES), 1)
+        table = got_ref[0:rows, :]
+        for g in range(1, nx // rows):
+            part = pltpu.roll(got_ref[g * rows : (g + 1) * rows, :], g * GROUP, 1)
+            table = jnp.where(lane < g * GROUP, table, part)
+        tab_ref[...] = jnp.broadcast_to(table[None], tab_ref.shape)
+    for copy in copies:
+        copy.wait()
 
 
 def window_kernel(
     cx, cy, nx, ny, ck_ref, kp_ref, ta_ref,
-    yup_ref, ydn_ref, xup_ref, xdn_ref, uu_ref, ud_ref, du_ref, dd_ref, tab_ref,
+    yup_ref, ydn_ref, xup_ref, xdn_ref, ids_ref, tab_ref,
     out_ref, msg_ref,
     s0, s1, s2, s3, kap, a4, a3, a2, a1, qa, qb,
     near_v, near_s, list_s, pick_v, which_v, amp_v, sum_v, sem,
 ):
     gx = lax.axis_index("gx")
     gy = lax.axis_index("gy")
-    me = gx * ny + gy
     halves = (slice(0, LANES), slice(LANES, 2 * LANES))
     lane = lax.broadcasted_iota(jnp.int32, (1, LANES), 1)
 
-    order = [(0, 0)] + [(a, b) for a in (-1, 0, 1) for b in (-1, 0, 1) if (a, b) != (0, 0)]
-    for i, (a, b) in enumerate(order):
-        there = (gx + a >= 0) & (gx + a < nx) & (gy + b >= 0) & (gy + b < ny)
-        source = jnp.where(there, me + a * ny + b, me)
-        seen = tab_ref[pl.ds(source, 1), :]
-        near_v[i : i + 1, :] = jnp.where(there, seen, -1.0).astype(jnp.int32)
+    spare = slice(LAYERS, LAYERS + 1)
+    tail = slice(cy - 1, cy)
+    near = (
+        ((0, 0), ids_ref[0:1, :]),
+        ((0, -1), yup_ref[0, 0, spare, :]),
+        ((0, 1), ydn_ref[0, 0, spare, :]),
+        ((-1, 0), xup_ref[LAYERS, 0, tail, :]),
+        ((-1, -1), xup_ref[LAYERS, 1, tail, :]),
+        ((-1, 1), xup_ref[LAYERS + 1, 0, tail, :]),
+        ((1, 0), xdn_ref[LAYERS, 0, tail, :]),
+        ((1, -1), xdn_ref[LAYERS, 1, tail, :]),
+        ((1, 1), xdn_ref[LAYERS + 1, 0, tail, :]),
+    )
+    for i, (_, codes) in enumerate(near):
+        near_v[i : i + 1, :] = codes.astype(jnp.int32) - 1
     ids = pltpu.make_async_copy(near_v, near_s, sem)
     ids.start()
 
@@ -116,19 +173,19 @@
                 ext[XO + cx + i, h, YO : YO + cy, :] = xdn_ref[at + i, h]
     for f, layer, count, start in CORNER:
         ext = fields[f][1]
-        for h in range(2):
-            for up_x, up_y, ref in ((1, 1, uu_ref), (1, 0, ud_ref), (0, 1, du_ref), (0, 0, dd_ref)):
-                x = XO - layer if up_x else XO + cx + layer - 1
-                y = YO - count if up_y else YO + cy
-                ext[x, h, y : y + count, :] = ref[h, start : start + count, :]
+        for ref, x in ((xup_ref, XO - layer), (xdn_ref, XO + cx + layer - 1)):
+            for h in range(2):
+                ext[x, h, YO - count : YO, :] = ref[LAYERS, h, start : start + count, :]
+                ext[x, h, YO + cy : YO + cy + count, :] = ref[LAYERS + 1, h, start : start + count, :]
 
     ids.wait()
     total = jnp.int32(0)
     own_total = jnp.int32(0)
-    for i, (a, b) in enumerate(order):
+    for i, ((a, b), _) in enumerate(near):
         for j in range(16):
-            place = near_s[i, POS + j]
-            tile = near_s[i, TIL + j]
+            code = near_s[i, j]
+            place = lax.shift_right_arithmetic(code, 10)
+            tile = code & (CODE - 1)
             x = lax.shift_right_logical(tile, 6) + (XO + a * cx)
             y = (lax.shift_right_logical(tile, 1) & (cy - 1)) + (YO + b * cy)
             keep = place >= 0
@@ -144,10 +201,15 @@
         if i == 0:
             own_total = total
 
+    rows = table_rows(nx)
+
     def pick(e, carry):
         place = list_s[3, e]
-        pick_v[pl.ds(e, 1), :] = tab_ref[pl.ds(lax.shift_right_logical(place, 3), 1), :]
-        which_v[pl.ds(e, 1), :] = jnp.broadcast_to(place & 7, (1, LANES))
+        owner = lax.shift_right_logical(place, 3)
+        column, line = lax.rem(owner, ny), lax.div(owner, ny)
+        at = column * rows + lax.rem(line, rows)
+        pick_v[pl.ds(e, 1), :] = tab_ref[pl.ds(at, 1), :]
+        which_v[pl.ds(e, 1), :] = jnp.broadcast_to(lax.div(line, rows) * GROUP + (place & 7), (1, LANES))
         return carry
 
     lax.fori_loop(0, total, pick, 0)
@@ -284,7 +346,7 @@
     part = jnp.zeros((16, LANES), jnp.float32)
     for n in range(4):
         sums = DT * jnp.sum(sum_v[n], axis=1, keepdims=True)
-        part = jnp.where(lanes[:16] - 8 * n == which_v[0:16, :], sums, part)
+        part = jnp.where(lanes[:16] - 8 * n == (which_v[0:16, :] & 7), sums, part)
     sum_v[0] = part
 
     def post(e, carry):
@@ -313,6 +375,7 @@
         out_ref[n : n + 1, :] = total[:, n * owned : (n + 1) * owned] * flags[n : n + 1, :]
 
 
+ANY = pl.BlockSpec(memory_space=pl.ANY)
 VM = pl.BlockSpec(memory_space=pltpu.VMEM)
 SM = pl.BlockSpec(memory_space=pltpu.SMEM)
 
@@ -328,38 +391,46 @@
     def shape(*dims):
         return jax.ShapeDtypeStruct(dims, f32)
 
-    packed = pl.pallas_call(
-        functools.partial(pack_kernel, cx, cy),
-        out_shape=[shape(cx, 2, 16, LANES)] * 2
-        + [shape(LAYERS, 2, cy, LANES)] * 2
-        + [shape(2, CORNER_ROWS, LANES)] * 4
-        + [shape(ndev, LANES)],
-        in_specs=[VM] * 3 + [SM] * 5,
-        out_specs=[VM] * 9,
+    def shift(value, axis, way):
+        size = lax.axis_size(axis)
+        pairs = [(i, i + way) for i in range(size) if 0 <= i + way < size]
+        return lax.ppermute(value, axis, pairs)
+
+    fields = (checkpoint, diffusivity, terminal_adjoint)
+    yup, ydn, ids, row = pl.pallas_call(
+        functools.partial(first_kernel, cx, cy),
+        out_shape=[shape(cx, 2, 16, LANES)] * 2 + [shape(8, LANES), shape(nx, LANES)],
+        in_specs=[ANY] * 4 + [SM] * 4,
+        out_specs=[VM] * 4,
+        scratch_shapes=[
+            pltpu.VMEM((3, cx, 8, cz), f32),
+            pltpu.VMEM((3, cx, 8, cz), f32),
+            pltpu.SMEM(owner_map.shape, jnp.int32),
+            pltpu.SemaphoreType.DMA((7,)),
+        ],
+        compiler_params=pltpu.CompilerParams(vmem_limit_bytes=60 << 20),
+        name="first",
+    )(*fields, owner_map, controls, act_ids, slot_tiles, slot_count)
+    yup, ydn = shift(yup, "gy", 1), shift(ydn, "gy", -1)
+    got = lax.all_to_all(row, "gx", 0, 0, tiled=True)
+    rows = table_rows(nx)
+    xup, xdn, table = pl.pallas_call(
+        functools.partial(second_kernel, cx, cy, nx, ny),
+        out_shape=[shape(LAYERS + 2, 2, cy, LANES)] * 2 + [shape(ny, rows, LANES)],
+        in_specs=[ANY] * 3 + [VM] * 4,
+        out_specs=[VM] * 3,
+        scratch_shapes=[pltpu.SemaphoreType.DMA((12,))],
         compiler_params=pltpu.CompilerParams(vmem_limit_bytes=32 << 20),
-        name="pack",
-    )(checkpoint, diffusivity, terminal_adjoint, controls, owner_map, act_ids, slot_tiles, slot_count)
-    yup, ydn, xup, xdn, uu, ud, du, dd, row = packed
-
-    def shift(value, a, b):
-        pairs = [
-            (i * ny + j, (i + a) * ny + j + b)
-            for i in range(nx)
-            for j in range(ny)
-            if 0 <= i + a < nx and 0 <= j + b < ny
-        ]
-        return lax.ppermute(value, AXES, pairs)
-
-    xup, xdn = shift(xup, 1, 0), shift(xdn, -1, 0)
-    yup, ydn = shift(yup, 0, 1), shift(ydn, 0, -1)
-    uu, ud, du, dd = shift(uu, 1, 1), shift(ud, 1, -1), shift(du, -1, 1), shift(dd, -1, -1)
-    table = lax.all_to_all(row, AXES, 0, 0, tiled=True)
+        name="second",
+    )(*fields, yup, ydn, ids, got)
+    xup, xdn = shift(xup, "gx", 1), shift(xdn, "gx", -1)
+    table = lax.all_to_all(table, "gy", 0, 0, tiled=True).reshape(ny * rows, LANES)
 
     ext = pltpu.VMEM((cx + 2 * XO, 2, YR, LANES), f32)
     start_adjoint, message = pl.pallas_call(
         functools.partial(window_kernel, cx, cy, nx, ny),
         out_shape=[shape(cx, cy, cz), shape(ndev, LANES)],
-        in_specs=[VM] * 12,
+        in_specs=[VM] * 9,
         out_specs=[VM] * 2,
         scratch_shapes=[ext] * 11
         + [
@@ -374,7 +445,7 @@
         ],
         compiler_params=pltpu.CompilerParams(vmem_limit_bytes=48 << 20),
         name="window",
-    )(checkpoint, diffusivity, terminal_adjoint, yup, ydn, xup, xdn, uu, ud, du, dd, table)
+    )(*fields, yup, ydn, xup, xdn, ids, table)
 
     got = lax.all_to_all(message, AXES, 0, 0, tiled=True)
     gradient = pl.pallas_call(

time: 144 us -> 111 us (0.77)
  starting transfers between devices: 46.6 us -> 12.6 us
  blocking collectives: 37.9 us -> 69.1 us
  waiting for transfers between devices: 26.3 us -> 0.01 us
  local copies, waits for them, and re-layouts: 5.25 us -> 0.02 us
    all_to_all x0 -> x2, blocking collectives: none -> 40.9 us  [the longest x1 22.9 us: shards(): lax.all_to_all(table, 'gy', 0, 0, tiled=True).reshape(ny * rows, LANES)]
    ppermute x8 -> x4, waiting for transfers between devices: 26.3 us -> 0.01 us  [shift(): return lax.ppermute(value, axis, pairs)]
    all_to_all x1 -> x0, starting transfers between devices: 22.2 us -> none  [shards(): table = lax.all_to_all(row, AXES, 0, 0, tiled=True)]
    ppermute x8 -> x4, starting transfers between devices: 24.4 us -> 12.6 us  [shift(): return lax.ppermute(value, axis, pairs)]
    all_to_all x1, blocking collectives: 37.9 us -> 28.2 us  [shards(): got = lax.all_to_all(message, AXES, 0, 0, tiled=True)]
    unnamed x22 -> x8, local copies, waits for them, and re-layouts: 5.25 us -> 0.02 us
    pallas_call x1 -> x2, Pallas kernels: 2.19 us -> 3.35 us  [the longest x1 3.06 us: shards(): pl.pallas_call(functools.partial(first_kernel, cx, cy), out_shape=[shape(...]
  transfers between devices with their start and end apart: 9 -> 4, of which waited for: 4 -> 0; matrix products, arithmetic and copies ran while one was open for 0% -> 0% of each run, Pallas kernels for 0% -> 0%
where the time goes in v2:
time: 111 us; the launch traced here: 110 us
  blocking collectives  69.1 us (62%)
  Pallas kernels  27 us (24%)
  starting transfers between devices  12.6 us (11%)
  between operations  1.4 us (1%)
    all_to_all x1, blocking collectives, shards(): got = lax.all_to_all(message, AXES, 0, 0, tiled=True)  28.2 us
    all_to_all x1, blocking collectives, shards(): lax.all_to_all(table, 'gy', 0, 0, tiled=True).reshape(ny * rows, LANES)  22.9 us
    pallas_call x1, Pallas kernels, shards(): pl.pallas_call(functools.partial(window_kernel, cx, cy, nx, ny), out_shap...  21.7 us
    all_to_all x1, blocking collectives, shards(): got = lax.all_to_all(row, 'gx', 0, 0, tiled=True)  18 us
    ppermute x4, starting transfers between devices, shift(): return lax.ppermute(value, axis, pairs)  12.6 us
    pallas_call x1, Pallas kernels, shards(): pl.pallas_call(functools.partial(first_kernel, cx, cy), out_shape=[shape(...  3.06 us
  transfers between devices with their start and end apart: 4, of which 0 were waited for; matrix products, arithmetic and copies ran while one was open for 0% of the time, Pallas kernels for 0%

profile of v2, /device:TPU:1, one launch (start us, length us, event | category | flops | bytes accessed | tf_op | source)
XLA Modules:
  0.0 110.1 jit_solution(3999783284974475852)
XLA Ops:
  1.3 0.0 copy-start
  1.3 0.0 copy-start.1
  1.3 0.0 copy-start.2
  1.3 3.1 %first.1 = (f32[16,2,16,128]{3,2,1,0:T(8,128)}, f32[16,2,16,128]{3,2,1,0:T(8,128)}, f32[8,128]{1,0:T(8,128)}, f32[32,128]{1,0:T(8,128)}) custom-call(f32[16,32,256]{2,1,0:T(8,128)} %ck_ref.5, f32[16,32,256]{2,1,0:T(8,128)} %kp_ref.5, f32[16,32,256]{2,1,0:T(8,128)} %ta_ref.5, s32[4096]{0:T(1024)} %own_ref.1, f32[4,8]{1,0:T(4,128)} %ctl_ref.1, s32[16]{0:T(128)} %act_ref.1, ...), custom_call_target="tpu_custom_call" | custom-call | tf_op jit(solution)/shard_map/first/pallas_call | solution.py:400
  4.4 6.6 %collective-permute-start = (f32[16,2,16,128]{3,2,1,0:T(8,128)}, f32[16,2,16,128]{3,2,1,0:T(8,128)S(1)}, u32[]{:S(2)}, u32[]{:S(2)}) collective-permute-start(f32[16,2,16,128]{3,2,1,0:T(8,128)} %get-tuple-element.11), channel_id=1, source_target_pairs={{0,1},{1,2},{2,3},{3,4},{4,5},{5,6},{6,7},{7,8},{8,9},{9,10},{10,1... | collective-permute-start | bytes 786440 | tf_op jit(solution)/shard_map/ppermute | solution.py:397
  11.0 1.3 %collective-permute-start.1 = (f32[16,2,16,128]{3,2,1,0:T(8,128)}, f32[16,2,16,128]{3,2,1,0:T(8,128)S(1)}, u32[]{:S(2)}, u32[]{:S(2)}) collective-permute-start(f32[16,2,16,128]{3,2,1,0:T(8,128)} %get-tuple-element.12), channel_id=1, source_target_pairs={{1,0},{2,1},{3,2},{4,3},{5,4},{6,5},{7,6},{8,7},{9,8},{10,9},{11,1... | collective-permute-start | bytes 786440 | tf_op jit(solution)/shard_map/ppermute | solution.py:397
  12.3 0.0 copy-start.3
  12.3 18.0 %all_to_all.27 = f32[32,1,128]{2,1,0:T(1,128)S(1)} all-to-all(f32[32,1,128]{2,1,0:T(1,128)} %bitcast.15), channel_id=1, replica_groups=mesh['gx'=32,'gy'=16] {'gx'}, dimensions={0} | all-to-all | bytes 32768 | tf_op jit(solution)/shard_map/all_to_all | solution.py:415
  30.3 0.0 collective-permute-done.yup_ref
  30.3 0.0 collective-permute-done.1.ydn_ref
  30.3 0.0 copy-done
  30.3 0.0 copy-done.1
  30.3 0.0 copy-done.2
  30.3 0.0 copy-done.3
  30.3 0.3 second.1
  30.6 2.8 %collective-permute-start.2 = (f32[17,2,32,128]{3,2,1,0:T(8,128)S(1)}, f32[17,2,32,128]{3,2,1,0:T(8,128)S(1)}, u32[]{:S(2)}, u32[]{:S(2)}) collective-permute-start(f32[17,2,32,128]{3,2,1,0:T(8,128)S(1)} %get-tuple-element.15), channel_id=1, source_target_pairs={{0,16},{16,32},{32,48},{48,64},{64,80},{80,96},{96,112},{112,128},... | collective-permute-start | bytes 1671176 | tf_op jit(solution)/shard_map/ppermute | solution.py:397
  33.4 1.9 %collective-permute-start.3 = (f32[17,2,32,128]{3,2,1,0:T(8,128)S(1)}, f32[17,2,32,128]{3,2,1,0:T(8,128)S(1)}, u32[]{:S(2)}, u32[]{:S(2)}) collective-permute-start(f32[17,2,32,128]{3,2,1,0:T(8,128)S(1)} %get-tuple-element.16), channel_id=1, source_target_pairs={{16,0},{32,16},{48,32},{64,48},{80,64},{96,80},{112,96},{128,112},... | collective-permute-start | bytes 1671176 | tf_op jit(solution)/shard_map/ppermute | solution.py:397
  35.3 22.9 %all_to_all.28 = f32[16,8,128]{2,1,0:T(8,128)S(1)} all-to-all(f32[16,8,128]{2,1,0:T(8,128)S(1)} %get-tuple-element.17), channel_id=1, replica_groups=mesh['gx'=32,'gy'=16] {'gy'}, dimensions={0} | all-to-all | bytes 131072 | tf_op jit(solution)/shard_map/all_to_all | solution.py:427
  58.3 0.0 collective-permute-done.2.xup_ref
  58.3 0.0 collective-permute-done.3.xdn_ref
  58.3 21.7 %window.1 = (f32[16,32,256]{2,1,0:T(8,128)}, f32[512,128]{1,0:T(8,128)S(1)}) custom-call(f32[16,32,256]{2,1,0:T(8,128)S(1)} %copy-done, f32[16,32,256]{2,1,0:T(8,128)S(1)} %copy-done.1, f32[16,32,256]{2,1,0:T(8,128)S(1)} %copy-done.2, f32[16,2,16,128]{3,2,1,0:T(8,128)S(1)} %collective-permute-done.yup_ref, ...), custom_call_target="tpu_custom_call" | custom-call | tf_op jit(solution)/shard_map/window/pallas_call | solution.py:430
  79.9 28.2 %all_to_all.29 = f32[512,1,128]{2,1,0:T(1,128)} all-to-all(f32[512,1,128]{2,1,0:T(1,128)S(1)} %bitcast.11), channel_id=1, replica_groups=mesh['gx'=32,'gy'=16] {'gx','gy'}, dimensions={0} | all-to-all | bytes 524288 | tf_op jit(solution)/shard_map/all_to_all | solution.py:450
  108.2 2.0 %gradient.1 = f32[4,8]{1,0:T(4,128)} custom-call(f32[512,128]{1,0:T(8,128)} %bitcast.13, s32[32,128]{1,0:T(8,128)} %bitcast.14, s32[4,2048]{1,0:T(4,128)} %free_ref.1), custom_call_target="tpu_custom_call" | custom-call | tf_op jit(solution)/shard_map/gradient/pallas_call | solution.py:451
Async XLA Ops:
  1.3 29.0 %copy-start = (f32[16,32,256]{2,1,0:T(8,128)S(1)}, f32[16,32,256]{2,1,0:T(8,128)}, u32[]{:S(2)}) copy-start(f32[16,32,256]{2,1,0:T(8,128)} %ck_ref.5) | copy-start | bytes 1572868
  1.3 29.0 %copy-start.1 = (f32[16,32,256]{2,1,0:T(8,128)S(1)}, f32[16,32,256]{2,1,0:T(8,128)}, u32[]{:S(2)}) copy-start(f32[16,32,256]{2,1,0:T(8,128)} %kp_ref.5) | copy-start | bytes 1572868
  1.3 29.0 %copy-start.2 = (f32[16,32,256]{2,1,0:T(8,128)S(1)}, f32[16,32,256]{2,1,0:T(8,128)}, u32[]{:S(2)}) copy-start(f32[16,32,256]{2,1,0:T(8,128)} %ta_ref.5) | copy-start | bytes 1572868
  4.4 25.9 %collective-permute-start = (f32[16,2,16,128]{3,2,1,0:T(8,128)}, f32[16,2,16,128]{3,2,1,0:T(8,128)S(1)}, u32[]{:S(2)}, u32[]{:S(2)}) collective-permute-start(f32[16,2,16,128]{3,2,1,0:T(8,128)} %get-tuple-element.11), channel_id=1, source_target_pairs={{0,1},{1,2},{2,3},{3,4},{4,5},{5,6},{6,7},{7,8},{8,9},{9,10},{10,1... | collective-permute-start | bytes 786440 | tf_op jit(solution)/shard_map/ppermute | solution.py:397
  11.0 19.3 %collective-permute-start.1 = (f32[16,2,16,128]{3,2,1,0:T(8,128)}, f32[16,2,16,128]{3,2,1,0:T(8,128)S(1)}, u32[]{:S(2)}, u32[]{:S(2)}) collective-permute-start(f32[16,2,16,128]{3,2,1,0:T(8,128)} %get-tuple-element.12), channel_id=1, source_target_pairs={{1,0},{2,1},{3,2},{4,3},{5,4},{6,5},{7,6},{8,7},{9,8},{10,9},{11,1... | collective-permute-start | bytes 786440 | tf_op jit(solution)/shard_map/ppermute | solution.py:397
  12.3 18.0 %copy-start.3 = (f32[8,128]{1,0:T(8,128)S(1)}, f32[8,128]{1,0:T(8,128)}, u32[]{:S(2)}) copy-start(f32[8,128]{1,0:T(8,128)} %get-tuple-element.13.ids_ref) | copy-start | bytes 12292
  30.6 27.6 %collective-permute-start.2 = (f32[17,2,32,128]{3,2,1,0:T(8,128)S(1)}, f32[17,2,32,128]{3,2,1,0:T(8,128)S(1)}, u32[]{:S(2)}, u32[]{:S(2)}) collective-permute-start(f32[17,2,32,128]{3,2,1,0:T(8,128)S(1)} %get-tuple-element.15), channel_id=1, source_target_pairs={{0,16},{16,32},{32,48},{48,64},{64,80},{80,96},{96,112},{112,128},... | collective-permute-start | bytes 1671176 | tf_op jit(solution)/shard_map/ppermute | solution.py:397
  33.4 24.9 %collective-permute-start.3 = (f32[17,2,32,128]{3,2,1,0:T(8,128)S(1)}, f32[17,2,32,128]{3,2,1,0:T(8,128)S(1)}, u32[]{:S(2)}, u32[]{:S(2)}) collective-permute-start(f32[17,2,32,128]{3,2,1,0:T(8,128)S(1)} %get-tuple-element.16), channel_id=1, source_target_pairs={{16,0},{32,16},{48,32},{64,48},{80,64},{96,80},{112,96},{128,112},... | collective-permute-start | bytes 1671176 | tf_op jit(solution)/shard_map/ppermute | solution.py:397

commit v3 on v2

--- a/solution.py
+++ b/solution.py
@@ -19,6 +19,7 @@
 YR = 56
 LANES = 128
 GROUP = 32
+BATCH = 4
 CODE = 1024
 
 
@@ -75,7 +76,7 @@
             at += wide
         return carry
 
-    lax.fori_loop(0, cx, rows, 0)
+    lax.fori_loop(0, cx, rows, 0, unroll=4)
     yup_ref[0, 0, LAYERS : LAYERS + 1, :] = ids
     ydn_ref[0, 0, LAYERS : LAYERS + 1, :] = ids
 
@@ -130,7 +131,7 @@
     yup_ref, ydn_ref, xup_ref, xdn_ref, ids_ref, tab_ref,
     out_ref, msg_ref,
     s0, s1, s2, s3, kap, a4, a3, a2, a1, qa, qb,
-    near_v, near_s, list_s, pick_v, which_v, amp_v, sum_v, sem,
+    near_v, near_s, list_s, pick_v, which_v, amp_v, sum_v, sem, res, out_sems,
 ):
     gx = lax.axis_index("gx")
     gy = lax.axis_index("gy")
@@ -159,24 +160,28 @@
     for f, (own, ext) in enumerate(fields):
         wide, at = WIDE[f], sum(WIDE[:f])
 
-        def assemble(x, carry, own=own, ext=ext, wide=wide, at=at):
+        def take(value, f=f):
+            return DT * value if f == 1 else value
+
+        def assemble(x, carry, own=own, ext=ext, wide=wide, at=at, take=take):
             for h in range(2):
-                ext[XO + x, h, YO : YO + cy, :] = own[x, :, halves[h]]
-                ext[XO + x, h, YO - wide : YO, :] = yup_ref[x, h, at : at + wide, :]
-                ext[XO + x, h, YO + cy : YO + cy + wide, :] = ydn_ref[x, h, at : at + wide, :]
+                ext[XO + x, h, YO : YO + cy, :] = take(own[x, :, halves[h]])
+                ext[XO + x, h, YO - wide : YO, :] = take(yup_ref[x, h, at : at + wide, :])
+                ext[XO + x, h, YO + cy : YO + cy + wide, :] = take(ydn_ref[x, h, at : at + wide, :])
             return carry
 
-        lax.fori_loop(0, cx, assemble, 0)
+        lax.fori_loop(0, cx, assemble, 0, unroll=True)
         for i in range(wide):
             for h in range(2):
-                ext[XO - wide + i, h, YO : YO + cy, :] = xup_ref[at + i, h]
-                ext[XO + cx + i, h, YO : YO + cy, :] = xdn_ref[at + i, h]
-    for f, layer, count, start in CORNER:
-        ext = fields[f][1]
-        for ref, x in ((xup_ref, XO - layer), (xdn_ref, XO + cx + layer - 1)):
-            for h in range(2):
-                ext[x, h, YO - count : YO, :] = ref[LAYERS, h, start : start + count, :]
-                ext[x, h, YO + cy : YO + cy + count, :] = ref[LAYERS + 1, h, start : start + count, :]
+                ext[XO - wide + i, h, YO : YO + cy, :] = take(xup_ref[at + i, h])
+                ext[XO + cx + i, h, YO : YO + cy, :] = take(xdn_ref[at + i, h])
+        for c, layer, count, start in CORNER:
+            if c != f:
+                continue
+            for ref, x in ((xup_ref, XO - layer), (xdn_ref, XO + cx + layer - 1)):
+                for h in range(2):
+                    ext[x, h, YO - count : YO, :] = take(ref[LAYERS, h, start : start + count, :])
+                    ext[x, h, YO + cy : YO + cy + count, :] = take(ref[LAYERS + 1, h, start : start + count, :])
 
     ids.wait()
     total = jnp.int32(0)
@@ -200,19 +205,27 @@
             total = total + keep.astype(jnp.int32)
         if i == 0:
             own_total = total
+    for j in range(BATCH):
+        for part in range(4):
+            list_s[part, total + j] = 0
+    batches = lax.div(total + BATCH - 1, BATCH)
 
     rows = table_rows(nx)
 
-    def pick(e, carry):
+    def pick(batch, carry):
+        for j in range(BATCH):
+            pick_one(batch * BATCH + j)
+        return carry
+
+    def pick_one(e):
         place = list_s[3, e]
         owner = lax.shift_right_logical(place, 3)
         column, line = lax.rem(owner, ny), lax.div(owner, ny)
         at = column * rows + lax.rem(line, rows)
         pick_v[pl.ds(e, 1), :] = tab_ref[pl.ds(at, 1), :]
         which_v[pl.ds(e, 1), :] = jnp.broadcast_to(lax.div(line, rows) * GROUP + (place & 7), (1, LANES))
-        return carry
-
-    lax.fori_loop(0, total, pick, 0)
+
+    lax.fori_loop(0, batches, pick, 0)
     lanes = lax.broadcasted_iota(jnp.int32, pick_v.shape, 1)
     for n in range(3):
         chosen = jnp.where(lanes - 8 * n == which_v[...], pick_v[...], 0.0)
@@ -237,53 +250,56 @@
         def _():
             ref[:, :, YO + cy : YO + cy + 1, :] = jnp.zeros((ref.shape[0], 2, 1, LANES), jnp.float32)
 
+    first = lax.broadcasted_iota(jnp.int32, (8, LANES), 1) == 0
+    last = lax.broadcasted_iota(jnp.int32, (8, LANES), 1) == LANES - 1
+
+    def spread(ref, x, h, y, tiles, extra=0):
+        return [ref[x, h, pl.ds(y + t, 8, stride=tiles), :] for t in range(-extra, tiles + extra)]
+
     def depth(v0, v1):
-        first = lax.broadcasted_iota(jnp.int32, v0.shape, 1) == 0
-        last = lax.broadcasted_iota(jnp.int32, v0.shape, 1) == LANES - 1
         f0, f1 = pltpu.roll(v0, 1, 1), pltpu.roll(v1, 1, 1)
         b0, b1 = pltpu.roll(v0, LANES - 1, 1), pltpu.roll(v1, LANES - 1, 1)
         before = (jnp.where(first, 0.0, f0), jnp.where(first, f0, f1))
         after = (jnp.where(last, b1, b0), jnp.where(last, 0.0, b1))
         return before, after
 
-    def forward(src, dst, lo, hi, y0, rows):
+    def forward(src, dst, lo, hi, y, tiles):
         def plane(x, carry):
-            mid = [src[x, h, pl.ds(y0, rows), :] for h in range(2)]
-            before, after = depth(*mid)
-            for h in range(2):
-                f = mid[h]
-                pairs = (
-                    (src[x + 1, h, pl.ds(y0, rows), :], src[x - 1, h, pl.ds(y0, rows), :]),
-                    (src[x, h, pl.ds(y0 + 1, rows), :], src[x, h, pl.ds(y0 - 1, rows), :]),
-                    (after[h], before[h]),
-                )
-                lap, adv = -6.0 * f, 0.0
-                for v, (p, m) in zip(VEL, pairs):
-                    both = p + m
-                    lap = lap + both
-                    adv = adv + (0.25 * v) * (both * (p - m))
-                kappa = kap[x, h, pl.ds(y0, rows), :]
-                dst[x, h, pl.ds(y0, rows), :] = f + DT * (kappa * lap - adv)
+            mid = [spread(src, x, h, y, tiles, 1) for h in range(2)]
+            nxt = [spread(src, x + 1, h, y, tiles) for h in range(2)]
+            prv = [spread(src, x - 1, h, y, tiles) for h in range(2)]
+            kappa = [spread(kap, x, h, y, tiles) for h in range(2)]
+            for t in range(tiles):
+                before, after = depth(mid[0][t + 1], mid[1][t + 1])
+                for h in range(2):
+                    f = mid[h][t + 1]
+                    pairs = ((nxt[h][t], prv[h][t]), (mid[h][t + 2], mid[h][t]), (after[h], before[h]))
+                    (sx, sy, sz), (dx, dy, dz) = zip(*[(p + m, p - m) for p, m in pairs])
+                    lap = (sx + sy) + (sz - 6.0 * f)
+                    adv = (0.25 * DT * VEL[0]) * (sx * dx) + ((0.25 * DT * VEL[1]) * (sy * dy) + (0.25 * DT * VEL[2]) * (sz * dz))
+                    dst[x, h, pl.ds(y + t, 8, stride=tiles), :] = f + (kappa[h][t] * lap - adv)
             return carry
 
-        lax.fori_loop(lo, hi, plane, 0)
+        lax.fori_loop(lo, hi, plane, 0, unroll=True)
 
     def actuate(n, dst):
-        def one(e, carry):
-            x, h, y = list_s[0, e], list_s[1, e], list_s[2, e]
-            dst[x, h, pl.ds(y, 1), :] += amp_v[n, pl.ds(e, 1), :]
+        def some(batch, carry):
+            for j in range(BATCH):
+                e = batch * BATCH + j
+                x, h, y = list_s[0, e], list_s[1, e], list_s[2, e]
+                dst[x, h, pl.ds(y, 1), :] += amp_v[n, pl.ds(e, 1), :]
             return carry
 
-        lax.fori_loop(0, total, one, 0)
+        lax.fori_loop(0, batches, some, 0)
         clear_outside(dst)
 
-    forward(s0, s1, XO - 5, XO, 8, 40)
-    forward(s0, s1, XO, XO + cx, 4, 48)
-    forward(s0, s1, XO + cx, XO + cx + 5, 8, 40)
+    forward(s0, s1, XO - 5, XO, YO - 4, 5)
+    forward(s0, s1, XO, XO + cx, YO - 5, 6)
+    forward(s0, s1, XO + cx, XO + cx + 5, YO - 4, 5)
     actuate(0, s1)
-    forward(s1, s2, XO - 4, XO + cx + 4, 8, 40)
+    forward(s1, s2, XO - 4, XO + cx + 4, YO - 4, 5)
     actuate(1, s2)
-    forward(s2, s3, XO - 3, XO + cx + 3, 8, 40)
+    forward(s2, s3, XO - 3, XO + cx + 3, YO - 3, 5)
     actuate(2, s3)
 
     def scale(x, carry):
@@ -291,36 +307,40 @@
             qa[x, h] = kap[x, h] * a4[x, h]
         return carry
 
-    lax.fori_loop(XO - 4, XO + cx + 4, scale, 0)
-
-    def step(adj, q, state, x, y0, rows):
-        mid = [adj[x, h, pl.ds(y0, rows), :] for h in range(2)]
-        qmid = [q[x, h, pl.ds(y0, rows), :] for h in range(2)]
-        before, after = depth(*mid)
-        qbefore, qafter = depth(*qmid)
-        result = []
-        for h in range(2):
-            lap = (
-                (q[x + 1, h, pl.ds(y0, rows), :] + q[x - 1, h, pl.ds(y0, rows), :])
-                + (q[x, h, pl.ds(y0 + 1, rows), :] + q[x, h, pl.ds(y0 - 1, rows), :])
-                + (qafter[h] + qbefore[h])
-            ) - 6.0 * qmid[h]
-            drift = (
-                (0.5 * VEL[0]) * (adj[x + 1, h, pl.ds(y0, rows), :] - adj[x - 1, h, pl.ds(y0, rows), :])
-                + (0.5 * VEL[1]) * (adj[x, h, pl.ds(y0 + 1, rows), :] - adj[x, h, pl.ds(y0 - 1, rows), :])
-                + (0.5 * VEL[2]) * (after[h] - before[h])
-            )
-            result.append(mid[h] + DT * (lap + state[x, h, pl.ds(y0, rows), :] * drift))
-        return result
+    lax.fori_loop(XO - 4, XO + cx + 4, scale, 0, unroll=True)
+
+    def step(adj, q, state, x, y, tiles, emit):
+        mid = [spread(adj, x, h, y, tiles, 1) for h in range(2)]
+        qmid = [spread(q, x, h, y, tiles, 1) for h in range(2)]
+        for t in range(tiles):
+            before, after = depth(mid[0][t + 1], mid[1][t + 1])
+            qbefore, qafter = depth(qmid[0][t + 1], qmid[1][t + 1])
+            for h in range(2):
+                at = pl.ds(y + t, 8, stride=tiles)
+                lap = (
+                    (q[x + 1, h, at, :] + q[x - 1, h, at, :])
+                    + (qmid[h][t + 2] + qmid[h][t])
+                    + ((qafter[h] + qbefore[h]) - 6.0 * qmid[h][t + 1])
+                )
+                drift = (
+                    (0.5 * DT * VEL[0]) * (adj[x + 1, h, at, :] - adj[x - 1, h, at, :])
+                    + (0.5 * DT * VEL[1]) * (mid[h][t + 2] - mid[h][t])
+                    + (0.5 * DT * VEL[2]) * (after[h] - before[h])
+                )
+                emit(h, t, at, mid[h][t + 1] + (lap + state[x, h, at, :] * drift))
 
     def backward(adj, q, state, dst, qdst, wide):
+        y = YO - wide
+
         def plane(x, carry):
-            for h, value in enumerate(step(adj, q, state, x, 8, 40)):
-                dst[x, h, pl.ds(8, 40), :] = value
-                qdst[x, h, pl.ds(8, 40), :] = kap[x, h, pl.ds(8, 40), :] * value
+            def emit(h, t, at, value):
+                dst[x, h, at, :] = value
+                qdst[x, h, at, :] = kap[x, h, at, :] * value
+
+            step(adj, q, state, x, y, 5, emit)
             return carry
 
-        lax.fori_loop(XO - wide, XO + cx + wide, plane, 0)
+        lax.fori_loop(XO - wide, XO + cx + wide, plane, 0, unroll=True)
         clear_outside(dst)
 
     backward(a4, qa, s3, a3, qb, 3)
@@ -328,11 +348,16 @@
     backward(a2, qa, s1, a1, qb, 1)
 
     def final(x, carry):
-        for h, value in enumerate(step(a1, qb, s0, XO + x, YO, cy)):
-            out_ref[x, :, halves[h]] = value
+        def emit(h, t, at, value):
+            res[x, h, pl.ds(t, 8, stride=cy // 8), :] = value
+
+        step(a1, qb, s0, XO + x, YO, cy // 8, emit)
         return carry
 
-    lax.fori_loop(0, cx, final, 0)
+    lax.fori_loop(0, cx, final, 0, unroll=True)
+    writes = [pltpu.make_async_copy(res.at[:, h], out_ref.at[:, :, halves[h]], out_sems.at[h]) for h in range(2)]
+    for write in writes:
+        write.start()
 
     msg_ref[...] = jnp.zeros(msg_ref.shape, jnp.float32)
 
@@ -355,6 +380,8 @@
         return carry
 
     lax.fori_loop(0, own_total, post, 0)
+    for write in writes:
+        write.wait()
 
 
 def gradient_kernel(ny, got_ref, own_ref, free_ref, out_ref):
@@ -431,17 +458,19 @@
         functools.partial(window_kernel, cx, cy, nx, ny),
         out_shape=[shape(cx, cy, cz), shape(ndev, LANES)],
         in_specs=[VM] * 9,
-        out_specs=[VM] * 2,
+        out_specs=[ANY, VM],
         scratch_shapes=[ext] * 11
         + [
             pltpu.VMEM((16, LANES), jnp.int32),
             pltpu.SMEM((16, LANES), jnp.int32),
             pltpu.SMEM((4, 160), jnp.int32),
-            pltpu.VMEM((144, LANES), f32),
-            pltpu.VMEM((144, LANES), jnp.int32),
-            pltpu.VMEM((3, 144, LANES), f32),
+            pltpu.VMEM((152, LANES), f32),
+            pltpu.VMEM((152, LANES), jnp.int32),
+            pltpu.VMEM((3, 152, LANES), f32),
             pltpu.VMEM((4, 16, LANES), f32),
             pltpu.SemaphoreType.DMA,
+            pltpu.VMEM((cx, 2, cy, LANES), f32),
+            pltpu.SemaphoreType.DMA((2,)),
         ],
         compiler_params=pltpu.CompilerParams(vmem_limit_bytes=48 << 20),
         name="window",

time: 111 us -> 98.5 us (0.89)
  Pallas kernels: 27 us -> 14.5 us
    pallas_call x1, Pallas kernels: 21.7 us -> 9.27 us  [shards(): pl.pallas_call(functools.partial(window_kernel, cx, cy, nx, ny), out_shap...]
where the time goes in v3:
time: 98.5 us; the launch traced here: 98 us
  blocking collectives  69.5 us (71%)
  Pallas kernels  14.5 us (15%)
  starting transfers between devices  12.6 us (13%)
  between operations  1.4 us (1%)
    all_to_all x1, blocking collectives, shards(): got = lax.all_to_all(message, AXES, 0, 0, tiled=True)  28.6 us
    all_to_all x1, blocking collectives, shards(): lax.all_to_all(table, 'gy', 0, 0, tiled=True).reshape(ny * rows, LANES)  22.9 us
    all_to_all x1, blocking collectives, shards(): got = lax.all_to_all(row, 'gx', 0, 0, tiled=True)  18 us
    ppermute x4, starting transfers between devices, shift(): return lax.ppermute(value, axis, pairs)  12.6 us
    pallas_call x1, Pallas kernels, shards(): pl.pallas_call(functools.partial(window_kernel, cx, cy, nx, ny), out_shap...  9.27 us
    pallas_call x1, Pallas kernels, shards(): pl.pallas_call(functools.partial(first_kernel, cx, cy), out_shape=[shape(...  2.99 us
  transfers between devices with their start and end apart: 4, of which 0 were waited for; matrix products, arithmetic and copies ran while one was open for 0% of the time, Pallas kernels for 0%

profile of v3, /device:TPU:1, one launch (start us, length us, event | category | flops | bytes accessed | tf_op | source)
XLA Modules:
  0.0 98.0 jit_solution(13618695476816700720)
XLA Ops:
  1.3 0.0 copy-start
  1.3 0.0 copy-start.1
  1.3 0.0 copy-start.2
  1.3 3.0 %first.1 = (f32[16,2,16,128]{3,2,1,0:T(8,128)}, f32[16,2,16,128]{3,2,1,0:T(8,128)}, f32[8,128]{1,0:T(8,128)}, f32[32,128]{1,0:T(8,128)}) custom-call(f32[16,32,256]{2,1,0:T(8,128)} %ck_ref.5, f32[16,32,256]{2,1,0:T(8,128)} %kp_ref.5, f32[16,32,256]{2,1,0:T(8,128)} %ta_ref.5, s32[4096]{0:T(1024)} %own_ref.1, f32[4,8]{1,0:T(4,128)} %ctl_ref.1, s32[16]{0:T(128)} %act_ref.1, ...), custom_call_target="tpu_custom_call" | custom-call | tf_op jit(solution)/shard_map/first/pallas_call | solution.py:427
  4.3 6.6 %collective-permute-start = (f32[16,2,16,128]{3,2,1,0:T(8,128)}, f32[16,2,16,128]{3,2,1,0:T(8,128)S(1)}, u32[]{:S(2)}, u32[]{:S(2)}) collective-permute-start(f32[16,2,16,128]{3,2,1,0:T(8,128)} %get-tuple-element.11), channel_id=1, source_target_pairs={{0,1},{1,2},{2,3},{3,4},{4,5},{5,6},{6,7},{7,8},{8,9},{9,10},{10,1... | collective-permute-start | bytes 786440 | tf_op jit(solution)/shard_map/ppermute | solution.py:424
  11.0 1.3 %collective-permute-start.1 = (f32[16,2,16,128]{3,2,1,0:T(8,128)}, f32[16,2,16,128]{3,2,1,0:T(8,128)S(1)}, u32[]{:S(2)}, u32[]{:S(2)}) collective-permute-start(f32[16,2,16,128]{3,2,1,0:T(8,128)} %get-tuple-element.12), channel_id=1, source_target_pairs={{1,0},{2,1},{3,2},{4,3},{5,4},{6,5},{7,6},{8,7},{9,8},{10,9},{11,1... | collective-permute-start | bytes 786440 | tf_op jit(solution)/shard_map/ppermute | solution.py:424
  12.3 0.0 copy-start.3
  12.3 18.0 %all_to_all.27 = f32[32,1,128]{2,1,0:T(1,128)S(1)} all-to-all(f32[32,1,128]{2,1,0:T(1,128)} %bitcast.15), channel_id=1, replica_groups=mesh['gx'=32,'gy'=16] {'gx'}, dimensions={0} | all-to-all | bytes 32768 | tf_op jit(solution)/shard_map/all_to_all | solution.py:442
  30.2 0.0 collective-permute-done.yup_ref
  30.2 0.0 collective-permute-done.1.ydn_ref
  30.2 0.0 copy-done
  30.2 0.0 copy-done.1
  30.3 0.0 copy-done.2
  30.3 0.0 copy-done.3
  30.3 0.3 second.1
  30.6 2.8 %collective-permute-start.2 = (f32[17,2,32,128]{3,2,1,0:T(8,128)S(1)}, f32[17,2,32,128]{3,2,1,0:T(8,128)S(1)}, u32[]{:S(2)}, u32[]{:S(2)}) collective-permute-start(f32[17,2,32,128]{3,2,1,0:T(8,128)S(1)} %get-tuple-element.15), channel_id=1, source_target_pairs={{0,16},{16,32},{32,48},{48,64},{64,80},{80,96},{96,112},{112,128},... | collective-permute-start | bytes 1671176 | tf_op jit(solution)/shard_map/ppermute | solution.py:424
  33.3 1.9 %collective-permute-start.3 = (f32[17,2,32,128]{3,2,1,0:T(8,128)S(1)}, f32[17,2,32,128]{3,2,1,0:T(8,128)S(1)}, u32[]{:S(2)}, u32[]{:S(2)}) collective-permute-start(f32[17,2,32,128]{3,2,1,0:T(8,128)S(1)} %get-tuple-element.16), channel_id=1, source_target_pairs={{16,0},{32,16},{48,32},{64,48},{80,64},{96,80},{112,96},{128,112},... | collective-permute-start | bytes 1671176 | tf_op jit(solution)/shard_map/ppermute | solution.py:424
  35.3 22.9 %all_to_all.28 = f32[16,8,128]{2,1,0:T(8,128)S(1)} all-to-all(f32[16,8,128]{2,1,0:T(8,128)S(1)} %get-tuple-element.17), channel_id=1, replica_groups=mesh['gx'=32,'gy'=16] {'gy'}, dimensions={0} | all-to-all | bytes 131072 | tf_op jit(solution)/shard_map/all_to_all | solution.py:454
  58.2 0.0 collective-permute-done.2.xup_ref
  58.2 0.0 collective-permute-done.3.xdn_ref
  58.2 9.3 %window.1 = (f32[16,32,256]{2,1,0:T(8,128)}, f32[512,128]{1,0:T(8,128)S(1)}) custom-call(f32[16,32,256]{2,1,0:T(8,128)S(1)} %copy-done, f32[16,32,256]{2,1,0:T(8,128)S(1)} %copy-done.1, f32[16,32,256]{2,1,0:T(8,128)S(1)} %copy-done.2, f32[16,2,16,128]{3,2,1,0:T(8,128)S(1)} %collective-permute-done.yup_ref, ...), custom_call_target="tpu_custom_call" | custom-call | tf_op jit(solution)/shard_map/window/pallas_call | solution.py:457
  67.5 28.6 %all_to_all.29 = f32[512,1,128]{2,1,0:T(1,128)} all-to-all(f32[512,1,128]{2,1,0:T(1,128)S(1)} %bitcast.11), channel_id=1, replica_groups=mesh['gx'=32,'gy'=16] {'gx','gy'}, dimensions={0} | all-to-all | bytes 524288 | tf_op jit(solution)/shard_map/all_to_all | solution.py:479
  96.1 2.0 %gradient.1 = f32[4,8]{1,0:T(4,128)} custom-call(f32[512,128]{1,0:T(8,128)} %bitcast.13, s32[32,128]{1,0:T(8,128)} %bitcast.14, s32[4,2048]{1,0:T(4,128)} %free_ref.1), custom_call_target="tpu_custom_call" | custom-call | tf_op jit(solution)/shard_map/gradient/pallas_call | solution.py:480
Async XLA Ops:
  1.3 29.0 %copy-start = (f32[16,32,256]{2,1,0:T(8,128)S(1)}, f32[16,32,256]{2,1,0:T(8,128)}, u32[]{:S(2)}) copy-start(f32[16,32,256]{2,1,0:T(8,128)} %ck_ref.5) | copy-start | bytes 1572868
  1.3 29.0 %copy-start.1 = (f32[16,32,256]{2,1,0:T(8,128)S(1)}, f32[16,32,256]{2,1,0:T(8,128)}, u32[]{:S(2)}) copy-start(f32[16,32,256]{2,1,0:T(8,128)} %kp_ref.5) | copy-start | bytes 1572868
  1.3 29.0 %copy-start.2 = (f32[16,32,256]{2,1,0:T(8,128)S(1)}, f32[16,32,256]{2,1,0:T(8,128)}, u32[]{:S(2)}) copy-start(f32[16,32,256]{2,1,0:T(8,128)} %ta_ref.5) | copy-start | bytes 1572868
  4.3 25.9 %collective-permute-start = (f32[16,2,16,128]{3,2,1,0:T(8,128)}, f32[16,2,16,128]{3,2,1,0:T(8,128)S(1)}, u32[]{:S(2)}, u32[]{:S(2)}) collective-permute-start(f32[16,2,16,128]{3,2,1,0:T(8,128)} %get-tuple-element.11), channel_id=1, source_target_pairs={{0,1},{1,2},{2,3},{3,4},{4,5},{5,6},{6,7},{7,8},{8,9},{9,10},{10,1... | collective-permute-start | bytes 786440 | tf_op jit(solution)/shard_map/ppermute | solution.py:424
  11.0 19.3 %collective-permute-start.1 = (f32[16,2,16,128]{3,2,1,0:T(8,128)}, f32[16,2,16,128]{3,2,1,0:T(8,128)S(1)}, u32[]{:S(2)}, u32[]{:S(2)}) collective-permute-start(f32[16,2,16,128]{3,2,1,0:T(8,128)} %get-tuple-element.12), channel_id=1, source_target_pairs={{1,0},{2,1},{3,2},{4,3},{5,4},{6,5},{7,6},{8,7},{9,8},{10,9},{11,1... | collective-permute-start | bytes 786440 | tf_op jit(solution)/shard_map/ppermute | solution.py:424
  12.3 18.0 %copy-start.3 = (f32[8,128]{1,0:T(8,128)S(1)}, f32[8,128]{1,0:T(8,128)}, u32[]{:S(2)}) copy-start(f32[8,128]{1,0:T(8,128)} %get-tuple-element.13.ids_ref) | copy-start | bytes 12292
  30.6 27.6 %collective-permute-start.2 = (f32[17,2,32,128]{3,2,1,0:T(8,128)S(1)}, f32[17,2,32,128]{3,2,1,0:T(8,128)S(1)}, u32[]{:S(2)}, u32[]{:S(2)}) collective-permute-start(f32[17,2,32,128]{3,2,1,0:T(8,128)S(1)} %get-tuple-element.15), channel_id=1, source_target_pairs={{0,16},{16,32},{32,48},{48,64},{64,80},{80,96},{96,112},{112,128},... | collective-permute-start | bytes 1671176 | tf_op jit(solution)/shard_map/ppermute | solution.py:424
  33.3 24.9 %collective-permute-start.3 = (f32[17,2,32,128]{3,2,1,0:T(8,128)S(1)}, f32[17,2,32,128]{3,2,1,0:T(8,128)S(1)}, u32[]{:S(2)}, u32[]{:S(2)}) collective-permute-start(f32[17,2,32,128]{3,2,1,0:T(8,128)S(1)} %get-tuple-element.16), channel_id=1, source_target_pairs={{16,0},{32,16},{48,32},{64,48},{80,64},{96,80},{112,96},{128,112},... | collective-permute-start | bytes 1671176 | tf_op jit(solution)/shard_map/ppermute | solution.py:424

commit v4 on v3

v4 whole, which is shorter than its diff:
```python
import functools

import jax
import jax.numpy as jnp
from jax import lax
from jax.experimental import pallas as pl
from jax.experimental.pallas import tpu as pltpu
from jax.sharding import PartitionSpec as P

TZ = 128
DT = 0.05
VEL = (1.0, 0.7, 0.4)
AXES = ("gx", "gy")

WIDE = (6, 5, 4)
LAYERS = sum(WIDE)
XO = 6
YO = 12
YR = 56
LANES = 128
ROW = 32
LISTED = 160
BATCH = 4
CODE = 1024


def corner_pieces():
    pieces, row = [], 0
    for field, wide in enumerate(WIDE):
        for layer in range(1, wide):
            pieces.append((field, layer, wide - layer, row))
            row += wide - layer
    return pieces, -(-row // 8) * 8


CORNER, CORNER_ROWS = corner_pieces()


def first_kernel(
    cx, cy, ck_ref, kp_ref, ta_ref, own_ref, act_ref, til_ref, cnt_ref,
    yup_ref, ydn_ref, xup_ref, xdn_ref, ids_ref, low, high, own_s, sems, plane_sems,
):
    planes = []
    at = 0
    for field, wide in zip((ck_ref, kp_ref, ta_ref), WIDE):
        for h in range(2):
            half = slice(h * LANES, (h + 1) * LANES)
            for ref, x in ((xup_ref, cx - wide), (xdn_ref, 0)):
                planes.append(
                    pltpu.make_async_copy(
                        field.at[x : x + wide, :, half], ref.at[at : at + wide, h], plane_sems.at[len(planes)]
                    )
                )
        at += wide
    copies = [pltpu.make_async_copy(own_ref, own_s, sems.at[6])]
    for f, field in enumerate((ck_ref, kp_ref, ta_ref)):
        copies.append(pltpu.make_async_copy(field.at[:, 0:8, :], low.at[f], sems.at[2 * f]))
        copies.append(pltpu.make_async_copy(field.at[:, cy - 8 : cy, :], high.at[f], sems.at[2 * f + 1]))
    for copy in copies + planes:
        copy.start()
    lane = lax.broadcasted_iota(jnp.int32, (1, LANES), 1)
    copies[0].wait()
    ids = jnp.zeros((1, LANES), jnp.int32)
    for j in range(act_ref.shape[0]):
        code = jnp.where(j < cnt_ref[0], own_s[act_ref[j]] * CODE + til_ref[j] + 1, 0)
        ids = jnp.where(lane == j, code, ids)
    ids = ids.astype(jnp.float32)
    ids_ref[...] = jnp.broadcast_to(ids, ids_ref.shape)
    for copy in copies[1:]:
        copy.wait()
    halves = (slice(0, LANES), slice(LANES, 2 * LANES))

    def rows(x, carry):
        at = 0
        for f, wide in enumerate(WIDE):
            for h in range(2):
                yup_ref[x, h, at : at + wide, :] = high[f, x, 8 - wide : 8, halves[h]]
                ydn_ref[x, h, at : at + wide, :] = low[f, x, 0:wide, halves[h]]
            at += wide
        return carry

    lax.fori_loop(0, cx, rows, 0, unroll=4)
    yup_ref[0, 0, LAYERS : LAYERS + 1, :] = ids
    ydn_ref[0, 0, LAYERS : LAYERS + 1, :] = ids
    for copy in planes:
        copy.wait()


def row_kernel(ctl_ref, ids_ref, row_ref):
    lane = lax.broadcasted_iota(jnp.int32, (1, ROW), 1)
    row = ids_ref[0:1, 0:ROW]
    steps, owned = ctl_ref.shape
    for n in range(steps):
        for k in range(owned):
            row = jnp.where(lane == n * owned + k, ctl_ref[n, k], row)
    row_ref[...] = jnp.broadcast_to(row, row_ref.shape)


def corner_kernel(cx, cy, yup_ref, ydn_ref, ids_ref, up_ref, dn_ref):
    for f, layer, count, start in CORNER:
        top = sum(WIDE[: f + 1])
        at = top - WIDE[f]
        for ref, x in ((up_ref, cx - layer), (dn_ref, layer - 1)):
            for h in range(2):
                ref[0, h, start : start + count, :] = yup_ref[x, h, top - count : top, :]
                ref[1, h, start : start + count, :] = ydn_ref[x, h, at : at + count, :]
    tail = slice(CORNER_ROWS - 1, CORNER_ROWS)
    for ref in (up_ref, dn_ref):
        ref[0, 0, tail, :] = ids_ref[0:1, :]
        ref[0, 1, tail, :] = yup_ref[0, 0, LAYERS : LAYERS + 1, :]
        ref[1, 0, tail, :] = ydn_ref[0, 0, LAYERS : LAYERS + 1, :]


def ends():
    lane = lax.broadcasted_iota(jnp.int32, (8, LANES), 1)
    return lane == 0, lane == LANES - 1


def spread(ref, x, h, y, tiles, extra=0):
    return [ref[x, h, pl.ds(y + t, 8, stride=tiles), :] for t in range(-extra, tiles + extra)]


def depth(v0, v1):
    first, last = ends()
    f0, f1 = pltpu.roll(v0, 1, 1), pltpu.roll(v1, 1, 1)
    b0, b1 = pltpu.roll(v0, LANES - 1, 1), pltpu.roll(v1, LANES - 1, 1)
    before = (jnp.where(first, 0.0, f0), jnp.where(first, f0, f1))
    after = (jnp.where(last, b1, b0), jnp.where(last, 0.0, b1))
    return before, after


def forward(src, dst, kap, lo, hi, y, tiles):
    def plane(x, carry):
        mid = [spread(src, x, h, y, tiles, 1) for h in range(2)]
        nxt = [spread(src, x + 1, h, y, tiles) for h in range(2)]
        prv = [spread(src, x - 1, h, y, tiles) for h in range(2)]
        kappa = [spread(kap, x, h, y, tiles) for h in range(2)]
        for t in range(tiles):
            before, after = depth(mid[0][t + 1], mid[1][t + 1])
            for h in range(2):
                f = mid[h][t + 1]
                pairs = ((nxt[h][t], prv[h][t]), (mid[h][t + 2], mid[h][t]), (after[h], before[h]))
                (sx, sy, sz), (dx, dy, dz) = zip(*[(p + m, p - m) for p, m in pairs])
                lap = (sx + sy) + (sz - 6.0 * f)
                adv = (0.25 * DT * VEL[0]) * (sx * dx) + ((0.25 * DT * VEL[1]) * (sy * dy) + (0.25 * DT * VEL[2]) * (sz * dz))
                dst[x, h, pl.ds(y + t, 8, stride=tiles), :] = f + (kappa[h][t] * lap - adv)
        return carry

    lax.fori_loop(lo, hi, plane, 0, unroll=True)


def step(adj, q, state, x, y, tiles, emit):
    mid = [spread(adj, x, h, y, tiles, 1) for h in range(2)]
    qmid = [spread(q, x, h, y, tiles, 1) for h in range(2)]
    for t in range(tiles):
        before, after = depth(mid[0][t + 1], mid[1][t + 1])
        qbefore, qafter = depth(qmid[0][t + 1], qmid[1][t + 1])
        for h in range(2):
            at = pl.ds(y + t, 8, stride=tiles)
            lap = (
                (q[x + 1, h, at, :] + q[x - 1, h, at, :])
                + (qmid[h][t + 2] + qmid[h][t])
                + ((qafter[h] + qbefore[h]) - 6.0 * qmid[h][t + 1])
            )
            drift = (
                (0.5 * DT * VEL[0]) * (adj[x + 1, h, at, :] - adj[x - 1, h, at, :])
                + (0.5 * DT * VEL[1]) * (mid[h][t + 2] - mid[h][t])
                + (0.5 * DT * VEL[2]) * (after[h] - before[h])
            )
            emit(h, t, at, mid[h][t + 1] + (lap + state[x, h, at, :] * drift))


def assemble_kernel(
    cx, cy, nx, ny, ck_ref, kp_ref, ta_ref,
    yup_ref, ydn_ref, xup_ref, xdn_ref, cup_ref, cdn_ref, ids_ref,
    s0, s1, kap, a4, qa, list_s, near_v, near_s, sem,
):
    halves = (slice(0, LANES), slice(LANES, 2 * LANES))

    spare = slice(LAYERS, LAYERS + 1)
    tail = slice(CORNER_ROWS - 1, CORNER_ROWS)
    near = (
        ((0, 0), ids_ref[0:1, :]),
        ((0, -1), yup_ref[0, 0, spare, :]),
        ((0, 1), ydn_ref[0, 0, spare, :]),
        ((-1, 0), cup_ref[0, 0, tail, :]),
        ((-1, -1), cup_ref[0, 1, tail, :]),
        ((-1, 1), cup_ref[1, 0, tail, :]),
        ((1, 0), cdn_ref[0, 0, tail, :]),
        ((1, -1), cdn_ref[0, 1, tail, :]),
        ((1, 1), cdn_ref[1, 0, tail, :]),
    )
    for i, (_, codes) in enumerate(near):
        near_v[i : i + 1, :] = codes.astype(jnp.int32) - 1
    ids = pltpu.make_async_copy(near_v, near_s, sem)
    ids.start()

    fields = ((ck_ref, s0), (kp_ref, kap), (ta_ref, a4))
    for f, (own, ext) in enumerate(fields):
        wide, at = WIDE[f], sum(WIDE[:f])

        def take(value, f=f):
            return DT * value if f == 1 else value

        def assemble(x, carry, own=own, ext=ext, wide=wide, at=at, take=take):
            for h in range(2):
                ext[XO + x, h, YO : YO + cy, :] = take(own[x, :, halves[h]])
                ext[XO + x, h, YO - wide : YO, :] = take(yup_ref[x, h, at : at + wide, :])
                ext[XO + x, h, YO + cy : YO + cy + wide, :] = take(ydn_ref[x, h, at : at + wide, :])
            return carry

        lax.fori_loop(0, cx, assemble, 0, unroll=True)
        for i in range(wide):
            for h in range(2):
                ext[XO - wide + i, h, YO : YO + cy, :] = take(xup_ref[at + i, h])
                ext[XO + cx + i, h, YO : YO + cy, :] = take(xdn_ref[at + i, h])
        for c, layer, count, start in CORNER:
            if c != f:
                continue
            for ref, x in ((cup_ref, XO - layer), (cdn_ref, XO + cx + layer - 1)):
                for h in range(2):
                    ext[x, h, YO - count : YO, :] = take(ref[0, h, start : start + count, :])
                    ext[x, h, YO + cy : YO + cy + count, :] = take(ref[1, h, start : start + count, :])

    ids.wait()
    total = jnp.int32(0)
    own_total = jnp.int32(0)
    for i, ((a, b), _) in enumerate(near):
        for j in range(16):
            code = near_s[i, j]
            place = lax.shift_right_arithmetic(code, 10)
            tile = code & (CODE - 1)
            x = lax.shift_right_logical(tile, 6) + (XO + a * cx)
            y = (lax.shift_right_logical(tile, 1) & (cy - 1)) + (YO + b * cy)
            keep = place >= 0
            if a != 0:
                keep &= (x >= XO - 5) & (x < XO + cx + 5)
            if b != 0:
                keep &= (y >= YO - 5) & (y < YO + cy + 5)
            list_s[0, total] = x
            list_s[1, total] = tile & 1
            list_s[2, total] = y
            list_s[3, total] = place
            total = total + keep.astype(jnp.int32)
        if i == 0:
            own_total = total
    for j in range(BATCH):
        for part in range(4):
            list_s[part, total + j] = 0
    list_s[0, LISTED] = total
    list_s[1, LISTED] = own_total

    forward(s0, s1, kap, XO - 5, XO, YO - 4, 5)
    forward(s0, s1, kap, XO, XO + cx, YO - 5, 6)
    forward(s0, s1, kap, XO + cx, XO + cx + 5, YO - 4, 5)

    def scale(x, carry):
        for h in range(2):
            qa[x, h] = kap[x, h] * a4[x, h]
        return carry

    lax.fori_loop(XO - 4, XO + cx + 4, scale, 0, unroll=True)


def window_kernel(
    cx, cy, nx, ny, s0, s1_ref, kap, a4, qa_ref, tab_ref, list_s,
    a1, qb, msg_ref, s1, s2, s3, a3, a2, qa, pick_v, which_v, amp_v, sum_v,
):
    gx = lax.axis_index("gx")
    gy = lax.axis_index("gy")
    total, own_total = list_s[0, LISTED], list_s[1, LISTED]
    batches = lax.div(total + BATCH - 1, BATCH)

    def pick(batch, carry):
        for j in range(BATCH):
            pick_one(batch * BATCH + j)
        return carry

    def pick_one(e):
        place = list_s[3, e]
        pick_v[pl.ds(e, 1), :] = tab_ref[pl.ds(lax.shift_right_logical(place, 3), 1), :]
        which_v[pl.ds(e, 1), :] = jnp.broadcast_to(place & 7, (1, ROW))

    lax.fori_loop(0, batches, pick, 0)
    lanes = lax.broadcasted_iota(jnp.int32, pick_v.shape, 1)
    for n in range(3):
        chosen = jnp.where(lanes - 8 * n == which_v[...], pick_v[...], 0.0)
        amp_v[n] = jnp.broadcast_to(DT * jnp.sum(chosen, axis=1, keepdims=True), amp_v.shape[1:])

    lo_x, hi_x, lo_y, hi_y = gx == 0, gx == nx - 1, gy == 0, gy == ny - 1

    def clear_outside(ref):
        @pl.when(lo_x)
        def _():
            ref[XO - 1] = jnp.zeros(ref.shape[1:], jnp.float32)

        @pl.when(hi_x)
        def _():
            ref[XO + cx] = jnp.zeros(ref.shape[1:], jnp.float32)

        @pl.when(lo_y)
        def _():
            ref[:, :, YO - 1 : YO, :] = jnp.zeros((ref.shape[0], 2, 1, LANES), jnp.float32)

        @pl.when(hi_y)
        def _():
            ref[:, :, YO + cy : YO + cy + 1, :] = jnp.zeros((ref.shape[0], 2, 1, LANES), jnp.float32)

    def actuate(n, dst):
        def some(batch, carry):
            for j in range(BATCH):
                e = batch * BATCH + j
                x, h, y = list_s[0, e], list_s[1, e], list_s[2, e]
                dst[x, h, pl.ds(y, 1), :] += amp_v[n, pl.ds(e, 1), :]
            return carry

        lax.fori_loop(0, batches, some, 0)
        clear_outside(dst)

    for x in range(XO - 5, XO + cx + 5):
        s1[x] = s1_ref[x]
    actuate(0, s1)
    forward(s1, s2, kap, XO - 4, XO + cx + 4, YO - 4, 5)
    actuate(1, s2)
    forward(s2, s3, kap, XO - 3, XO + cx + 3, YO - 3, 5)
    actuate(2, s3)

    def backward(adj, q, state, dst, qdst, wide):
        y = YO - wide

        def plane(x, carry):
            def emit(h, t, at, value):
                dst[x, h, at, :] = value
                qdst[x, h, at, :] = kap[x, h, at, :] * value

            step(adj, q, state, x, y, 5, emit)
            return carry

        lax.fori_loop(XO - wide, XO + cx + wide, plane, 0, unroll=True)
        clear_outside(dst)

    backward(a4, qa_ref, s3, a3, qb, 3)
    backward(a3, qb, s2, a2, qa, 2)
    backward(a2, qa, s1, a1, qb, 1)

    msg_ref[...] = jnp.zeros(msg_ref.shape, jnp.float32)

    def foot(e, carry):
        x, h, y = list_s[0, e], list_s[1, e], list_s[2, e]
        for n, adj in enumerate((a1, a2, a3, a4)):
            sum_v[n, pl.ds(e, 1), :] = adj[x, h, pl.ds(y, 1), :]
        return carry

    lax.fori_loop(0, own_total, foot, 0)
    part = jnp.zeros((16, ROW), jnp.float32)
    for n in range(4):
        sums = DT * jnp.sum(sum_v[n], axis=1, keepdims=True)
        part = jnp.where(lanes[:16] - 8 * n == which_v[0:16, :], sums, part)
    sum_v[0, :, 0:ROW] = part

    def post(e, carry):
        at = pl.ds(lax.shift_right_logical(list_s[3, e], 3), 1)
        msg_ref[at, :] += sum_v[0, pl.ds(e, 1), 0:ROW]
        return carry

    lax.fori_loop(0, own_total, post, 0)


def final_kernel(cx, cy, ny, a1, qb, s0, own_ref, free_ref, out_ref, flag_ref, res, out_sems):
    def final(x, carry):
        def emit(h, t, at, value):
            res[x, h, pl.ds(t, 8, stride=cy // 8), :] = value

        step(a1, qb, s0, XO + x, YO, cy // 8, emit)
        return carry

    lax.fori_loop(0, cx, final, 0, unroll=True)
    halves = (slice(0, LANES), slice(LANES, 2 * LANES))
    writes = [pltpu.make_async_copy(res.at[:, h], out_ref.at[:, :, halves[h]], out_sems.at[h]) for h in range(2)]
    for write in writes:
        write.start()
    me = lax.axis_index("gx") * ny + lax.axis_index("gy")
    steps, owned = flag_ref.shape
    flat = lax.broadcasted_iota(jnp.int32, own_ref.shape, 0) * LANES + lax.broadcasted_iota(
        jnp.int32, own_ref.shape, 1
    )
    listed = free_ref[...]
    column = lax.broadcasted_iota(jnp.int32, (steps, owned), 1)
    flags = jnp.zeros((steps, owned), jnp.float32)
    for k in range(owned):
        actuator = jnp.sum(jnp.where(own_ref[...] == me * owned + k, flat, 0))
        hit = jnp.max(jnp.where(listed == actuator, 1.0, 0.0), axis=1, keepdims=True)
        flags = jnp.where(column == k, hit, flags)
    flag_ref[...] = flags
    for write in writes:
        write.wait()


def gradient_kernel(got_ref, flag_ref, out_ref):
    steps, owned = out_ref.shape
    total = jnp.sum(got_ref[...], axis=0, keepdims=True)
    for n in range(steps):
        out_ref[n : n + 1, :] = total[:, n * owned : (n + 1) * owned] * flag_ref[n : n + 1, :]


ANY = pl.BlockSpec(memory_space=pl.ANY)
VM = pl.BlockSpec(memory_space=pltpu.VMEM)
SM = pl.BlockSpec(memory_space=pltpu.SMEM)


def shards(
    checkpoint, terminal_adjoint, diffusivity, controls, owner_map, act_ids, slot_tiles, slot_count, free_list,
):
    cx, cy, cz = checkpoint.shape
    nx, ny = lax.axis_size("gx"), lax.axis_size("gy")
    ndev = nx * ny
    f32 = jnp.float32

    def shape(*dims):
        return jax.ShapeDtypeStruct(dims, f32)

    def shift(value, axis, way):
        size = lax.axis_size(axis)
        pairs = [(i, i + way) for i in range(size) if 0 <= i + way < size]
        return lax.ppermute(value, axis, pairs)

    fields = (checkpoint, diffusivity, terminal_adjoint)
    yup, ydn, xup, xdn, ids = pl.pallas_call(
        functools.partial(first_kernel, cx, cy),
        out_shape=[shape(cx, 2, 16, LANES)] * 2 + [shape(LAYERS, 2, cy, LANES)] * 2 + [shape(8, LANES)],
        in_specs=[ANY] * 4 + [SM] * 3,
        out_specs=[VM] * 5,
        scratch_shapes=[
            pltpu.VMEM((3, cx, 8, cz), f32),
            pltpu.VMEM((3, cx, 8, cz), f32),
            pltpu.SMEM(owner_map.shape, jnp.int32),
            pltpu.SemaphoreType.DMA((7,)),
            pltpu.SemaphoreType.DMA((12,)),
        ],
        compiler_params=pltpu.CompilerParams(vmem_limit_bytes=36 << 20),
        name="first",
    )(*fields, owner_map, act_ids, slot_tiles, slot_count)
    yup, ydn = shift(yup, "gy", 1), shift(ydn, "gy", -1)
    xup, xdn = shift(xup, "gx", 1), shift(xdn, "gx", -1)
    row = pl.pallas_call(
        row_kernel, out_shape=shape(ndev, ROW), in_specs=[SM, VM], out_specs=VM, name="row"
    )(controls, ids)
    table = lax.all_to_all(row, AXES, 0, 0, tiled=True)
    cup, cdn = pl.pallas_call(
        functools.partial(corner_kernel, cx, cy),
        out_shape=[shape(2, 2, CORNER_ROWS, LANES)] * 2,
        in_specs=[VM] * 3,
        out_specs=[VM] * 2,
        name="corner",
    )(yup, ydn, ids)
    cup, cdn = shift(cup, "gx", 1), shift(cdn, "gx", -1)

    dims = (cx + 2 * XO, 2, YR, LANES)
    s0, s1, kap, a4, qa, listed = pl.pallas_call(
        functools.partial(assemble_kernel, cx, cy, nx, ny),
        out_shape=[shape(*dims)] * 5 + [jax.ShapeDtypeStruct((4, LISTED + 1), jnp.int32)],
        in_specs=[VM] * 10,
        out_specs=[VM] * 5 + [SM],
        scratch_shapes=[
            pltpu.VMEM((16, LANES), jnp.int32),
            pltpu.SMEM((16, LANES), jnp.int32),
            pltpu.SemaphoreType.DMA,
        ],
        compiler_params=pltpu.CompilerParams(vmem_limit_bytes=24 << 20),
        cost_estimate=pl.CostEstimate(flops=20 << 20, bytes_accessed=12 << 20, transcendentals=0),
        name="assemble",
    )(*fields, yup, ydn, xup, xdn, cup, cdn, ids)

    ext = pltpu.VMEM(dims, f32)
    a1, qb, message = pl.pallas_call(
        functools.partial(window_kernel, cx, cy, nx, ny),
        out_shape=[shape(*dims)] * 2 + [shape(ndev, ROW)],
        in_specs=[VM] * 6 + [SM],
        out_specs=[VM] * 3,
        scratch_shapes=[ext] * 6
        + [
            pltpu.VMEM((152, ROW), f32),
            pltpu.VMEM((152, ROW), jnp.int32),
            pltpu.VMEM((3, 152, LANES), f32),
            pltpu.VMEM((4, 16, LANES), f32),
        ],
        compiler_params=pltpu.CompilerParams(vmem_limit_bytes=32 << 20),
        name="window",
    )(s0, s1, kap, a4, qa, table, listed)

    got = lax.all_to_all(message, AXES, 0, 0, tiled=True)
    start_adjoint, flags = pl.pallas_call(
        functools.partial(final_kernel, cx, cy, ny),
        out_shape=[shape(cx, cy, cz), shape(*controls.shape)],
        in_specs=[VM] * 5,
        out_specs=[ANY, VM],
        scratch_shapes=[pltpu.VMEM((cx, 2, cy, LANES), f32), pltpu.SemaphoreType.DMA((2,))],
        compiler_params=pltpu.CompilerParams(vmem_limit_bytes=24 << 20),
        cost_estimate=pl.CostEstimate(flops=5 << 20, bytes_accessed=4 << 20, transcendentals=0),
        name="final",
    )(a1, qb, s0, owner_map.reshape(-1, LANES), free_list)
    gradient = pl.pallas_call(
        gradient_kernel, out_shape=shape(*controls.shape), in_specs=[VM] * 2, out_specs=VM, name="gradient"
    )(got, flags)
    return start_adjoint, gradient


def solution(mesh):
    placed = (
        P("gx", "gy", None),
        P("gx", "gy", None),
        P("gx", "gy", None),
        P(None, ("gx", "gy")),
        P(),
        P(("gx", "gy")),
        P(("gx", "gy")),
        P(("gx", "gy")),
        P(),
    )
    return jax.shard_map(
        shards,
        mesh=mesh,
        in_specs=placed,
        out_specs=(P("gx", "gy", None), P(None, ("gx", "gy"))),
        check_vma=False,
    )
```

time: 98.5 us -> 130 us (1.32)
  blocking collectives: 69.5 us -> 0 us
  starting transfers between devices: 12.6 us -> 64.6 us
  local copies, waits for them, and re-layouts: 0.02 us -> 27.7 us
  waiting for transfers between devices: 0.01 us -> 16.5 us
  Pallas kernels: 14.5 us -> 18.3 us
    all_to_all x3 -> x0, blocking collectives: 69.5 us -> none  [the longest x1 28.6 us: shards(): got = lax.all_to_all(message, AXES, 0, 0, tiled=True)]
    all_to_all x0 -> x2, starting transfers between devices: none -> 42.7 us  [the longest x1 23.3 us: shards(): table = lax.all_to_all(row, AXES, 0, 0, tiled=True)]
    unnamed x8 -> x68, local copies, waits for them, and re-layouts: 0.02 us -> 27.7 us
    all_to_all x0 -> x2, waiting for transfers between devices: none -> 14 us  [the longest x1 14 us: shards(): got = lax.all_to_all(message, AXES, 0, 0, tiled=True)]
    ppermute x4 -> x6, starting transfers between devices: 12.6 us -> 21.9 us  [shift(): return lax.ppermute(value, axis, pairs)]
    pallas_call x2 -> x5, Pallas kernels: 2.24 us -> 9.49 us  [the longest x1 3.22 us: shards(): pl.pallas_call(functools.partial(assemble_kernel, cx, cy, nx, ny), out_sh...]
    pallas_call x1, Pallas kernels: 9.27 us -> 6.07 us  [shards(): pl.pallas_call(functools.partial(window_kernel, cx, cy, nx, ny), out_shap...]
    ppermute x4 -> x6, waiting for transfers between devices: 0.01 us -> 2.52 us  [shift(): return lax.ppermute(value, axis, pairs)]
  transfers between devices with their start and end apart: 4 -> 8, of which waited for: 0 -> 2; matrix products, arithmetic and copies ran while one was open for 0% -> 0% of each run, Pallas kernels for 0% -> 6%
where the time goes in v4:
time: 130 us; the launch traced here: 129 us
  starting transfers between devices  64.6 us (50%)
  local copies, waits for them, and re-layouts  27.7 us (21%)
  Pallas kernels  18.3 us (14%)
  waiting for transfers between devices  16.5 us (13%)
  between operations  1.51 us (1%)
    unnamed x68, local copies, waits for them, and re-layouts  27.7 us
    all_to_all x1, starting transfers between devices, shards(): table = lax.all_to_all(row, AXES, 0, 0, tiled=True)  23.3 us
    ppermute x6, starting transfers between devices, shift(): return lax.ppermute(value, axis, pairs)  21.9 us
    all_to_all x1, starting transfers between devices, shards(): got = lax.all_to_all(message, AXES, 0, 0, tiled=True)  19.4 us
    all_to_all x1, waiting for transfers between devices, shards(): got = lax.all_to_all(message, AXES, 0, 0, tiled=True)  14 us
    pallas_call x1, Pallas kernels, shards(): pl.pallas_call(functools.partial(window_kernel, cx, cy, nx, ny), out_shap...  6.07 us
    pallas_call x1, Pallas kernels, shards(): pl.pallas_call(functools.partial(assemble_kernel, cx, cy, nx, ny), out_sh...  3.22 us
    pallas_call x1, Pallas kernels, shards(): pl.pallas_call(functools.partial(first_kernel, cx, cy), out_shape=[shape(...  2.8 us
  transfers between devices with their start and end apart: 8, of which 2 were waited for; matrix products, arithmetic and copies ran while one was open for 0% of the time, Pallas kernels for 6%

profile of v4, /device:TPU:1, one launch (start us, length us, event | category | flops | bytes accessed | tf_op | source)
XLA Modules:
  0.0 128.7 jit_solution(10537769904107413726)
XLA Ops:
  1.3 1.0 copy-done
  2.3 1.0 copy-done.2
  3.4 1.0 copy-done.4
  4.4 0.7 copy-done.25
  5.1 0.7 copy-done.31
  5.8 0.7 copy-done.32
  6.4 2.8 %first.1 = (f32[16,2,16,128]{3,2,1,0:T(8,128)}, f32[16,2,16,128]{3,2,1,0:T(8,128)}, f32[15,2,32,128]{3,2,1,0:T(8,128)}, f32[15,2,32,128]{3,2,1,0:T(8,128)}, f32[8,128]{1,0:T(8,128)S(1)}) custom-call(f32[16,32,256]{2,1,0:T(8,128)S(1)} %copy-done, f32[16,32,256]{2,1,0:T(8,128)S(1)} %copy-done.2, f32[16,32,256]{2,1,0:T(8,128)S(1)} %copy-done.4, ...), custom_call_target="tpu_custom_call" | custom-call | tf_op jit(solution)/shard_map/first/pallas_call | solution.py:428
  9.3 5.4 %collective-permute-start.2 = (f32[15,2,32,128]{3,2,1,0:T(8,128)}, f32[15,2,32,128]{3,2,1,0:T(8,128)S(1)}, u32[]{:S(2)}, u32[]{:S(2)}) collective-permute-start(f32[15,2,32,128]{3,2,1,0:T(8,128)} %get-tuple-element.22), channel_id=1, source_target_pairs={{0,16},{16,32},{32,48},{48,64},{64,80},{80,96},{96,112},{112,128},... | collective-permute-start | bytes 1474568 | tf_op jit(solution)/shard_map/ppermute | solution.py:425
  14.7 4.7 %collective-permute-start.3 = (f32[15,2,32,128]{3,2,1,0:T(8,128)}, f32[15,2,32,128]{3,2,1,0:T(8,128)S(1)}, u32[]{:S(2)}, u32[]{:S(2)}) collective-permute-start(f32[15,2,32,128]{3,2,1,0:T(8,128)} %get-tuple-element.23), channel_id=1, source_target_pairs={{16,0},{32,16},{48,32},{64,48},{80,64},{96,80},{112,96},{128,112},... | collective-permute-start | bytes 1474568 | tf_op jit(solution)/shard_map/ppermute | solution.py:425
  19.4 3.0 %collective-permute-start = (f32[16,2,16,128]{3,2,1,0:T(8,128)}, f32[16,2,16,128]{3,2,1,0:T(8,128)S(1)}, u32[]{:S(2)}, u32[]{:S(2)}) collective-permute-start(f32[16,2,16,128]{3,2,1,0:T(8,128)} %get-tuple-element.20), channel_id=1, source_target_pairs={{0,1},{1,2},{2,3},{3,4},{4,5},{5,6},{6,7},{7,8},{8,9},{9,10},{10,1... | collective-permute-start | bytes 786440 | tf_op jit(solution)/shard_map/ppermute | solution.py:425
  22.4 1.3 %collective-permute-start.1 = (f32[16,2,16,128]{3,2,1,0:T(8,128)}, f32[16,2,16,128]{3,2,1,0:T(8,128)S(1)}, u32[]{:S(2)}, u32[]{:S(2)}) collective-permute-start(f32[16,2,16,128]{3,2,1,0:T(8,128)} %get-tuple-element.21), channel_id=1, source_target_pairs={{1,0},{2,1},{3,2},{4,3},{5,4},{6,5},{7,6},{8,7},{9,8},{10,9},{11,1... | collective-permute-start | bytes 786440 | tf_op jit(solution)/shard_map/ppermute | solution.py:425
  23.7 1.5 %row.1 = f32[512,32]{1,0:T(8,128)} custom-call(f32[4,8]{1,0:T(4,128)} %ctl_ref.1, f32[8,128]{1,0:T(8,128)} %copy-done.27), custom_call_target="tpu_custom_call" | custom-call | tf_op jit(solution)/shard_map/row/pallas_call | solution.py:445
  25.2 23.3 %all-to-all-start = ((f32[512,1,32]{2,1,0:T(1,128)}), f32[512,1,32]{2,1,0:T(1,128)S(1)}, u32[]{:S(2)}, u32[]{:S(2)}) async-start(f32[512,1,32]{2,1,0:T(1,128)} %bitcast.12), calls=%async_computation | async-start | bytes 524288 | tf_op jit(solution)/shard_map/all_to_all | solution.py:448
  48.5 0.0 collective-permute-done.yup_ref
  48.5 0.7 copy-done.16
  49.3 0.7 copy-done.18
  50.0 1.7 %corner.1 = (f32[2,2,32,128]{3,2,1,0:T(8,128)}, f32[2,2,32,128]{3,2,1,0:T(8,128)}) custom-call(f32[16,2,16,128]{3,2,1,0:T(8,128)} %copy-done.16, f32[16,2,16,128]{3,2,1,0:T(8,128)} %copy-done.18, f32[8,128]{1,0:T(8,128)} %copy-done.27), custom_call_target="tpu_custom_call" | custom-call | tf_op jit(solution)/shard_map/corner/pallas_call | solution.py:449
  51.7 3.9 %collective-permute-start.4 = (f32[2,2,32,128]{3,2,1,0:T(8,128)}, f32[2,2,32,128]{3,2,1,0:T(8,128)S(1)}, u32[]{:S(2)}, u32[]{:S(2)}) collective-permute-start(f32[2,2,32,128]{3,2,1,0:T(8,128)} %get-tuple-element.25), channel_id=1, source_target_pairs={{0,16},{16,32},{32,48},{48,64},{64,80},{80,96},{96,112},{112,128},... | collective-permute-start | bytes 196616 | tf_op jit(solution)/shard_map/ppermute | solution.py:425
  55.6 3.6 %collective-permute-start.5 = (f32[2,2,32,128]{3,2,1,0:T(8,128)}, f32[2,2,32,128]{3,2,1,0:T(8,128)S(1)}, u32[]{:S(2)}, u32[]{:S(2)}) collective-permute-start(f32[2,2,32,128]{3,2,1,0:T(8,128)} %get-tuple-element.26), channel_id=1, source_target_pairs={{16,0},{32,16},{48,32},{64,48},{80,64},{96,80},{112,96},{128,112},... | collective-permute-start | bytes 196616 | tf_op jit(solution)/shard_map/ppermute | solution.py:425
  59.2 0.0 collective-permute-done.4.cup_ref
  59.2 2.5 %collective-permute-done.5.cdn_ref = f32[2,2,32,128]{3,2,1,0:T(8,128)S(1)} collective-permute-done((f32[2,2,32,128]{3,2,1,0:T(8,128)}, f32[2,2,32,128]{3,2,1,0:T(8,128)S(1)}, u32[]{:S(2)}, u32[]{:S(2)}) %collective-permute-start.5) | collective-permute-done | bytes 65568 | tf_op jit(solution)/shard_map/ppermute | solution.py:425
  61.7 0.0 collective-permute-done.2.xup_ref
  61.7 0.8 copy-done.20
  62.5 0.8 copy-done.22
  63.3 0.9 copy-done.17
  64.2 0.9 copy-done.19
  65.2 1.0 copy-done.21
  66.2 1.0 copy-done.23
  67.3 0.7 copy-done.28
  67.9 3.2 %assemble.1 = (f32[28,2,56,128]{3,2,1,0:T(8,128)S(1)}, f32[28,2,56,128]{3,2,1,0:T(8,128)S(1)}, f32[28,2,56,128]{3,2,1,0:T(8,128)S(1)}, f32[28,2,56,128]{3,2,1,0:...) custom-call(f32[16,32,256]{2,1,0:T(8,128)S(1)} %copy-done.1, f32[16,32,256]{2,1,0:T(8,128)S(1)} %copy-done.3, ...), custom_call_target="tpu_custom_call" | custom-call | flops 20971520 | bytes 12582912 | tf_op jit(solution)/shard_map/assemble/pallas_call | solution.py:459
  71.2 1.2 copy-done.6
  72.4 1.1 copy-done.8
  73.5 1.2 copy-done.10
  74.7 1.2 copy-done.12
  75.8 1.4 %copy-done.7 = f32[28,2,56,128]{3,2,1,0:T(8,128)S(1)} copy-done((f32[28,2,56,128]{3,2,1,0:T(8,128)S(1)}, f32[28,2,56,128]{3,2,1,0:T(8,128)}, u32[]{:S(2)}) %copy-start.7) | copy-done | bytes 1605656
  77.3 1.4 %copy-done.9 = f32[28,2,56,128]{3,2,1,0:T(8,128)S(1)} copy-done((f32[28,2,56,128]{3,2,1,0:T(8,128)S(1)}, f32[28,2,56,128]{3,2,1,0:T(8,128)}, u32[]{:S(2)}) %copy-start.9) | copy-done | bytes 1605656
  78.7 1.4 %copy-done.11 = f32[28,2,56,128]{3,2,1,0:T(8,128)S(1)} copy-done((f32[28,2,56,128]{3,2,1,0:T(8,128)S(1)}, f32[28,2,56,128]{3,2,1,0:T(8,128)}, u32[]{:S(2)}) %copy-start.11) | copy-done | bytes 1605656
  80.1 1.4 %copy-done.13 = f32[28,2,56,128]{3,2,1,0:T(8,128)S(1)} copy-done((f32[28,2,56,128]{3,2,1,0:T(8,128)S(1)}, f32[28,2,56,128]{3,2,1,0:T(8,128)}, u32[]{:S(2)}) %copy-start.13) | copy-done | bytes 1605656
  81.5 6.1 %window.1 = (f32[28,2,56,128]{3,2,1,0:T(8,128)S(1)}, f32[28,2,56,128]{3,2,1,0:T(8,128)S(1)}, f32[512,32]{1,0:T(8,128)S(1)}) custom-call(f32[28,2,56,128]{3,2,1,0:T(8,128)S(1)} %get-tuple-element.27.s0, f32[28,2,56,128]{3,2,1,0:T(8,128)S(1)} %copy-done.7, f32[28,2,56,128]{3,2,1,0:T(8,128)S(1)} %copy-done.9, f32[28,2,56,128]{3,2,1,0:T(8,128)S(1)} %copy-done.11, ...), custom_call_target="tpu_custom_call" | custom-call | tf_op jit(solution)/shard_map/window/pallas_call | solution.py:475
  87.6 1.2 copy-done.14
  88.8 0.7 copy-done.24
  89.5 19.4 %all-to-all-start.1 = ((f32[512,1,32]{2,1,0:T(1,128)}), f32[512,1,32]{2,1,0:T(1,128)S(1)}, u32[]{:S(2)}, u32[]{:S(2)}) async-start(f32[512,1,32]{2,1,0:T(1,128)} %bitcast.10), calls=%async_computation.1 | async-start | bytes 524288 | tf_op jit(solution)/shard_map/all_to_all | solution.py:491
  108.9 1.4 %copy-done.15 = f32[28,2,56,128]{3,2,1,0:T(8,128)S(1)} copy-done((f32[28,2,56,128]{3,2,1,0:T(8,128)S(1)}, f32[28,2,56,128]{3,2,1,0:T(8,128)}, u32[]{:S(2)}) %copy-start.15) | copy-done | bytes 1605656
  110.3 1.4 %final.1 = (f32[16,32,256]{2,1,0:T(8,128)}, f32[4,8]{1,0:T(4,128)S(1)}) custom-call(f32[28,2,56,128]{3,2,1,0:T(8,128)S(1)} %get-tuple-element.33.a1, f32[28,2,56,128]{3,2,1,0:T(8,128)S(1)} %copy-done.15, f32[28,2,56,128]{3,2,1,0:T(8,128)S(1)} %get-tuple-element.27.s0, s32[32,128]{1,0:T(8,128)S(1)} %bitcast.11, s32[4,2048]{1,0:T(4,128)S(1)} %copy-done.29), custom_call_target="tpu_custom_call" | custom-call | flops 5242880 | bytes 4194304 | tf_op jit(solution)/shard_map/final/pallas_call | solution.py:492
  111.8 0.6 copy-done.30
  112.3 14.0 %all-to-all-done.1 = f32[512,1,32]{2,1,0:T(1,128)S(1)} async-done(((f32[512,1,32]{2,1,0:T(1,128)}), f32[512,1,32]{2,1,0:T(1,128)S(1)}, u32[]{:S(2)}, u32[]{:S(2)}) %all-to-all-start.1) | async-done | bytes 65568 | tf_op jit(solution)/shard_map/all_to_all | solution.py:491
  126.3 0.7 copy-done.33
  127.1 1.7 %gradient.1 = f32[4,8]{1,0:T(4,128)} custom-call(f32[512,32]{1,0:T(8,128)} %bitcast.13, f32[4,8]{1,0:T(4,128)} %copy-done.30), custom_call_target="tpu_custom_call" | custom-call | tf_op jit(solution)/shard_map/gradient/pallas_call | solution.py:502
  (43 shorter events, 0.1 us)
Async XLA Ops:
  1.3 1.0 copy-start
  2.3 1.0 copy-start.2
  3.4 1.0 copy-start.4
  4.4 0.7 copy-start.25
  5.1 0.7 copy-start.31
  5.8 0.7 copy-start.32
  6.4 56.9 %copy-start.1 = (f32[16,32,256]{2,1,0:T(8,128)S(1)}, f32[16,32,256]{2,1,0:T(8,128)}, u32[]{:S(2)}) copy-start(f32[16,32,256]{2,1,0:T(8,128)} %ck_ref.3) | copy-start | bytes 1572868
  6.4 56.9 %copy-start.3 = (f32[16,32,256]{2,1,0:T(8,128)S(1)}, f32[16,32,256]{2,1,0:T(8,128)}, u32[]{:S(2)}) copy-start(f32[16,32,256]{2,1,0:T(8,128)} %kp_ref.3) | copy-start | bytes 1572868
  6.4 56.9 %copy-start.5 = (f32[16,32,256]{2,1,0:T(8,128)S(1)}, f32[16,32,256]{2,1,0:T(8,128)}, u32[]{:S(2)}) copy-start(f32[16,32,256]{2,1,0:T(8,128)} %ta_ref.3) | copy-start | bytes 1572868
  9.2 13.2 %copy-start.27 = (f32[8,128]{1,0:T(8,128)}, f32[8,128]{1,0:T(8,128)S(1)}, u32[]{:S(2)}) copy-start(f32[8,128]{1,0:T(8,128)S(1)} %get-tuple-element.24.ids_ref) | copy-start | bytes 12292
  9.3 52.4 %collective-permute-start.2 = (f32[15,2,32,128]{3,2,1,0:T(8,128)}, f32[15,2,32,128]{3,2,1,0:T(8,128)S(1)}, u32[]{:S(2)}, u32[]{:S(2)}) collective-permute-start(f32[15,2,32,128]{3,2,1,0:T(8,128)} %get-tuple-element.22), channel_id=1, source_target_pairs={{0,16},{16,32},{32,48},{48,64},{64,80},{80,96},{96,112},{112,128},... | collective-permute-start | bytes 1474568 | tf_op jit(solution)/shard_map/ppermute | solution.py:425
  14.7 47.8 %collective-permute-start.3 = (f32[15,2,32,128]{3,2,1,0:T(8,128)}, f32[15,2,32,128]{3,2,1,0:T(8,128)S(1)}, u32[]{:S(2)}, u32[]{:S(2)}) collective-permute-start(f32[15,2,32,128]{3,2,1,0:T(8,128)} %get-tuple-element.23), channel_id=1, source_target_pairs={{16,0},{32,16},{48,32},{64,48},{80,64},{96,80},{112,96},{128,112},... | collective-permute-start | bytes 1474568 | tf_op jit(solution)/shard_map/ppermute | solution.py:425
  19.4 29.1 %collective-permute-start = (f32[16,2,16,128]{3,2,1,0:T(8,128)}, f32[16,2,16,128]{3,2,1,0:T(8,128)S(1)}, u32[]{:S(2)}, u32[]{:S(2)}) collective-permute-start(f32[16,2,16,128]{3,2,1,0:T(8,128)} %get-tuple-element.20), channel_id=1, source_target_pairs={{0,1},{1,2},{2,3},{3,4},{4,5},{5,6},{6,7},{7,8},{8,9},{9,10},{10,1... | collective-permute-start | bytes 786440 | tf_op jit(solution)/shard_map/ppermute | solution.py:425
  22.4 26.1 %collective-permute-start.1 = (f32[16,2,16,128]{3,2,1,0:T(8,128)}, f32[16,2,16,128]{3,2,1,0:T(8,128)S(1)}, u32[]{:S(2)}, u32[]{:S(2)}) collective-permute-start(f32[16,2,16,128]{3,2,1,0:T(8,128)} %get-tuple-element.21), channel_id=1, source_target_pairs={{1,0},{2,1},{3,2},{4,3},{5,4},{6,5},{7,6},{8,7},{9,8},{10,9},{11,1... | collective-permute-start | bytes 786440 | tf_op jit(solution)/shard_map/ppermute | solution.py:425
  25.2 50.7 %all-to-all-start = ((f32[512,1,32]{2,1,0:T(1,128)}), f32[512,1,32]{2,1,0:T(1,128)S(1)}, u32[]{:S(2)}, u32[]{:S(2)}) async-start(f32[512,1,32]{2,1,0:T(1,128)} %bitcast.12), calls=%async_computation | async-start | bytes 524288 | tf_op jit(solution)/shard_map/all_to_all | solution.py:448
  48.5 0.7 copy-start.16
  49.2 0.7 copy-start.18
  51.7 7.5 %collective-permute-start.4 = (f32[2,2,32,128]{3,2,1,0:T(8,128)}, f32[2,2,32,128]{3,2,1,0:T(8,128)S(1)}, u32[]{:S(2)}, u32[]{:S(2)}) collective-permute-start(f32[2,2,32,128]{3,2,1,0:T(8,128)} %get-tuple-element.25), channel_id=1, source_target_pairs={{0,16},{16,32},{32,48},{48,64},{64,80},{80,96},{96,112},{112,128},... | collective-permute-start | bytes 196616 | tf_op jit(solution)/shard_map/ppermute | solution.py:425
  55.6 6.1 %collective-permute-start.5 = (f32[2,2,32,128]{3,2,1,0:T(8,128)}, f32[2,2,32,128]{3,2,1,0:T(8,128)S(1)}, u32[]{:S(2)}, u32[]{:S(2)}) collective-permute-start(f32[2,2,32,128]{3,2,1,0:T(8,128)} %get-tuple-element.26), channel_id=1, source_target_pairs={{16,0},{32,16},{48,32},{64,48},{80,64},{96,80},{112,96},{128,112},... | collective-permute-start | bytes 196616 | tf_op jit(solution)/shard_map/ppermute | solution.py:425
  61.7 0.8 copy-start.20
  62.5 0.8 copy-start.22
  63.3 1.0 copy-start.17
  64.2 0.9 copy-start.19
  65.2 1.0 copy-start.21
  66.2 1.0 copy-start.23
  67.3 0.7 copy-start.28
  71.2 1.2 copy-start.6
  72.4 1.1 copy-start.8
  73.5 1.2 copy-start.10
  74.7 1.2 copy-start.12
  75.8 1.4 %copy-start.7 = (f32[28,2,56,128]{3,2,1,0:T(8,128)S(1)}, f32[28,2,56,128]{3,2,1,0:T(8,128)}, u32[]{:S(2)}) copy-start(f32[28,2,56,128]{3,2,1,0:T(8,128)} %copy-done.6) | copy-start | bytes 4816900
  77.3 1.4 %copy-start.9 = (f32[28,2,56,128]{3,2,1,0:T(8,128)S(1)}, f32[28,2,56,128]{3,2,1,0:T(8,128)}, u32[]{:S(2)}) copy-start(f32[28,2,56,128]{3,2,1,0:T(8,128)} %copy-done.8) | copy-start | bytes 4816900
  78.7 1.4 %copy-start.11 = (f32[28,2,56,128]{3,2,1,0:T(8,128)S(1)}, f32[28,2,56,128]{3,2,1,0:T(8,128)}, u32[]{:S(2)}) copy-start(f32[28,2,56,128]{3,2,1,0:T(8,128)} %copy-done.10) | copy-start | bytes 4816900
  80.1 1.4 %copy-start.13 = (f32[28,2,56,128]{3,2,1,0:T(8,128)S(1)}, f32[28,2,56,128]{3,2,1,0:T(8,128)}, u32[]{:S(2)}) copy-start(f32[28,2,56,128]{3,2,1,0:T(8,128)} %copy-done.12) | copy-start | bytes 4816900
  81.5 27.4 %copy-start.26 = (s32[4096]{0:T(1024)S(1)}, s32[4096]{0:T(1024)}, u32[]{:S(2)}) copy-start(s32[4096]{0:T(1024)} %own_ref.1) | copy-start | bytes 49156
  81.5 27.4 %copy-start.29 = (s32[4,2048]{1,0:T(4,128)S(1)}, s32[4,2048]{1,0:T(4,128)}, u32[]{:S(2)}) copy-start(s32[4,2048]{1,0:T(4,128)} %free_ref.1) | copy-start | bytes 98308
  87.6 1.2 copy-start.14
  88.8 0.7 copy-start.24
  89.5 36.8 %all-to-all-start.1 = ((f32[512,1,32]{2,1,0:T(1,128)}), f32[512,1,32]{2,1,0:T(1,128)S(1)}, u32[]{:S(2)}, u32[]{:S(2)}) async-start(f32[512,1,32]{2,1,0:T(1,128)} %bitcast.10), calls=%async_computation.1 | async-start | bytes 524288 | tf_op jit(solution)/shard_map/all_to_all | solution.py:491
  108.9 1.4 %copy-start.15 = (f32[28,2,56,128]{3,2,1,0:T(8,128)S(1)}, f32[28,2,56,128]{3,2,1,0:T(8,128)}, u32[]{:S(2)}) copy-start(f32[28,2,56,128]{3,2,1,0:T(8,128)} %copy-done.14) | copy-start | bytes 4816900
  111.7 0.6 copy-start.30
  126.3 0.7 copy-start.33

commit v5 on v3

--- a/solution.py
+++ b/solution.py
@@ -35,8 +35,27 @@
 CORNER, CORNER_ROWS = corner_pieces()
 
 
-def table_rows(nx):
-    return max(8, nx * GROUP // LANES)
+def lines(nx):
+    return [[4 * y + 2 * low + core for y in range(nx // 4) for core in range(2)] for low in range(2)]
+
+
+def sheets(nx, ny):
+    return [
+        [(4 * y + 2 * low + core) * ny + j for low in range(2) for j in range(ny)]
+        for y in range(nx // 4)
+        for core in range(2)
+    ]
+
+
+def fold(rows):
+    count = rows.shape[0]
+    if count < 8:
+        return jnp.concatenate([rows, jnp.zeros((8 - count, LANES), jnp.float32)], axis=0)
+    lane = lax.broadcasted_iota(jnp.int32, (8, LANES), 1)
+    table = rows[0:8]
+    for g in range(1, count // 8):
+        table = jnp.where(lane < g * GROUP, table, pltpu.roll(rows[8 * g : 8 * g + 8], g * GROUP, 1))
+    return table
 
 
 def first_kernel(
@@ -76,7 +95,7 @@
             at += wide
         return carry
 
-    lax.fori_loop(0, cx, rows, 0, unroll=4)
+    lax.fori_loop(0, cx, rows, 0, unroll=True)
     yup_ref[0, 0, LAYERS : LAYERS + 1, :] = ids
     ydn_ref[0, 0, LAYERS : LAYERS + 1, :] = ids
 
@@ -110,26 +129,15 @@
         ref[LAYERS, 0, cy - 1 : cy, :] = ids_ref[0:1, :]
         ref[LAYERS, 1, cy - 1 : cy, :] = yup_ref[0, 0, LAYERS : LAYERS + 1, :]
         ref[LAYERS + 1, 0, cy - 1 : cy, :] = ydn_ref[0, 0, LAYERS : LAYERS + 1, :]
-    rows = table_rows(nx)
-    if nx < rows:
-        for j in range(ny):
-            tab_ref[j, 0:nx, :] = got_ref[...]
-            tab_ref[j, nx:rows, :] = jnp.zeros((rows - nx, LANES), jnp.float32)
-    else:
-        lane = lax.broadcasted_iota(jnp.int32, (rows, LANES), 1)
-        table = got_ref[0:rows, :]
-        for g in range(1, nx // rows):
-            part = pltpu.roll(got_ref[g * rows : (g + 1) * rows, :], g * GROUP, 1)
-            table = jnp.where(lane < g * GROUP, table, part)
-        tab_ref[...] = jnp.broadcast_to(table[None], tab_ref.shape)
+    tab_ref[...] = jnp.broadcast_to(fold(got_ref[...])[None], tab_ref.shape)
     for copy in copies:
         copy.wait()
 
 
 def window_kernel(
     cx, cy, nx, ny, ck_ref, kp_ref, ta_ref,
-    yup_ref, ydn_ref, xup_ref, xdn_ref, ids_ref, tab_ref,
-    out_ref, msg_ref,
+    yup_ref, ydn_ref, xup_ref, xdn_ref, ids_ref, tab_ref, own_ref, free_ref,
+    out_ref, msg_ref, flag_ref,
     s0, s1, s2, s3, kap, a4, a3, a2, a1, qa, qb,
     near_v, near_s, list_s, pick_v, which_v, amp_v, sum_v, sem, res, out_sems,
 ):
@@ -155,6 +163,21 @@
         near_v[i : i + 1, :] = codes.astype(jnp.int32) - 1
     ids = pltpu.make_async_copy(near_v, near_s, sem)
     ids.start()
+
+    me = gx * ny + gy
+    steps, owned = flag_ref.shape
+    flat = lax.broadcasted_iota(jnp.int32, own_ref.shape, 0) * LANES + lax.broadcasted_iota(
+        jnp.int32, own_ref.shape, 1
+    )
+    free = free_ref[...]
+    column = lax.broadcasted_iota(jnp.int32, (steps, owned), 1)
+    flags = jnp.zeros((steps, owned), jnp.float32)
+    for k in range(owned):
+        mine = jnp.where(own_ref[...] == me * owned + k, flat, 0)
+        actuator = jnp.sum(jnp.sum(mine, axis=0, keepdims=True), axis=1, keepdims=True)
+        hit = jnp.max(jnp.where(free == actuator, 1.0, 0.0), axis=1, keepdims=True)
+        flags = jnp.where(column == k, hit, flags)
+    flag_ref[...] = flags
 
     fields = ((ck_ref, s0), (kp_ref, kap), (ta_ref, a4))
     for f, (own, ext) in enumerate(fields):
@@ -210,8 +233,6 @@
             list_s[part, total + j] = 0
     batches = lax.div(total + BATCH - 1, BATCH)
 
-    rows = table_rows(nx)
-
     def pick(batch, carry):
         for j in range(BATCH):
             pick_one(batch * BATCH + j)
@@ -220,10 +241,13 @@
     def pick_one(e):
         place = list_s[3, e]
         owner = lax.shift_right_logical(place, 3)
-        column, line = lax.rem(owner, ny), lax.div(owner, ny)
-        at = column * rows + lax.rem(line, rows)
+        line, j = lax.div(owner, ny), lax.rem(owner, ny)
+        q = 2 * lax.shift_right_logical(line, 2) + (line & 1)
+        at = 8 * ((lax.shift_right_logical(line, 1) & 1) * ny + j) + (q & 7)
+        list_s[3, e] = at
         pick_v[pl.ds(e, 1), :] = tab_ref[pl.ds(at, 1), :]
-        which_v[pl.ds(e, 1), :] = jnp.broadcast_to(lax.div(line, rows) * GROUP + (place & 7), (1, LANES))
+        column = GROUP * lax.shift_right_logical(q, 3) + (place & 7)
+        which_v[pl.ds(e, 1), :] = jnp.broadcast_to(column, (1, LANES))
 
     lax.fori_loop(0, batches, pick, 0)
     lanes = lax.broadcasted_iota(jnp.int32, pick_v.shape, 1)
@@ -371,11 +395,11 @@
     part = jnp.zeros((16, LANES), jnp.float32)
     for n in range(4):
         sums = DT * jnp.sum(sum_v[n], axis=1, keepdims=True)
-        part = jnp.where(lanes[:16] - 8 * n == (which_v[0:16, :] & 7), sums, part)
+        part = jnp.where(lanes[:16] - 8 * n == which_v[0:16, :], sums, part)
     sum_v[0] = part
 
     def post(e, carry):
-        at = pl.ds(lax.shift_right_logical(list_s[3, e], 3), 1)
+        at = pl.ds(list_s[3, e], 1)
         msg_ref[at, :] += sum_v[0, pl.ds(e, 1), :]
         return carry
 
@@ -384,22 +408,18 @@
         write.wait()
 
 
-def gradient_kernel(ny, got_ref, own_ref, free_ref, out_ref):
-    me = lax.axis_index("gx") * ny + lax.axis_index("gy")
+def sum_kernel(got_ref, out_ref):
+    total = jnp.sum(got_ref[...], axis=0)
+    for at in range(0, out_ref.shape[0], 8):
+        rows = min(8, out_ref.shape[0])
+        out_ref[at : at + rows, :] = pltpu.roll(total, (LANES - GROUP * (at // 8)) % LANES, 1)[0:rows]
+
+
+def gradient_kernel(got_ref, flag_ref, out_ref):
     steps, owned = out_ref.shape
     total = jnp.sum(got_ref[...], axis=0, keepdims=True)
-    flat = lax.broadcasted_iota(jnp.int32, own_ref.shape, 0) * LANES + lax.broadcasted_iota(
-        jnp.int32, own_ref.shape, 1
-    )
-    listed = free_ref[...]
-    column = lax.broadcasted_iota(jnp.int32, (steps, owned), 1)
-    flags = jnp.zeros((steps, owned), jnp.float32)
-    for k in range(owned):
-        actuator = jnp.sum(jnp.where(own_ref[...] == me * owned + k, flat, 0))
-        hit = jnp.max(jnp.where(listed == actuator, 1.0, 0.0), axis=1, keepdims=True)
-        flags = jnp.where(column == k, hit, flags)
     for n in range(steps):
-        out_ref[n : n + 1, :] = total[:, n * owned : (n + 1) * owned] * flags[n : n + 1, :]
+        out_ref[n : n + 1, :] = total[:, n * owned : (n + 1) * owned] * flag_ref[n : n + 1, :]
 
 
 ANY = pl.BlockSpec(memory_space=pl.ANY)
@@ -412,7 +432,6 @@
 ):
     cx, cy, cz = checkpoint.shape
     nx, ny = lax.axis_size("gx"), lax.axis_size("gy")
-    ndev = nx * ny
     f32 = jnp.float32
 
     def shape(*dims):
@@ -426,7 +445,7 @@
     fields = (checkpoint, diffusivity, terminal_adjoint)
     yup, ydn, ids, row = pl.pallas_call(
         functools.partial(first_kernel, cx, cy),
-        out_shape=[shape(cx, 2, 16, LANES)] * 2 + [shape(8, LANES), shape(nx, LANES)],
+        out_shape=[shape(cx, 2, 16, LANES)] * 2 + [shape(8, LANES), shape(nx // 2, LANES)],
         in_specs=[ANY] * 4 + [SM] * 4,
         out_specs=[VM] * 4,
         scratch_shapes=[
@@ -439,11 +458,11 @@
         name="first",
     )(*fields, owner_map, controls, act_ids, slot_tiles, slot_count)
     yup, ydn = shift(yup, "gy", 1), shift(ydn, "gy", -1)
-    got = lax.all_to_all(row, "gx", 0, 0, tiled=True)
-    rows = table_rows(nx)
+    line, sheet = lines(nx), sheets(nx, ny)
+    got = lax.all_to_all(row, "gx", 0, 0, axis_index_groups=line, tiled=True)
     xup, xdn, table = pl.pallas_call(
         functools.partial(second_kernel, cx, cy, nx, ny),
-        out_shape=[shape(LAYERS + 2, 2, cy, LANES)] * 2 + [shape(ny, rows, LANES)],
+        out_shape=[shape(LAYERS + 2, 2, cy, LANES)] * 2 + [shape(2 * ny, 8, LANES)],
         in_specs=[ANY] * 3 + [VM] * 4,
         out_specs=[VM] * 3,
         scratch_shapes=[pltpu.SemaphoreType.DMA((12,))],
@@ -451,14 +470,14 @@
         name="second",
     )(*fields, yup, ydn, ids, got)
     xup, xdn = shift(xup, "gx", 1), shift(xdn, "gx", -1)
-    table = lax.all_to_all(table, "gy", 0, 0, tiled=True).reshape(ny * rows, LANES)
+    table = lax.all_to_all(table, AXES, 0, 0, axis_index_groups=sheet, tiled=True).reshape(16 * ny, LANES)
 
     ext = pltpu.VMEM((cx + 2 * XO, 2, YR, LANES), f32)
-    start_adjoint, message = pl.pallas_call(
+    start_adjoint, message, flags = pl.pallas_call(
         functools.partial(window_kernel, cx, cy, nx, ny),
-        out_shape=[shape(cx, cy, cz), shape(ndev, LANES)],
-        in_specs=[VM] * 9,
-        out_specs=[ANY, VM],
+        out_shape=[shape(cx, cy, cz), shape(16 * ny, LANES), shape(*controls.shape)],
+        in_specs=[VM] * 11,
+        out_specs=[ANY, VM, VM],
         scratch_shapes=[ext] * 11
         + [
             pltpu.VMEM((16, LANES), jnp.int32),
@@ -474,16 +493,17 @@
         ],
         compiler_params=pltpu.CompilerParams(vmem_limit_bytes=48 << 20),
         name="window",
-    )(*fields, yup, ydn, xup, xdn, ids, table)
-
-    got = lax.all_to_all(message, AXES, 0, 0, tiled=True)
+    )(*fields, yup, ydn, xup, xdn, ids, table, owner_map.reshape(-1, LANES), free_list)
+
+    message = message.reshape(2 * ny, 8, LANES)
+    got = lax.all_to_all(message, AXES, 0, 0, axis_index_groups=sheet, tiled=True)
+    part = pl.pallas_call(
+        sum_kernel, out_shape=shape(nx // 2, LANES), in_specs=[VM], out_specs=VM, name="partial_sums"
+    )(got)
+    got = lax.all_to_all(part, "gx", 0, 0, axis_index_groups=line, tiled=True)
     gradient = pl.pallas_call(
-        functools.partial(gradient_kernel, ny),
-        out_shape=shape(*controls.shape),
-        in_specs=[VM] * 3,
-        out_specs=VM,
-        name="gradient",
-    )(got, owner_map.reshape(-1, LANES), free_list)
+        gradient_kernel, out_shape=shape(*controls.shape), in_specs=[VM] * 2, out_specs=VM, name="gradient"
+    )(got, flags)
     return start_adjoint, gradient
 
 

time: 98.5 us -> 101 us (1.025)
  waiting for transfers between devices: 0.01 us -> 2.28 us
  blocking collectives: 69.5 us -> 68.2 us
  Pallas kernels: 14.5 us -> 15.7 us
    ppermute x4, waiting for transfers between devices: 0.01 us -> 2.28 us  [shift(): return lax.ppermute(value, axis, pairs)]
    all_to_all x3 -> x4, blocking collectives: 69.5 us -> 68.2 us  [the longest x1 23 us: shards(): lax.all_to_all(table, AXES, 0, 0, axis_index_groups=sheet, tiled=True)]
    pallas_call x1 -> x2, Pallas kernels: 1.95 us -> 3.01 us  [the longest x1 1.6 us: shards(): pl.pallas_call(sum_kernel, out_shape=shape(nx // 2, LANES), in_specs=[VM]...]
  transfers between devices with their start and end apart: 4 -> 4, of which waited for: 0 -> 1; matrix products, arithmetic and copies ran while one was open for 0% -> 0% of each run, Pallas kernels for 0% -> 0%
where the time goes in v5:
time: 101 us
  blocking collectives  68.2 us (68%)
  Pallas kernels  15.7 us (16%)
  starting transfers between devices  12.6 us (12%)
  waiting for transfers between devices  2.28 us (2%)
  between operations  1.42 us (1%)
    all_to_all x1, blocking collectives, shards(): lax.all_to_all(table, AXES, 0, 0, axis_index_groups=sheet, tiled=True)  23 us
    all_to_all x1, blocking collectives, shards(): got = lax.all_to_all(part, 'gx', 0, 0, axis_index_groups=line, tiled=True)  17 us
    all_to_all x1, blocking collectives, shards(): got = lax.all_to_all(row, 'gx', 0, 0, axis_index_groups=line, tiled=True)  15.1 us
    all_to_all x1, blocking collectives, shards(): lax.all_to_all(message, AXES, 0, 0, axis_index_groups=sheet, tiled=True)  13.1 us
    ppermute x4, starting transfers between devices, shift(): return lax.ppermute(value, axis, pairs)  12.6 us
    pallas_call x1, Pallas kernels, shards(): pl.pallas_call(functools.partial(window_kernel, cx, cy, nx, ny), out_shap...  9.35 us
    pallas_call x1, Pallas kernels, shards(): pl.pallas_call(functools.partial(first_kernel, cx, cy), out_shape=[shape(...  2.97 us
    ppermute x4, waiting for transfers between devices, shift(): return lax.ppermute(value, axis, pairs)  2.28 us
  transfers between devices with their start and end apart: 4, of which 1 were waited for; matrix products, arithmetic and copies ran while one was open for 0% of the time, Pallas kernels for 0%

profile of v5, /device:TPU:1, one launch (start us, length us, event | category | flops | bytes accessed | tf_op | source)
XLA Modules:
  0.0 100.8 jit_solution(12368110137338615645)
XLA Ops:
  1.3 0.0 copy-start
  1.3 0.0 copy-start.1
  1.3 0.0 copy-start.2
  1.3 3.0 %first.1 = (f32[16,2,16,128]{3,2,1,0:T(8,128)}, f32[16,2,16,128]{3,2,1,0:T(8,128)}, f32[8,128]{1,0:T(8,128)}, f32[16,128]{1,0:T(8,128)}) custom-call(f32[16,32,256]{2,1,0:T(8,128)} %ck_ref.5, f32[16,32,256]{2,1,0:T(8,128)} %kp_ref.5, f32[16,32,256]{2,1,0:T(8,128)} %ta_ref.5, s32[4096]{0:T(1024)} %own_ref.1, f32[4,8]{1,0:T(4,128)} %ctl_ref.1, s32[16]{0:T(128)} %act_ref.1, ...), custom_call_target="tpu_custom_call" | custom-call | tf_op jit(solution)/shard_map/first/pallas_call | solution.py:446
  4.3 6.6 %collective-permute-start = (f32[16,2,16,128]{3,2,1,0:T(8,128)}, f32[16,2,16,128]{3,2,1,0:T(8,128)S(1)}, u32[]{:S(2)}, u32[]{:S(2)}) collective-permute-start(f32[16,2,16,128]{3,2,1,0:T(8,128)} %get-tuple-element.12), channel_id=1, source_target_pairs={{0,1},{1,2},{2,3},{3,4},{4,5},{5,6},{6,7},{7,8},{8,9},{9,10},{10,1... | collective-permute-start | bytes 786440 | tf_op jit(solution)/shard_map/ppermute | solution.py:443
  10.9 1.3 %collective-permute-start.1 = (f32[16,2,16,128]{3,2,1,0:T(8,128)}, f32[16,2,16,128]{3,2,1,0:T(8,128)S(1)}, u32[]{:S(2)}, u32[]{:S(2)}) collective-permute-start(f32[16,2,16,128]{3,2,1,0:T(8,128)} %get-tuple-element.13), channel_id=1, source_target_pairs={{1,0},{2,1},{3,2},{4,3},{5,4},{6,5},{7,6},{8,7},{9,8},{10,9},{11,1... | collective-permute-start | bytes 786440 | tf_op jit(solution)/shard_map/ppermute | solution.py:443
  12.2 0.0 copy-start.5
  12.3 15.1 %all_to_all.32 = f32[16,1,128]{2,1,0:T(1,128)S(1)} all-to-all(f32[16,1,128]{2,1,0:T(1,128)} %bitcast.17), channel_id=1, replica_groups={{0,16,64,80,128,144,192,208,256,272,320,336,384,400,448,464},{32,48,96,..., dimensions={0} | all-to-all | bytes 16384 | tf_op jit(solution)/shard_map/all_to_all | solution.py:462
  27.3 0.0 collective-permute-done.yup_ref
  27.3 2.3 %collective-permute-done.1.ydn_ref = f32[16,2,16,128]{3,2,1,0:T(8,128)S(1)} collective-permute-done((f32[16,2,16,128]{3,2,1,0:T(8,128)}, f32[16,2,16,128]{3,2,1,0:T(8,128)S(1)}, u32[]{:S(2)}, u32[]{:S(2)}) %collective-permute-start.1) | collective-permute-done | bytes 262176 | tf_op jit(solution)/shard_map/ppermute | solution.py:443
  29.6 0.0 copy-done
  29.6 0.0 copy-done.1
  29.6 0.0 copy-done.2
  29.6 0.0 copy-done.5
  29.6 0.3 second.1
  30.0 2.3 %collective-permute-start.2 = (f32[17,2,32,128]{3,2,1,0:T(8,128)S(1)}, f32[17,2,32,128]{3,2,1,0:T(8,128)S(1)}, u32[]{:S(2)}, u32[]{:S(2)}) collective-permute-start(f32[17,2,32,128]{3,2,1,0:T(8,128)S(1)} %get-tuple-element.16), channel_id=1, source_target_pairs={{0,16},{16,32},{32,48},{48,64},{64,80},{80,96},{96,112},{112,128},... | collective-permute-start | bytes 1671176 | tf_op jit(solution)/shard_map/ppermute | solution.py:443
  32.3 2.4 %collective-permute-start.3 = (f32[17,2,32,128]{3,2,1,0:T(8,128)S(1)}, f32[17,2,32,128]{3,2,1,0:T(8,128)S(1)}, u32[]{:S(2)}, u32[]{:S(2)}) collective-permute-start(f32[17,2,32,128]{3,2,1,0:T(8,128)S(1)} %get-tuple-element.17), channel_id=1, source_target_pairs={{16,0},{32,16},{48,32},{64,48},{80,64},{96,80},{112,96},{128,112},... | collective-permute-start | bytes 1671176 | tf_op jit(solution)/shard_map/ppermute | solution.py:443
  34.6 0.0 copy-start.3
  34.7 0.0 copy-start.4
  34.7 23.0 %all_to_all.33 = f32[32,8,128]{2,1,0:T(8,128)S(1)} all-to-all(f32[32,8,128]{2,1,0:T(8,128)S(1)} %get-tuple-element.18), channel_id=1, replica_groups={{0,1,2,3,4,5,6,7,8,9,10,11,12,13,14,15,32,33,34,35,36,37,38,39,40,41,42..., dimensions={0} | all-to-all | bytes 262144 | tf_op jit(solution)/shard_map/all_to_all | solution.py:473
  57.7 0.0 collective-permute-done.2.xup_ref
  57.7 0.0 collective-permute-done.3.xdn_ref
  57.7 0.0 copy-done.3
  57.7 0.0 copy-done.4
  57.7 9.3 %window.1 = (f32[16,32,256]{2,1,0:T(8,128)}, f32[256,128]{1,0:T(8,128)S(1)}, f32[4,8]{1,0:T(4,128)S(1)}) custom-call(f32[16,32,256]{2,1,0:T(8,128)S(1)} %copy-done, f32[16,32,256]{2,1,0:T(8,128)S(1)} %copy-done.1, f32[16,32,256]{2,1,0:T(8,128)S(1)} %copy-done.2, f32[16,2,16,128]{3,2,1,0:T(8,128)S(1)} %collective-permute-done.yup_ref, ...), custom_call_target="tpu_custom_call" | custom-call | tf_op jit(solution)/shard_map/window/pallas_call | solution.py:476
  67.0 0.0 copy-start.6
  67.0 0.6 copy-done.6
  67.6 13.1 %all_to_all.34.got_ref = f32[32,8,128]{2,1,0:T(8,128)} all-to-all(f32[32,8,128]{2,1,0:T(8,128)S(1)} %bitcast.12), channel_id=1, replica_groups={{0,1,2,3,4,5,6,7,8,9,10,11,12,13,14,15,32,33,34,35,36,37,38,39,40,41,42..., dimensions={0} | all-to-all | bytes 262144 | tf_op jit(solution)/shard_map/all_to_all | solution.py:499
  80.7 1.6 %partial_sums.1 = f32[16,128]{1,0:T(8,128)} custom-call(f32[32,8,128]{2,1,0:T(8,128)} %all_to_all.34.got_ref), custom_call_target="tpu_custom_call" | custom-call | tf_op jit(solution)/shard_map/partial_sums/pallas_call | solution.py:500
  82.3 17.0 %all_to_all.35 = f32[16,1,128]{2,1,0:T(1,128)} all-to-all(f32[16,1,128]{2,1,0:T(1,128)} %bitcast.15), channel_id=1, replica_groups={{0,16,64,80,128,144,192,208,256,272,320,336,384,400,448,464},{32,48,96,..., dimensions={0} | all-to-all | bytes 16384 | tf_op jit(solution)/shard_map/all_to_all | solution.py:503
  99.4 1.4 %gradient.1 = f32[4,8]{1,0:T(4,128)} custom-call(f32[16,128]{1,0:T(8,128)} %bitcast.16, f32[4,8]{1,0:T(4,128)} %copy-done.6), custom_call_target="tpu_custom_call" | custom-call | tf_op jit(solution)/shard_map/gradient/pallas_call | solution.py:504
Async XLA Ops:
  1.3 28.3 %copy-start = (f32[16,32,256]{2,1,0:T(8,128)S(1)}, f32[16,32,256]{2,1,0:T(8,128)}, u32[]{:S(2)}) copy-start(f32[16,32,256]{2,1,0:T(8,128)} %ck_ref.5) | copy-start | bytes 1572868
  1.3 28.3 %copy-start.1 = (f32[16,32,256]{2,1,0:T(8,128)S(1)}, f32[16,32,256]{2,1,0:T(8,128)}, u32[]{:S(2)}) copy-start(f32[16,32,256]{2,1,0:T(8,128)} %kp_ref.5) | copy-start | bytes 1572868
  1.3 28.3 %copy-start.2 = (f32[16,32,256]{2,1,0:T(8,128)S(1)}, f32[16,32,256]{2,1,0:T(8,128)}, u32[]{:S(2)}) copy-start(f32[16,32,256]{2,1,0:T(8,128)} %ta_ref.5) | copy-start | bytes 1572868
  4.3 23.1 %collective-permute-start = (f32[16,2,16,128]{3,2,1,0:T(8,128)}, f32[16,2,16,128]{3,2,1,0:T(8,128)S(1)}, u32[]{:S(2)}, u32[]{:S(2)}) collective-permute-start(f32[16,2,16,128]{3,2,1,0:T(8,128)} %get-tuple-element.12), channel_id=1, source_target_pairs={{0,1},{1,2},{2,3},{3,4},{4,5},{5,6},{6,7},{7,8},{8,9},{9,10},{10,1... | collective-permute-start | bytes 786440 | tf_op jit(solution)/shard_map/ppermute | solution.py:443
  10.9 18.7 %collective-permute-start.1 = (f32[16,2,16,128]{3,2,1,0:T(8,128)}, f32[16,2,16,128]{3,2,1,0:T(8,128)S(1)}, u32[]{:S(2)}, u32[]{:S(2)}) collective-permute-start(f32[16,2,16,128]{3,2,1,0:T(8,128)} %get-tuple-element.13), channel_id=1, source_target_pairs={{1,0},{2,1},{3,2},{4,3},{5,4},{6,5},{7,6},{8,7},{9,8},{10,9},{11,1... | collective-permute-start | bytes 786440 | tf_op jit(solution)/shard_map/ppermute | solution.py:443
  12.2 17.4 %copy-start.5 = (f32[8,128]{1,0:T(8,128)S(1)}, f32[8,128]{1,0:T(8,128)}, u32[]{:S(2)}) copy-start(f32[8,128]{1,0:T(8,128)} %get-tuple-element.14.ids_ref) | copy-start | bytes 12292
  30.0 27.7 %collective-permute-start.2 = (f32[17,2,32,128]{3,2,1,0:T(8,128)S(1)}, f32[17,2,32,128]{3,2,1,0:T(8,128)S(1)}, u32[]{:S(2)}, u32[]{:S(2)}) collective-permute-start(f32[17,2,32,128]{3,2,1,0:T(8,128)S(1)} %get-tuple-element.16), channel_id=1, source_target_pairs={{0,16},{16,32},{32,48},{48,64},{64,80},{80,96},{96,112},{112,128},... | collective-permute-start | bytes 1671176 | tf_op jit(solution)/shard_map/ppermute | solution.py:443
  32.3 25.4 %collective-permute-start.3 = (f32[17,2,32,128]{3,2,1,0:T(8,128)S(1)}, f32[17,2,32,128]{3,2,1,0:T(8,128)S(1)}, u32[]{:S(2)}, u32[]{:S(2)}) collective-permute-start(f32[17,2,32,128]{3,2,1,0:T(8,128)S(1)} %get-tuple-element.17), channel_id=1, source_target_pairs={{16,0},{32,16},{48,32},{64,48},{80,64},{96,80},{112,96},{128,112},... | collective-permute-start | bytes 1671176 | tf_op jit(solution)/shard_map/ppermute | solution.py:443
  34.6 23.0 %copy-start.3 = (s32[4096]{0:T(1024)S(1)}, s32[4096]{0:T(1024)}, u32[]{:S(2)}) copy-start(s32[4096]{0:T(1024)} %own_ref.1) | copy-start | bytes 49156
  34.7 23.0 %copy-start.4 = (s32[4,2048]{1,0:T(4,128)S(1)}, s32[4,2048]{1,0:T(4,128)}, u32[]{:S(2)}) copy-start(s32[4,2048]{1,0:T(4,128)} %free_ref.1) | copy-start | bytes 98308
  67.0 0.6 copy-start.6

commit v6 on v3

--- a/solution.py
+++ b/solution.py
@@ -19,6 +19,7 @@
 YR = 56
 LANES = 128
 GROUP = 32
+PIECE = 4
 BATCH = 4
 CODE = 1024
 
@@ -41,29 +42,36 @@
 
 def first_kernel(
     cx, cy, ck_ref, kp_ref, ta_ref, own_ref, ctl_ref, act_ref, til_ref, cnt_ref,
-    yup_ref, ydn_ref, ids_ref, row_ref, low, high, own_s, sems,
+    yup_ref, ydn_ref, ids_ref, row_ref, low, high, own_s, ctl_s, act_s, til_s, cnt_s, sems, small_sems,
 ):
-    copies = [pltpu.make_async_copy(own_ref, own_s, sems.at[6])]
+    small = [
+        pltpu.make_async_copy(source, place, small_sems.at[i])
+        for i, (source, place) in enumerate(
+            ((own_ref, own_s), (act_ref, act_s), (til_ref, til_s), (cnt_ref, cnt_s), (ctl_ref, ctl_s))
+        )
+    ]
+    copies = []
     for f, field in enumerate((ck_ref, kp_ref, ta_ref)):
         copies.append(pltpu.make_async_copy(field.at[:, 0:8, :], low.at[f], sems.at[2 * f]))
         copies.append(pltpu.make_async_copy(field.at[:, cy - 8 : cy, :], high.at[f], sems.at[2 * f + 1]))
-    for copy in copies:
+    for copy in small + copies:
         copy.start()
     lane = lax.broadcasted_iota(jnp.int32, (1, LANES), 1)
+    for copy in small:
+        copy.wait()
     row = jnp.zeros((1, LANES), jnp.float32)
-    steps, owned = ctl_ref.shape
+    steps, owned = ctl_s.shape
     for n in range(steps):
         for k in range(owned):
-            row = jnp.where(lane == n * owned + k, ctl_ref[n, k], row)
+            row = jnp.where(lane == n * owned + k, ctl_s[n, k], row)
     row_ref[...] = jnp.broadcast_to(row, row_ref.shape)
-    copies[0].wait()
     ids = jnp.zeros((1, LANES), jnp.int32)
-    for j in range(act_ref.shape[0]):
-        code = jnp.where(j < cnt_ref[0], own_s[act_ref[j]] * CODE + til_ref[j] + 1, 0)
+    for j in range(act_s.shape[0]):
+        code = jnp.where(j < cnt_s[0], own_s[act_s[j]] * CODE + til_s[j] + 1, 0)
         ids = jnp.where(lane == j, code, ids)
     ids = ids.astype(jnp.float32)
     ids_ref[...] = jnp.broadcast_to(ids, ids_ref.shape)
-    for copy in copies[1:]:
+    for copy in copies:
         copy.wait()
     halves = (slice(0, LANES), slice(LANES, 2 * LANES))
 
@@ -76,7 +84,7 @@
             at += wide
         return carry
 
-    lax.fori_loop(0, cx, rows, 0, unroll=4)
+    lax.fori_loop(0, cx, rows, 0, unroll=True)
     yup_ref[0, 0, LAYERS : LAYERS + 1, :] = ids
     ydn_ref[0, 0, LAYERS : LAYERS + 1, :] = ids
 
@@ -128,8 +136,8 @@
 
 def window_kernel(
     cx, cy, nx, ny, ck_ref, kp_ref, ta_ref,
-    yup_ref, ydn_ref, xup_ref, xdn_ref, ids_ref, tab_ref,
-    out_ref, msg_ref,
+    yup_ref, ydn_ref, xup_ref, xdn_ref, ids_ref, tab_ref, own_ref, free_ref,
+    out_ref, msg_ref, flag_ref,
     s0, s1, s2, s3, kap, a4, a3, a2, a1, qa, qb,
     near_v, near_s, list_s, pick_v, which_v, amp_v, sum_v, sem, res, out_sems,
 ):
@@ -156,6 +164,22 @@
     ids = pltpu.make_async_copy(near_v, near_s, sem)
     ids.start()
 
+    me = gx * ny + gy
+    steps, owned = flag_ref.shape
+    flat = lax.broadcasted_iota(jnp.int32, own_ref.shape, 0) * LANES + lax.broadcasted_iota(
+        jnp.int32, own_ref.shape, 1
+    )
+    free = free_ref[...]
+    column = lax.broadcasted_iota(jnp.int32, (steps, owned), 1)
+    flags = jnp.zeros((steps, owned), jnp.float32)
+    for k in range(owned):
+        mine = jnp.where(own_ref[...] == me * owned + k, flat, 0)
+        actuator = jnp.sum(jnp.sum(mine, axis=0, keepdims=True), axis=1, keepdims=True)
+        hit = jnp.max(jnp.where(free == actuator, 1.0, 0.0), axis=1, keepdims=True)
+        flags = jnp.where(column == k, hit, flags)
+    flag_ref[...] = flags
+
+    ids.wait()
     fields = ((ck_ref, s0), (kp_ref, kap), (ta_ref, a4))
     for f, (own, ext) in enumerate(fields):
         wide, at = WIDE[f], sum(WIDE[:f])
@@ -183,7 +207,6 @@
                     ext[x, h, YO - count : YO, :] = take(ref[LAYERS, h, start : start + count, :])
                     ext[x, h, YO + cy : YO + cy + count, :] = take(ref[LAYERS + 1, h, start : start + count, :])
 
-    ids.wait()
     total = jnp.int32(0)
     own_total = jnp.int32(0)
     for i, ((a, b), _) in enumerate(near):
@@ -347,17 +370,18 @@
     backward(a3, qb, s2, a2, qa, 2)
     backward(a2, qa, s1, a1, qb, 1)
 
-    def final(x, carry):
-        def emit(h, t, at, value):
-            res[x, h, pl.ds(t, 8, stride=cy // 8), :] = value
-
-        step(a1, qb, s0, XO + x, YO, cy // 8, emit)
-        return carry
-
-    lax.fori_loop(0, cx, final, 0, unroll=True)
-    writes = [pltpu.make_async_copy(res.at[:, h], out_ref.at[:, :, halves[h]], out_sems.at[h]) for h in range(2)]
-    for write in writes:
-        write.start()
+    writes = []
+    for part in range(0, cx, PIECE):
+        for x in range(part, part + PIECE):
+
+            def emit(h, t, at, value, x=x):
+                res[x, h, pl.ds(t, 8, stride=cy // 8), :] = value
+
+            step(a1, qb, s0, XO + x, YO, cy // 8, emit)
+        for h in range(2):
+            there = out_ref.at[part : part + PIECE, :, halves[h]]
+            writes.append(pltpu.make_async_copy(res.at[part : part + PIECE, h], there, out_sems.at[len(writes)]))
+            writes[-1].start()
 
     msg_ref[...] = jnp.zeros(msg_ref.shape, jnp.float32)
 
@@ -384,22 +408,11 @@
         write.wait()
 
 
-def gradient_kernel(ny, got_ref, own_ref, free_ref, out_ref):
-    me = lax.axis_index("gx") * ny + lax.axis_index("gy")
+def gradient_kernel(got_ref, flag_ref, out_ref):
     steps, owned = out_ref.shape
     total = jnp.sum(got_ref[...], axis=0, keepdims=True)
-    flat = lax.broadcasted_iota(jnp.int32, own_ref.shape, 0) * LANES + lax.broadcasted_iota(
-        jnp.int32, own_ref.shape, 1
-    )
-    listed = free_ref[...]
-    column = lax.broadcasted_iota(jnp.int32, (steps, owned), 1)
-    flags = jnp.zeros((steps, owned), jnp.float32)
-    for k in range(owned):
-        actuator = jnp.sum(jnp.where(own_ref[...] == me * owned + k, flat, 0))
-        hit = jnp.max(jnp.where(listed == actuator, 1.0, 0.0), axis=1, keepdims=True)
-        flags = jnp.where(column == k, hit, flags)
     for n in range(steps):
-        out_ref[n : n + 1, :] = total[:, n * owned : (n + 1) * owned] * flags[n : n + 1, :]
+        out_ref[n : n + 1, :] = total[:, n * owned : (n + 1) * owned] * flag_ref[n : n + 1, :]
 
 
 ANY = pl.BlockSpec(memory_space=pl.ANY)
@@ -427,13 +440,18 @@
     yup, ydn, ids, row = pl.pallas_call(
         functools.partial(first_kernel, cx, cy),
         out_shape=[shape(cx, 2, 16, LANES)] * 2 + [shape(8, LANES), shape(nx, LANES)],
-        in_specs=[ANY] * 4 + [SM] * 4,
+        in_specs=[ANY] * 8,
         out_specs=[VM] * 4,
         scratch_shapes=[
             pltpu.VMEM((3, cx, 8, cz), f32),
             pltpu.VMEM((3, cx, 8, cz), f32),
             pltpu.SMEM(owner_map.shape, jnp.int32),
-            pltpu.SemaphoreType.DMA((7,)),
+            pltpu.SMEM(controls.shape, f32),
+            pltpu.SMEM(act_ids.shape, jnp.int32),
+            pltpu.SMEM(slot_tiles.shape, jnp.int32),
+            pltpu.SMEM(slot_count.shape, jnp.int32),
+            pltpu.SemaphoreType.DMA((6,)),
+            pltpu.SemaphoreType.DMA((5,)),
         ],
         compiler_params=pltpu.CompilerParams(vmem_limit_bytes=60 << 20),
         name="first",
@@ -454,11 +472,11 @@
     table = lax.all_to_all(table, "gy", 0, 0, tiled=True).reshape(ny * rows, LANES)
 
     ext = pltpu.VMEM((cx + 2 * XO, 2, YR, LANES), f32)
-    start_adjoint, message = pl.pallas_call(
+    start_adjoint, message, flags = pl.pallas_call(
         functools.partial(window_kernel, cx, cy, nx, ny),
-        out_shape=[shape(cx, cy, cz), shape(ndev, LANES)],
-        in_specs=[VM] * 9,
-        out_specs=[ANY, VM],
+        out_shape=[shape(cx, cy, cz), shape(ndev, LANES), shape(*controls.shape)],
+        in_specs=[VM] * 11,
+        out_specs=[ANY, VM, VM],
         scratch_shapes=[ext] * 11
         + [
             pltpu.VMEM((16, LANES), jnp.int32),
@@ -470,20 +488,16 @@
             pltpu.VMEM((4, 16, LANES), f32),
             pltpu.SemaphoreType.DMA,
             pltpu.VMEM((cx, 2, cy, LANES), f32),
-            pltpu.SemaphoreType.DMA((2,)),
+            pltpu.SemaphoreType.DMA((2 * cx // PIECE,)),
         ],
         compiler_params=pltpu.CompilerParams(vmem_limit_bytes=48 << 20),
         name="window",
-    )(*fields, yup, ydn, xup, xdn, ids, table)
+    )(*fields, yup, ydn, xup, xdn, ids, table, owner_map.reshape(-1, LANES), free_list)
 
     got = lax.all_to_all(message, AXES, 0, 0, tiled=True)
     gradient = pl.pallas_call(
-        functools.partial(gradient_kernel, ny),
-        out_shape=shape(*controls.shape),
-        in_specs=[VM] * 3,
-        out_specs=VM,
-        name="gradient",
-    )(got, owner_map.reshape(-1, LANES), free_list)
+        gradient_kernel, out_shape=shape(*controls.shape), in_specs=[VM] * 2, out_specs=VM, name="gradient"
+    )(got, flags)
     return start_adjoint, gradient
 
 

time: 98.5 us -> 98 us (level)
  no operation moved by 1% of the time
where the time goes in v6:
time: 98 us; the launch traced here: 97.5 us
  blocking collectives  69.3 us (71%)
  Pallas kernels  14.1 us (14%)
  starting transfers between devices  12.6 us (13%)
  between operations  1.43 us (1%)
    all_to_all x1, blocking collectives, shards(): got = lax.all_to_all(message, AXES, 0, 0, tiled=True)  28.5 us
    all_to_all x1, blocking collectives, shards(): lax.all_to_all(table, 'gy', 0, 0, tiled=True).reshape(ny * rows, LANES)  22.9 us
    all_to_all x1, blocking collectives, shards(): got = lax.all_to_all(row, 'gx', 0, 0, tiled=True)  18 us
    ppermute x4, starting transfers between devices, shift(): return lax.ppermute(value, axis, pairs)  12.6 us
    pallas_call x1, Pallas kernels, shards(): pl.pallas_call(functools.partial(window_kernel, cx, cy, nx, ny), out_shap...  9.89 us
    pallas_call x1, Pallas kernels, shards(): pl.pallas_call(functools.partial(first_kernel, cx, cy), out_shape=[shape(...  2.27 us
  transfers between devices with their start and end apart: 4, of which 0 were waited for; matrix products, arithmetic and copies ran while one was open for 0% of the time, Pallas kernels for 0%

profile of v6, /device:TPU:1, one launch (start us, length us, event | category | flops | bytes accessed | tf_op | source)
XLA Modules:
  0.0 97.5 jit_solution(10110988170906634279)
XLA Ops:
  1.3 0.0 copy-start
  1.3 0.0 copy-start.1
  1.3 0.0 copy-start.2
  1.3 2.3 %first.1 = (f32[16,2,16,128]{3,2,1,0:T(8,128)}, f32[16,2,16,128]{3,2,1,0:T(8,128)}, f32[8,128]{1,0:T(8,128)}, f32[32,128]{1,0:T(8,128)}) custom-call(f32[16,32,256]{2,1,0:T(8,128)} %ck_ref.5, f32[16,32,256]{2,1,0:T(8,128)} %kp_ref.5, f32[16,32,256]{2,1,0:T(8,128)} %ta_ref.5, s32[4096]{0:T(1024)} %own_ref.1, f32[4,8]{1,0:T(4,128)} %ctl_ref.1, s32[16]{0:T(128)} %act_ref.1, ...), custom_call_target="tpu_custom_call" | custom-call | tf_op jit(solution)/shard_map/first/pallas_call | solution.py:440
  3.6 6.6 %collective-permute-start = (f32[16,2,16,128]{3,2,1,0:T(8,128)}, f32[16,2,16,128]{3,2,1,0:T(8,128)S(1)}, u32[]{:S(2)}, u32[]{:S(2)}) collective-permute-start(f32[16,2,16,128]{3,2,1,0:T(8,128)} %get-tuple-element.12), channel_id=1, source_target_pairs={{0,1},{1,2},{2,3},{3,4},{4,5},{5,6},{6,7},{7,8},{8,9},{9,10},{10,1... | collective-permute-start | bytes 786440 | tf_op jit(solution)/shard_map/ppermute | solution.py:437
  10.2 1.3 %collective-permute-start.1 = (f32[16,2,16,128]{3,2,1,0:T(8,128)}, f32[16,2,16,128]{3,2,1,0:T(8,128)S(1)}, u32[]{:S(2)}, u32[]{:S(2)}) collective-permute-start(f32[16,2,16,128]{3,2,1,0:T(8,128)} %get-tuple-element.13), channel_id=1, source_target_pairs={{1,0},{2,1},{3,2},{4,3},{5,4},{6,5},{7,6},{8,7},{9,8},{10,9},{11,1... | collective-permute-start | bytes 786440 | tf_op jit(solution)/shard_map/ppermute | solution.py:437
  11.5 0.0 copy-start.5
  11.6 18.0 %all_to_all.27 = f32[32,1,128]{2,1,0:T(1,128)S(1)} all-to-all(f32[32,1,128]{2,1,0:T(1,128)} %bitcast.15), channel_id=1, replica_groups=mesh['gx'=32,'gy'=16] {'gx'}, dimensions={0} | all-to-all | bytes 32768 | tf_op jit(solution)/shard_map/all_to_all | solution.py:460
  29.5 0.0 collective-permute-done.yup_ref
  29.5 0.0 collective-permute-done.1.ydn_ref
  29.5 0.0 copy-done
  29.5 0.0 copy-done.1
  29.5 0.0 copy-done.2
  29.5 0.0 copy-done.5
  29.6 0.3 second.1
  29.9 2.8 %collective-permute-start.2 = (f32[17,2,32,128]{3,2,1,0:T(8,128)S(1)}, f32[17,2,32,128]{3,2,1,0:T(8,128)S(1)}, u32[]{:S(2)}, u32[]{:S(2)}) collective-permute-start(f32[17,2,32,128]{3,2,1,0:T(8,128)S(1)} %get-tuple-element.16), channel_id=1, source_target_pairs={{0,16},{16,32},{32,48},{48,64},{64,80},{80,96},{96,112},{112,128},... | collective-permute-start | bytes 1671176 | tf_op jit(solution)/shard_map/ppermute | solution.py:437
  32.6 1.9 %collective-permute-start.3 = (f32[17,2,32,128]{3,2,1,0:T(8,128)S(1)}, f32[17,2,32,128]{3,2,1,0:T(8,128)S(1)}, u32[]{:S(2)}, u32[]{:S(2)}) collective-permute-start(f32[17,2,32,128]{3,2,1,0:T(8,128)S(1)} %get-tuple-element.17), channel_id=1, source_target_pairs={{16,0},{32,16},{48,32},{64,48},{80,64},{96,80},{112,96},{128,112},... | collective-permute-start | bytes 1671176 | tf_op jit(solution)/shard_map/ppermute | solution.py:437
  34.5 0.0 copy-start.3
  34.6 0.0 copy-start.4
  34.6 22.9 %all_to_all.28 = f32[16,8,128]{2,1,0:T(8,128)S(1)} all-to-all(f32[16,8,128]{2,1,0:T(8,128)S(1)} %get-tuple-element.18), channel_id=1, replica_groups=mesh['gx'=32,'gy'=16] {'gy'}, dimensions={0} | all-to-all | bytes 131072 | tf_op jit(solution)/shard_map/all_to_all | solution.py:472
  57.5 0.0 collective-permute-done.2.xup_ref
  57.5 0.0 collective-permute-done.3.xdn_ref
  57.5 0.0 copy-done.3
  57.5 0.0 copy-done.4
  57.5 9.9 %window.1 = (f32[16,32,256]{2,1,0:T(8,128)}, f32[512,128]{1,0:T(8,128)S(1)}, f32[4,8]{1,0:T(4,128)S(1)}) custom-call(f32[16,32,256]{2,1,0:T(8,128)S(1)} %copy-done, f32[16,32,256]{2,1,0:T(8,128)S(1)} %copy-done.1, f32[16,32,256]{2,1,0:T(8,128)S(1)} %copy-done.2, f32[16,2,16,128]{3,2,1,0:T(8,128)S(1)} %collective-permute-done.yup_ref, ...), custom_call_target="tpu_custom_call" | custom-call | tf_op jit(solution)/shard_map/window/pallas_call | solution.py:475
  67.4 0.0 copy-start.6
  67.4 28.5 %all_to_all.29 = f32[512,1,128]{2,1,0:T(1,128)} all-to-all(f32[512,1,128]{2,1,0:T(1,128)S(1)} %bitcast.11), channel_id=1, replica_groups=mesh['gx'=32,'gy'=16] {'gx','gy'}, dimensions={0} | all-to-all | bytes 524288 | tf_op jit(solution)/shard_map/all_to_all | solution.py:497
  95.9 0.0 copy-done.6
  95.9 1.7 %gradient.1 = f32[4,8]{1,0:T(4,128)} custom-call(f32[512,128]{1,0:T(8,128)} %bitcast.14, f32[4,8]{1,0:T(4,128)} %copy-done.6), custom_call_target="tpu_custom_call" | custom-call | tf_op jit(solution)/shard_map/gradient/pallas_call | solution.py:498
Async XLA Ops:
  1.3 28.2 %copy-start = (f32[16,32,256]{2,1,0:T(8,128)S(1)}, f32[16,32,256]{2,1,0:T(8,128)}, u32[]{:S(2)}) copy-start(f32[16,32,256]{2,1,0:T(8,128)} %ck_ref.5) | copy-start | bytes 1572868
  1.3 28.2 %copy-start.1 = (f32[16,32,256]{2,1,0:T(8,128)S(1)}, f32[16,32,256]{2,1,0:T(8,128)}, u32[]{:S(2)}) copy-start(f32[16,32,256]{2,1,0:T(8,128)} %kp_ref.5) | copy-start | bytes 1572868
  1.3 28.2 %copy-start.2 = (f32[16,32,256]{2,1,0:T(8,128)S(1)}, f32[16,32,256]{2,1,0:T(8,128)}, u32[]{:S(2)}) copy-start(f32[16,32,256]{2,1,0:T(8,128)} %ta_ref.5) | copy-start | bytes 1572868
  3.6 25.9 %collective-permute-start = (f32[16,2,16,128]{3,2,1,0:T(8,128)}, f32[16,2,16,128]{3,2,1,0:T(8,128)S(1)}, u32[]{:S(2)}, u32[]{:S(2)}) collective-permute-start(f32[16,2,16,128]{3,2,1,0:T(8,128)} %get-tuple-element.12), channel_id=1, source_target_pairs={{0,1},{1,2},{2,3},{3,4},{4,5},{5,6},{6,7},{7,8},{8,9},{9,10},{10,1... | collective-permute-start | bytes 786440 | tf_op jit(solution)/shard_map/ppermute | solution.py:437
  10.2 19.3 %collective-permute-start.1 = (f32[16,2,16,128]{3,2,1,0:T(8,128)}, f32[16,2,16,128]{3,2,1,0:T(8,128)S(1)}, u32[]{:S(2)}, u32[]{:S(2)}) collective-permute-start(f32[16,2,16,128]{3,2,1,0:T(8,128)} %get-tuple-element.13), channel_id=1, source_target_pairs={{1,0},{2,1},{3,2},{4,3},{5,4},{6,5},{7,6},{8,7},{9,8},{10,9},{11,1... | collective-permute-start | bytes 786440 | tf_op jit(solution)/shard_map/ppermute | solution.py:437
  11.5 18.0 %copy-start.5 = (f32[8,128]{1,0:T(8,128)S(1)}, f32[8,128]{1,0:T(8,128)}, u32[]{:S(2)}) copy-start(f32[8,128]{1,0:T(8,128)} %get-tuple-element.14.ids_ref) | copy-start | bytes 12292
  29.9 27.6 %collective-permute-start.2 = (f32[17,2,32,128]{3,2,1,0:T(8,128)S(1)}, f32[17,2,32,128]{3,2,1,0:T(8,128)S(1)}, u32[]{:S(2)}, u32[]{:S(2)}) collective-permute-start(f32[17,2,32,128]{3,2,1,0:T(8,128)S(1)} %get-tuple-element.16), channel_id=1, source_target_pairs={{0,16},{16,32},{32,48},{48,64},{64,80},{80,96},{96,112},{112,128},... | collective-permute-start | bytes 1671176 | tf_op jit(solution)/shard_map/ppermute | solution.py:437
  32.6 24.9 %collective-permute-start.3 = (f32[17,2,32,128]{3,2,1,0:T(8,128)S(1)}, f32[17,2,32,128]{3,2,1,0:T(8,128)S(1)}, u32[]{:S(2)}, u32[]{:S(2)}) collective-permute-start(f32[17,2,32,128]{3,2,1,0:T(8,128)S(1)} %get-tuple-element.17), channel_id=1, source_target_pairs={{16,0},{32,16},{48,32},{64,48},{80,64},{96,80},{112,96},{128,112},... | collective-permute-start | bytes 1671176 | tf_op jit(solution)/shard_map/ppermute | solution.py:437
  34.5 22.9 %copy-start.3 = (s32[4096]{0:T(1024)S(1)}, s32[4096]{0:T(1024)}, u32[]{:S(2)}) copy-start(s32[4096]{0:T(1024)} %own_ref.1) | copy-start | bytes 49156
  34.6 22.9 %copy-start.4 = (s32[4,2048]{1,0:T(4,128)S(1)}, s32[4,2048]{1,0:T(4,128)}, u32[]{:S(2)}) copy-start(s32[4,2048]{1,0:T(4,128)} %free_ref.1) | copy-start | bytes 98308
  67.4 28.5 %copy-start.6 = (f32[4,8]{1,0:T(4,128)}, f32[4,8]{1,0:T(4,128)S(1)}, u32[]{:S(2)}) copy-start(f32[4,8]{1,0:T(4,128)S(1)} %get-tuple-element.21.flag_ref) | copy-start | bytes 388

commit v7 on v6

--- a/solution.py
+++ b/solution.py
@@ -18,6 +18,7 @@
 YO = 12
 YR = 56
 LANES = 128
+FOLD = 8
 GROUP = 32
 PIECE = 4
 BATCH = 4
@@ -159,25 +160,35 @@
         ((1, -1), xdn_ref[LAYERS, 1, tail, :]),
         ((1, 1), xdn_ref[LAYERS + 1, 0, tail, :]),
     )
-    for i, (_, codes) in enumerate(near):
-        near_v[i : i + 1, :] = codes.astype(jnp.int32) - 1
+    for i, ((a, b), codes) in enumerate(near):
+        code = codes.astype(jnp.int32) - 1
+        place, tile = lax.shift_right_arithmetic(code, 10), code & (CODE - 1)
+        x = lax.shift_right_logical(tile, 6) + (XO + a * cx)
+        y = (lax.shift_right_logical(tile, 1) & (cy - 1)) + (YO + b * cy)
+        keep = code >= 0
+        if a != 0:
+            keep &= (x >= XO - 5) & (x < XO + cx + 5)
+        if b != 0:
+            keep &= (y >= YO - 5) & (y < YO + cy + 5)
+        near_v[i : i + 1, :] = jnp.where(keep, place * 4096 + x * 128 + (tile & 1) * 64 + y, -1)
     ids = pltpu.make_async_copy(near_v, near_s, sem)
     ids.start()
 
-    me = gx * ny + gy
-    steps, owned = flag_ref.shape
-    flat = lax.broadcasted_iota(jnp.int32, own_ref.shape, 0) * LANES + lax.broadcasted_iota(
-        jnp.int32, own_ref.shape, 1
-    )
-    free = free_ref[...]
-    column = lax.broadcasted_iota(jnp.int32, (steps, owned), 1)
-    flags = jnp.zeros((steps, owned), jnp.float32)
-    for k in range(owned):
-        mine = jnp.where(own_ref[...] == me * owned + k, flat, 0)
-        actuator = jnp.sum(jnp.sum(mine, axis=0, keepdims=True), axis=1, keepdims=True)
-        hit = jnp.max(jnp.where(free == actuator, 1.0, 0.0), axis=1, keepdims=True)
-        flags = jnp.where(column == k, hit, flags)
-    flag_ref[...] = flags
+    wide_lane = lax.broadcasted_iota(jnp.int32, (8, LANES), 1)
+    sub = lax.broadcasted_iota(jnp.int32, (8, LANES), 0)
+    owner = (gx * ny + gy) * 8 + sub
+    found = jnp.zeros((8, LANES), jnp.int32)
+    for r in range(own_ref.shape[0]):
+        found = found + jnp.where(own_ref[r : r + 1, :] == owner, r * LANES + wide_lane, 0)
+    actuator = jnp.broadcast_to(jnp.sum(found, axis=1, keepdims=True), (8, LANES))
+    flags = jnp.zeros((8, LANES), jnp.float32)
+    for n in range(free_ref.shape[0]):
+        hit = jnp.zeros((8, LANES), jnp.float32)
+        for c in range(free_ref.shape[1] // LANES):
+            hit = jnp.where(free_ref[n : n + 1, c * LANES : (c + 1) * LANES] == actuator, 1.0, hit)
+        hit = jnp.broadcast_to(jnp.max(hit, axis=1, keepdims=True), (8, LANES))
+        flags = jnp.where(wide_lane == 8 * n + sub, hit, flags)
+    flag_ref[...] = jnp.broadcast_to(jnp.sum(flags, axis=0, keepdims=True), (8, LANES))
 
     ids.wait()
     fields = ((ck_ref, s0), (kp_ref, kap), (ta_ref, a4))
@@ -209,29 +220,25 @@
 
     total = jnp.int32(0)
     own_total = jnp.int32(0)
-    for i, ((a, b), _) in enumerate(near):
+    for i in range(len(near)):
         for j in range(16):
-            code = near_s[i, j]
-            place = lax.shift_right_arithmetic(code, 10)
-            tile = code & (CODE - 1)
-            x = lax.shift_right_logical(tile, 6) + (XO + a * cx)
-            y = (lax.shift_right_logical(tile, 1) & (cy - 1)) + (YO + b * cy)
-            keep = place >= 0
-            if a != 0:
-                keep &= (x >= XO - 5) & (x < XO + cx + 5)
-            if b != 0:
-                keep &= (y >= YO - 5) & (y < YO + cy + 5)
-            list_s[0, total] = x
-            list_s[1, total] = tile & 1
-            list_s[2, total] = y
-            list_s[3, total] = place
-            total = total + keep.astype(jnp.int32)
+            entry = near_s[i, j]
+            list_s[total] = entry
+            total = total + (entry >= 0).astype(jnp.int32)
         if i == 0:
             own_total = total
     for j in range(BATCH):
-        for part in range(4):
-            list_s[part, total + j] = 0
+        list_s[total + j] = 0
     batches = lax.div(total + BATCH - 1, BATCH)
+
+    def locate(e):
+        entry = list_s[e]
+        return lax.shift_right_logical(entry, 7) & 31, lax.shift_right_logical(entry, 6) & 1, entry & 63
+
+    def posted(e):
+        place = lax.shift_right_logical(list_s[e], 12)
+        owner = lax.shift_right_logical(place, 3)
+        return lax.rem(owner, ny), lax.div(owner, ny), place & 7
 
     rows = table_rows(nx)
 
@@ -241,12 +248,10 @@
         return carry
 
     def pick_one(e):
-        place = list_s[3, e]
-        owner = lax.shift_right_logical(place, 3)
-        column, line = lax.rem(owner, ny), lax.div(owner, ny)
+        column, line, k = posted(e)
         at = column * rows + lax.rem(line, rows)
         pick_v[pl.ds(e, 1), :] = tab_ref[pl.ds(at, 1), :]
-        which_v[pl.ds(e, 1), :] = jnp.broadcast_to(lax.div(line, rows) * GROUP + (place & 7), (1, LANES))
+        which_v[pl.ds(e, 1), :] = jnp.broadcast_to(lax.div(line, rows) * GROUP + k, (1, LANES))
 
     lax.fori_loop(0, batches, pick, 0)
     lanes = lax.broadcasted_iota(jnp.int32, pick_v.shape, 1)
@@ -309,7 +314,7 @@
         def some(batch, carry):
             for j in range(BATCH):
                 e = batch * BATCH + j
-                x, h, y = list_s[0, e], list_s[1, e], list_s[2, e]
+                x, h, y = locate(e)
                 dst[x, h, pl.ds(y, 1), :] += amp_v[n, pl.ds(e, 1), :]
             return carry
 
@@ -386,21 +391,23 @@
     msg_ref[...] = jnp.zeros(msg_ref.shape, jnp.float32)
 
     def foot(e, carry):
-        x, h, y = list_s[0, e], list_s[1, e], list_s[2, e]
+        x, h, y = locate(e)
         for n, adj in enumerate((a1, a2, a3, a4)):
             sum_v[n, pl.ds(e, 1), :] = adj[x, h, pl.ds(y, 1), :]
+        column, line, k = posted(e)
+        which_v[pl.ds(e, 1), :] = jnp.broadcast_to(lax.div(column, 8) * GROUP + k, (1, LANES))
         return carry
 
     lax.fori_loop(0, own_total, foot, 0)
     part = jnp.zeros((16, LANES), jnp.float32)
     for n in range(4):
         sums = DT * jnp.sum(sum_v[n], axis=1, keepdims=True)
-        part = jnp.where(lanes[:16] - 8 * n == (which_v[0:16, :] & 7), sums, part)
+        part = jnp.where(lanes[:16] - 8 * n == which_v[0:16, :], sums, part)
     sum_v[0] = part
 
     def post(e, carry):
-        at = pl.ds(lax.shift_right_logical(list_s[3, e], 3), 1)
-        msg_ref[at, :] += sum_v[0, pl.ds(e, 1), :]
+        column, line, k = posted(e)
+        msg_ref[pl.ds(line * FOLD + lax.rem(column, 8), 1), :] += sum_v[0, pl.ds(e, 1), :]
         return carry
 
     lax.fori_loop(0, own_total, post, 0)
@@ -408,11 +415,18 @@
         write.wait()
 
 
+def sum_kernel(got_ref, out_ref):
+    total = jnp.sum(got_ref[...], axis=0)
+    for at in range(0, out_ref.shape[0], 8):
+        rows = min(8, out_ref.shape[0])
+        out_ref[at : at + rows, :] = pltpu.roll(total, (LANES - GROUP * (at // 8)) % LANES, 1)[0:rows]
+
+
 def gradient_kernel(got_ref, flag_ref, out_ref):
     steps, owned = out_ref.shape
-    total = jnp.sum(got_ref[...], axis=0, keepdims=True)
+    total = jnp.sum(got_ref[...], axis=0, keepdims=True) * flag_ref[0:1, :]
     for n in range(steps):
-        out_ref[n : n + 1, :] = total[:, n * owned : (n + 1) * owned] * flag_ref[n : n + 1, :]
+        out_ref[n : n + 1, :] = total[:, n * owned : (n + 1) * owned]
 
 
 ANY = pl.BlockSpec(memory_space=pl.ANY)
@@ -425,7 +439,6 @@
 ):
     cx, cy, cz = checkpoint.shape
     nx, ny = lax.axis_size("gx"), lax.axis_size("gy")
-    ndev = nx * ny
     f32 = jnp.float32
 
     def shape(*dims):
@@ -474,14 +487,14 @@
     ext = pltpu.VMEM((cx + 2 * XO, 2, YR, LANES), f32)
     start_adjoint, message, flags = pl.pallas_call(
         functools.partial(window_kernel, cx, cy, nx, ny),
-        out_shape=[shape(cx, cy, cz), shape(ndev, LANES), shape(*controls.shape)],
+        out_shape=[shape(cx, cy, cz), shape(nx * FOLD, LANES), shape(8, LANES)],
         in_specs=[VM] * 11,
         out_specs=[ANY, VM, VM],
         scratch_shapes=[ext] * 11
         + [
             pltpu.VMEM((16, LANES), jnp.int32),
             pltpu.SMEM((16, LANES), jnp.int32),
-            pltpu.SMEM((4, 160), jnp.int32),
+            pltpu.SMEM((160,), jnp.int32),
             pltpu.VMEM((152, LANES), f32),
             pltpu.VMEM((152, LANES), jnp.int32),
             pltpu.VMEM((3, 152, LANES), f32),
@@ -494,7 +507,11 @@
         name="window",
     )(*fields, yup, ydn, xup, xdn, ids, table, owner_map.reshape(-1, LANES), free_list)
 
-    got = lax.all_to_all(message, AXES, 0, 0, tiled=True)
+    got = lax.all_to_all(message.reshape(nx, FOLD, LANES), "gx", 0, 0, tiled=True)
+    part = pl.pallas_call(
+        sum_kernel, out_shape=shape(ny, LANES), in_specs=[VM], out_specs=VM, name="partial_sums"
+    )(got)
+    got = lax.all_to_all(part, "gy", 0, 0, tiled=True)
     gradient = pl.pallas_call(
         gradient_kernel, out_shape=shape(*controls.shape), in_specs=[VM] * 2, out_specs=VM, name="gradient"
     )(got, flags)

time: 98 us -> 99.2 us (1.012)
    pallas_call x0 -> x1, Pallas kernels: none -> 1.6 us  [shards(): pl.pallas_call(sum_kernel, out_shape=shape(ny, LANES), in_specs=[VM], out...]
    pallas_call x1, Pallas kernels: 9.89 us -> 8.86 us  [shards(): pl.pallas_call(functools.partial(window_kernel, cx, cy, nx, ny), out_shap...]
    all_to_all x1 -> x2, blocking collectives: 28.5 us -> 28.7 us  [the longest x1 16.1 us: shards(): lax.all_to_all(message.reshape(nx, FOLD, LANES), 'gx', 0, 0, tiled=True)]
where the time goes in v7:
time: 99.2 us; the launch traced here: 98.6 us
  blocking collectives  69.5 us (70%)
  Pallas kernels  14.4 us (15%)
  starting transfers between devices  12.6 us (13%)
  between operations  1.43 us (1%)
    all_to_all x1, blocking collectives, shards(): lax.all_to_all(table, 'gy', 0, 0, tiled=True).reshape(ny * rows, LANES)  22.9 us
    all_to_all x1, blocking collectives, shards(): got = lax.all_to_all(row, 'gx', 0, 0, tiled=True)  18 us
    all_to_all x1, blocking collectives, shards(): lax.all_to_all(message.reshape(nx, FOLD, LANES), 'gx', 0, 0, tiled=True)  16.1 us
    ppermute x4, starting transfers between devices, shift(): return lax.ppermute(value, axis, pairs)  12.6 us
    all_to_all x1, blocking collectives, shards(): got = lax.all_to_all(part, 'gy', 0, 0, tiled=True)  12.6 us
    pallas_call x1, Pallas kernels, shards(): pl.pallas_call(functools.partial(window_kernel, cx, cy, nx, ny), out_shap...  8.86 us
    pallas_call x1, Pallas kernels, shards(): pl.pallas_call(functools.partial(first_kernel, cx, cy), out_shape=[shape(...  2.27 us
  transfers between devices with their start and end apart: 4, of which 0 were waited for; matrix products, arithmetic and copies ran while one was open for 0% of the time, Pallas kernels for 0%

profile of v7, /device:TPU:1, one launch (start us, length us, event | category | flops | bytes accessed | tf_op | source)
XLA Modules:
  0.0 98.6 jit_solution(10652888645093003978)
XLA Ops:
  1.3 0.0 copy-start
  1.3 0.0 copy-start.1
  1.3 0.0 copy-start.2
  1.3 2.3 %first.1 = (f32[16,2,16,128]{3,2,1,0:T(8,128)}, f32[16,2,16,128]{3,2,1,0:T(8,128)}, f32[8,128]{1,0:T(8,128)}, f32[32,128]{1,0:T(8,128)}) custom-call(f32[16,32,256]{2,1,0:T(8,128)} %ck_ref.5, f32[16,32,256]{2,1,0:T(8,128)} %kp_ref.5, f32[16,32,256]{2,1,0:T(8,128)} %ta_ref.5, s32[4096]{0:T(1024)} %own_ref.1, f32[4,8]{1,0:T(4,128)} %ctl_ref.1, s32[16]{0:T(128)} %act_ref.1, ...), custom_call_target="tpu_custom_call" | custom-call | tf_op jit(solution)/shard_map/first/pallas_call | solution.py:453
  3.6 6.6 %collective-permute-start = (f32[16,2,16,128]{3,2,1,0:T(8,128)}, f32[16,2,16,128]{3,2,1,0:T(8,128)S(1)}, u32[]{:S(2)}, u32[]{:S(2)}) collective-permute-start(f32[16,2,16,128]{3,2,1,0:T(8,128)} %get-tuple-element.12), channel_id=1, source_target_pairs={{0,1},{1,2},{2,3},{3,4},{4,5},{5,6},{6,7},{7,8},{8,9},{9,10},{10,1... | collective-permute-start | bytes 786440 | tf_op jit(solution)/shard_map/ppermute | solution.py:450
  10.2 1.3 %collective-permute-start.1 = (f32[16,2,16,128]{3,2,1,0:T(8,128)}, f32[16,2,16,128]{3,2,1,0:T(8,128)S(1)}, u32[]{:S(2)}, u32[]{:S(2)}) collective-permute-start(f32[16,2,16,128]{3,2,1,0:T(8,128)} %get-tuple-element.13), channel_id=1, source_target_pairs={{1,0},{2,1},{3,2},{4,3},{5,4},{6,5},{7,6},{8,7},{9,8},{10,9},{11,1... | collective-permute-start | bytes 786440 | tf_op jit(solution)/shard_map/ppermute | solution.py:450
  11.5 0.0 copy-start.5
  11.6 18.0 %all_to_all.32 = f32[32,1,128]{2,1,0:T(1,128)S(1)} all-to-all(f32[32,1,128]{2,1,0:T(1,128)} %bitcast.17), channel_id=1, replica_groups=mesh['gx'=32,'gy'=16] {'gx'}, dimensions={0} | all-to-all | bytes 32768 | tf_op jit(solution)/shard_map/all_to_all | solution.py:473
  29.5 0.0 collective-permute-done.yup_ref
  29.5 0.0 collective-permute-done.1.ydn_ref
  29.5 0.0 copy-done
  29.5 0.0 copy-done.1
  29.5 0.0 copy-done.2
  29.5 0.0 copy-done.5
  29.6 0.3 second.1
  29.9 2.8 %collective-permute-start.2 = (f32[17,2,32,128]{3,2,1,0:T(8,128)S(1)}, f32[17,2,32,128]{3,2,1,0:T(8,128)S(1)}, u32[]{:S(2)}, u32[]{:S(2)}) collective-permute-start(f32[17,2,32,128]{3,2,1,0:T(8,128)S(1)} %get-tuple-element.16), channel_id=1, source_target_pairs={{0,16},{16,32},{32,48},{48,64},{64,80},{80,96},{96,112},{112,128},... | collective-permute-start | bytes 1671176 | tf_op jit(solution)/shard_map/ppermute | solution.py:450
  32.6 1.9 %collective-permute-start.3 = (f32[17,2,32,128]{3,2,1,0:T(8,128)S(1)}, f32[17,2,32,128]{3,2,1,0:T(8,128)S(1)}, u32[]{:S(2)}, u32[]{:S(2)}) collective-permute-start(f32[17,2,32,128]{3,2,1,0:T(8,128)S(1)} %get-tuple-element.17), channel_id=1, source_target_pairs={{16,0},{32,16},{48,32},{64,48},{80,64},{96,80},{112,96},{128,112},... | collective-permute-start | bytes 1671176 | tf_op jit(solution)/shard_map/ppermute | solution.py:450
  34.5 0.0 copy-start.3
  34.6 0.0 copy-start.4
  34.6 22.9 %all_to_all.33 = f32[16,8,128]{2,1,0:T(8,128)S(1)} all-to-all(f32[16,8,128]{2,1,0:T(8,128)S(1)} %get-tuple-element.18), channel_id=1, replica_groups=mesh['gx'=32,'gy'=16] {'gy'}, dimensions={0} | all-to-all | bytes 131072 | tf_op jit(solution)/shard_map/all_to_all | solution.py:485
  57.5 0.0 collective-permute-done.2.xup_ref
  57.5 0.0 collective-permute-done.3.xdn_ref
  57.5 0.0 copy-done.3
  57.5 0.0 copy-done.4
  57.5 8.9 %window.1 = (f32[16,32,256]{2,1,0:T(8,128)}, f32[256,128]{1,0:T(8,128)S(1)}, f32[8,128]{1,0:T(8,128)S(1)}) custom-call(f32[16,32,256]{2,1,0:T(8,128)S(1)} %copy-done, f32[16,32,256]{2,1,0:T(8,128)S(1)} %copy-done.1, f32[16,32,256]{2,1,0:T(8,128)S(1)} %copy-done.2, f32[16,2,16,128]{3,2,1,0:T(8,128)S(1)} %collective-permute-done.yup_ref, ...), custom_call_target="tpu_custom_call" | custom-call | tf_op jit(solution)/shard_map/window/pallas_call | solution.py:488
  66.4 0.0 copy-start.6
  66.4 0.6 copy-done.6
  66.9 16.1 %all_to_all.34.got_ref = f32[32,8,128]{2,1,0:T(8,128)} all-to-all(f32[32,8,128]{2,1,0:T(8,128)S(1)} %bitcast.12), channel_id=1, replica_groups=mesh['gx'=32,'gy'=16] {'gx'}, dimensions={0} | all-to-all | bytes 262144 | tf_op jit(solution)/shard_map/all_to_all | solution.py:510
  83.1 1.6 %partial_sums.1 = f32[16,128]{1,0:T(8,128)} custom-call(f32[32,8,128]{2,1,0:T(8,128)} %all_to_all.34.got_ref), custom_call_target="tpu_custom_call" | custom-call | tf_op jit(solution)/shard_map/partial_sums/pallas_call | solution.py:511
  84.7 12.6 %all_to_all.35 = f32[16,1,128]{2,1,0:T(1,128)} all-to-all(f32[16,1,128]{2,1,0:T(1,128)} %bitcast.15), channel_id=1, replica_groups=mesh['gx'=32,'gy'=16] {'gy'}, dimensions={0} | all-to-all | bytes 16384 | tf_op jit(solution)/shard_map/all_to_all | solution.py:514
  97.2 1.4 %gradient.1 = f32[4,8]{1,0:T(4,128)} custom-call(f32[16,128]{1,0:T(8,128)} %bitcast.16, f32[8,128]{1,0:T(8,128)} %copy-done.6), custom_call_target="tpu_custom_call" | custom-call | tf_op jit(solution)/shard_map/gradient/pallas_call | solution.py:515
Async XLA Ops:
  1.3 28.2 %copy-start = (f32[16,32,256]{2,1,0:T(8,128)S(1)}, f32[16,32,256]{2,1,0:T(8,128)}, u32[]{:S(2)}) copy-start(f32[16,32,256]{2,1,0:T(8,128)} %ck_ref.5) | copy-start | bytes 1572868
  1.3 28.2 %copy-start.1 = (f32[16,32,256]{2,1,0:T(8,128)S(1)}, f32[16,32,256]{2,1,0:T(8,128)}, u32[]{:S(2)}) copy-start(f32[16,32,256]{2,1,0:T(8,128)} %kp_ref.5) | copy-start | bytes 1572868
  1.3 28.2 %copy-start.2 = (f32[16,32,256]{2,1,0:T(8,128)S(1)}, f32[16,32,256]{2,1,0:T(8,128)}, u32[]{:S(2)}) copy-start(f32[16,32,256]{2,1,0:T(8,128)} %ta_ref.5) | copy-start | bytes 1572868
  3.6 25.9 %collective-permute-start = (f32[16,2,16,128]{3,2,1,0:T(8,128)}, f32[16,2,16,128]{3,2,1,0:T(8,128)S(1)}, u32[]{:S(2)}, u32[]{:S(2)}) collective-permute-start(f32[16,2,16,128]{3,2,1,0:T(8,128)} %get-tuple-element.12), channel_id=1, source_target_pairs={{0,1},{1,2},{2,3},{3,4},{4,5},{5,6},{6,7},{7,8},{8,9},{9,10},{10,1... | collective-permute-start | bytes 786440 | tf_op jit(solution)/shard_map/ppermute | solution.py:450
  10.2 19.3 %collective-permute-start.1 = (f32[16,2,16,128]{3,2,1,0:T(8,128)}, f32[16,2,16,128]{3,2,1,0:T(8,128)S(1)}, u32[]{:S(2)}, u32[]{:S(2)}) collective-permute-start(f32[16,2,16,128]{3,2,1,0:T(8,128)} %get-tuple-element.13), channel_id=1, source_target_pairs={{1,0},{2,1},{3,2},{4,3},{5,4},{6,5},{7,6},{8,7},{9,8},{10,9},{11,1... | collective-permute-start | bytes 786440 | tf_op jit(solution)/shard_map/ppermute | solution.py:450
  11.5 18.0 %copy-start.5 = (f32[8,128]{1,0:T(8,128)S(1)}, f32[8,128]{1,0:T(8,128)}, u32[]{:S(2)}) copy-start(f32[8,128]{1,0:T(8,128)} %get-tuple-element.14.ids_ref) | copy-start | bytes 12292
  29.9 27.6 %collective-permute-start.2 = (f32[17,2,32,128]{3,2,1,0:T(8,128)S(1)}, f32[17,2,32,128]{3,2,1,0:T(8,128)S(1)}, u32[]{:S(2)}, u32[]{:S(2)}) collective-permute-start(f32[17,2,32,128]{3,2,1,0:T(8,128)S(1)} %get-tuple-element.16), channel_id=1, source_target_pairs={{0,16},{16,32},{32,48},{48,64},{64,80},{80,96},{96,112},{112,128},... | collective-permute-start | bytes 1671176 | tf_op jit(solution)/shard_map/ppermute | solution.py:450
  32.6 24.9 %collective-permute-start.3 = (f32[17,2,32,128]{3,2,1,0:T(8,128)S(1)}, f32[17,2,32,128]{3,2,1,0:T(8,128)S(1)}, u32[]{:S(2)}, u32[]{:S(2)}) collective-permute-start(f32[17,2,32,128]{3,2,1,0:T(8,128)S(1)} %get-tuple-element.17), channel_id=1, source_target_pairs={{16,0},{32,16},{48,32},{64,48},{80,64},{96,80},{112,96},{128,112},... | collective-permute-start | bytes 1671176 | tf_op jit(solution)/shard_map/ppermute | solution.py:450
  34.5 22.9 %copy-start.3 = (s32[4096]{0:T(1024)S(1)}, s32[4096]{0:T(1024)}, u32[]{:S(2)}) copy-start(s32[4096]{0:T(1024)} %own_ref.1) | copy-start | bytes 49156
  34.6 22.9 %copy-start.4 = (s32[4,2048]{1,0:T(4,128)S(1)}, s32[4,2048]{1,0:T(4,128)}, u32[]{:S(2)}) copy-start(s32[4,2048]{1,0:T(4,128)} %free_ref.1) | copy-start | bytes 98308
  66.4 0.6 copy-start.6

commit v8 on v7

--- a/solution.py
+++ b/solution.py
@@ -18,7 +18,6 @@
 YO = 12
 YR = 56
 LANES = 128
-FOLD = 8
 GROUP = 32
 PIECE = 4
 BATCH = 4
@@ -394,8 +393,6 @@
         x, h, y = locate(e)
         for n, adj in enumerate((a1, a2, a3, a4)):
             sum_v[n, pl.ds(e, 1), :] = adj[x, h, pl.ds(y, 1), :]
-        column, line, k = posted(e)
-        which_v[pl.ds(e, 1), :] = jnp.broadcast_to(lax.div(column, 8) * GROUP + k, (1, LANES))
         return carry
 
     lax.fori_loop(0, own_total, foot, 0)
@@ -407,7 +404,7 @@
 
     def post(e, carry):
         column, line, k = posted(e)
-        msg_ref[pl.ds(line * FOLD + lax.rem(column, 8), 1), :] += sum_v[0, pl.ds(e, 1), :]
+        msg_ref[pl.ds(column * rows + lax.rem(line, rows), 1), :] += sum_v[0, pl.ds(e, 1), :]
         return carry
 
     lax.fori_loop(0, own_total, post, 0)
@@ -487,7 +484,7 @@
     ext = pltpu.VMEM((cx + 2 * XO, 2, YR, LANES), f32)
     start_adjoint, message, flags = pl.pallas_call(
         functools.partial(window_kernel, cx, cy, nx, ny),
-        out_shape=[shape(cx, cy, cz), shape(nx * FOLD, LANES), shape(8, LANES)],
+        out_shape=[shape(cx, cy, cz), shape(ny * rows, LANES), shape(8, LANES)],
         in_specs=[VM] * 11,
         out_specs=[ANY, VM, VM],
         scratch_shapes=[ext] * 11
@@ -507,11 +504,11 @@
         name="window",
     )(*fields, yup, ydn, xup, xdn, ids, table, owner_map.reshape(-1, LANES), free_list)
 
-    got = lax.all_to_all(message.reshape(nx, FOLD, LANES), "gx", 0, 0, tiled=True)
+    got = lax.all_to_all(message.reshape(ny, rows, LANES), "gy", 0, 0, tiled=True)
     part = pl.pallas_call(
-        sum_kernel, out_shape=shape(ny, LANES), in_specs=[VM], out_specs=VM, name="partial_sums"
+        sum_kernel, out_shape=shape(nx, LANES), in_specs=[VM], out_specs=VM, name="partial_sums"
     )(got)
-    got = lax.all_to_all(part, "gy", 0, 0, tiled=True)
+    got = lax.all_to_all(part, "gx", 0, 0, tiled=True)
     gradient = pl.pallas_call(
         gradient_kernel, out_shape=shape(*controls.shape), in_specs=[VM] * 2, out_specs=VM, name="gradient"
     )(got, flags)

time: 99.2 us -> 99 us (level)
  no operation moved by 1% of the time
where the time goes in v8:
time: 99 us; the launch traced here: 98.5 us
  blocking collectives  69.5 us (70%)
  Pallas kernels  14.3 us (14%)
  starting transfers between devices  12.6 us (13%)
  between operations  1.43 us (1%)
    all_to_all x1, blocking collectives, shards(): lax.all_to_all(table, 'gy', 0, 0, tiled=True).reshape(ny * rows, LANES)  22.9 us
    all_to_all x1, blocking collectives, shards(): got = lax.all_to_all(row, 'gx', 0, 0, tiled=True)  18 us
    all_to_all x1, blocking collectives, shards(): got = lax.all_to_all(part, 'gx', 0, 0, tiled=True)  16.3 us
    ppermute x4, starting transfers between devices, shift(): return lax.ppermute(value, axis, pairs)  12.6 us
    all_to_all x1, blocking collectives, shards(): lax.all_to_all(message.reshape(ny, rows, LANES), 'gy', 0, 0, tiled=True)  12.3 us
    pallas_call x1, Pallas kernels, shards(): pl.pallas_call(functools.partial(window_kernel, cx, cy, nx, ny), out_shap...  8.86 us
    pallas_call x1, Pallas kernels, shards(): pl.pallas_call(functools.partial(first_kernel, cx, cy), out_shape=[shape(...  2.27 us
  transfers between devices with their start and end apart: 4, of which 0 were waited for; matrix products, arithmetic and copies ran while one was open for 0% of the time, Pallas kernels for 0%

profile of v8, /device:TPU:1, one launch (start us, length us, event | category | flops | bytes accessed | tf_op | source)
XLA Modules:
  0.0 98.5 jit_solution(6554278181950027316)
XLA Ops:
  1.3 0.0 copy-start
  1.3 0.0 copy-start.1
  1.3 0.0 copy-start.2
  1.3 2.3 %first.1 = (f32[16,2,16,128]{3,2,1,0:T(8,128)}, f32[16,2,16,128]{3,2,1,0:T(8,128)}, f32[8,128]{1,0:T(8,128)}, f32[32,128]{1,0:T(8,128)}) custom-call(f32[16,32,256]{2,1,0:T(8,128)} %ck_ref.5, f32[16,32,256]{2,1,0:T(8,128)} %kp_ref.5, f32[16,32,256]{2,1,0:T(8,128)} %ta_ref.5, s32[4096]{0:T(1024)} %own_ref.1, f32[4,8]{1,0:T(4,128)} %ctl_ref.1, s32[16]{0:T(128)} %act_ref.1, ...), custom_call_target="tpu_custom_call" | custom-call | tf_op jit(solution)/shard_map/first/pallas_call | solution.py:450
  3.6 6.6 %collective-permute-start = (f32[16,2,16,128]{3,2,1,0:T(8,128)}, f32[16,2,16,128]{3,2,1,0:T(8,128)S(1)}, u32[]{:S(2)}, u32[]{:S(2)}) collective-permute-start(f32[16,2,16,128]{3,2,1,0:T(8,128)} %get-tuple-element.12), channel_id=1, source_target_pairs={{0,1},{1,2},{2,3},{3,4},{4,5},{5,6},{6,7},{7,8},{8,9},{9,10},{10,1... | collective-permute-start | bytes 786440 | tf_op jit(solution)/shard_map/ppermute | solution.py:447
  10.2 1.3 %collective-permute-start.1 = (f32[16,2,16,128]{3,2,1,0:T(8,128)}, f32[16,2,16,128]{3,2,1,0:T(8,128)S(1)}, u32[]{:S(2)}, u32[]{:S(2)}) collective-permute-start(f32[16,2,16,128]{3,2,1,0:T(8,128)} %get-tuple-element.13), channel_id=1, source_target_pairs={{1,0},{2,1},{3,2},{4,3},{5,4},{6,5},{7,6},{8,7},{9,8},{10,9},{11,1... | collective-permute-start | bytes 786440 | tf_op jit(solution)/shard_map/ppermute | solution.py:447
  11.5 0.0 copy-start.5
  11.6 18.0 %all_to_all.32 = f32[32,1,128]{2,1,0:T(1,128)S(1)} all-to-all(f32[32,1,128]{2,1,0:T(1,128)} %bitcast.17), channel_id=1, replica_groups=mesh['gx'=32,'gy'=16] {'gx'}, dimensions={0} | all-to-all | bytes 32768 | tf_op jit(solution)/shard_map/all_to_all | solution.py:470
  29.5 0.0 collective-permute-done.yup_ref
  29.5 0.0 collective-permute-done.1.ydn_ref
  29.5 0.0 copy-done
  29.5 0.0 copy-done.1
  29.5 0.0 copy-done.2
  29.5 0.0 copy-done.5
  29.6 0.3 second.1
  29.9 2.8 %collective-permute-start.2 = (f32[17,2,32,128]{3,2,1,0:T(8,128)S(1)}, f32[17,2,32,128]{3,2,1,0:T(8,128)S(1)}, u32[]{:S(2)}, u32[]{:S(2)}) collective-permute-start(f32[17,2,32,128]{3,2,1,0:T(8,128)S(1)} %get-tuple-element.16), channel_id=1, source_target_pairs={{0,16},{16,32},{32,48},{48,64},{64,80},{80,96},{96,112},{112,128},... | collective-permute-start | bytes 1671176 | tf_op jit(solution)/shard_map/ppermute | solution.py:447
  32.6 1.9 %collective-permute-start.3 = (f32[17,2,32,128]{3,2,1,0:T(8,128)S(1)}, f32[17,2,32,128]{3,2,1,0:T(8,128)S(1)}, u32[]{:S(2)}, u32[]{:S(2)}) collective-permute-start(f32[17,2,32,128]{3,2,1,0:T(8,128)S(1)} %get-tuple-element.17), channel_id=1, source_target_pairs={{16,0},{32,16},{48,32},{64,48},{80,64},{96,80},{112,96},{128,112},... | collective-permute-start | bytes 1671176 | tf_op jit(solution)/shard_map/ppermute | solution.py:447
  34.5 0.0 copy-start.3
  34.6 0.0 copy-start.4
  34.6 22.9 %all_to_all.33 = f32[16,8,128]{2,1,0:T(8,128)S(1)} all-to-all(f32[16,8,128]{2,1,0:T(8,128)S(1)} %get-tuple-element.18), channel_id=1, replica_groups=mesh['gx'=32,'gy'=16] {'gy'}, dimensions={0} | all-to-all | bytes 131072 | tf_op jit(solution)/shard_map/all_to_all | solution.py:482
  57.5 0.0 collective-permute-done.2.xup_ref
  57.5 0.0 collective-permute-done.3.xdn_ref
  57.5 0.0 copy-done.3
  57.5 0.0 copy-done.4
  57.5 8.9 %window.1 = (f32[16,32,256]{2,1,0:T(8,128)}, f32[128,128]{1,0:T(8,128)S(1)}, f32[8,128]{1,0:T(8,128)S(1)}) custom-call(f32[16,32,256]{2,1,0:T(8,128)S(1)} %copy-done, f32[16,32,256]{2,1,0:T(8,128)S(1)} %copy-done.1, f32[16,32,256]{2,1,0:T(8,128)S(1)} %copy-done.2, f32[16,2,16,128]{3,2,1,0:T(8,128)S(1)} %collective-permute-done.yup_ref, ...), custom_call_target="tpu_custom_call" | custom-call | tf_op jit(solution)/shard_map/window/pallas_call | solution.py:485
  66.4 0.0 copy-start.6
  66.4 0.6 copy-done.6
  66.9 12.3 %all_to_all.34.got_ref = f32[16,8,128]{2,1,0:T(8,128)} all-to-all(f32[16,8,128]{2,1,0:T(8,128)S(1)} %bitcast.14), channel_id=1, replica_groups=mesh['gx'=32,'gy'=16] {'gy'}, dimensions={0} | all-to-all | bytes 131072 | tf_op jit(solution)/shard_map/all_to_all | solution.py:507
  79.3 1.5 %partial_sums.1 = f32[32,128]{1,0:T(8,128)} custom-call(f32[16,8,128]{2,1,0:T(8,128)} %all_to_all.34.got_ref), custom_call_target="tpu_custom_call" | custom-call | tf_op jit(solution)/shard_map/partial_sums/pallas_call | solution.py:508
  80.8 16.3 %all_to_all.35 = f32[32,1,128]{2,1,0:T(1,128)} all-to-all(f32[32,1,128]{2,1,0:T(1,128)} %bitcast.15), channel_id=1, replica_groups=mesh['gx'=32,'gy'=16] {'gx'}, dimensions={0} | all-to-all | bytes 32768 | tf_op jit(solution)/shard_map/all_to_all | solution.py:511
  97.1 1.4 %gradient.1 = f32[4,8]{1,0:T(4,128)} custom-call(f32[32,128]{1,0:T(8,128)} %bitcast.16, f32[8,128]{1,0:T(8,128)} %copy-done.6), custom_call_target="tpu_custom_call" | custom-call | tf_op jit(solution)/shard_map/gradient/pallas_call | solution.py:512
Async XLA Ops:
  1.3 28.2 %copy-start = (f32[16,32,256]{2,1,0:T(8,128)S(1)}, f32[16,32,256]{2,1,0:T(8,128)}, u32[]{:S(2)}) copy-start(f32[16,32,256]{2,1,0:T(8,128)} %ck_ref.5) | copy-start | bytes 1572868
  1.3 28.2 %copy-start.1 = (f32[16,32,256]{2,1,0:T(8,128)S(1)}, f32[16,32,256]{2,1,0:T(8,128)}, u32[]{:S(2)}) copy-start(f32[16,32,256]{2,1,0:T(8,128)} %kp_ref.5) | copy-start | bytes 1572868
  1.3 28.2 %copy-start.2 = (f32[16,32,256]{2,1,0:T(8,128)S(1)}, f32[16,32,256]{2,1,0:T(8,128)}, u32[]{:S(2)}) copy-start(f32[16,32,256]{2,1,0:T(8,128)} %ta_ref.5) | copy-start | bytes 1572868
  3.6 25.9 %collective-permute-start = (f32[16,2,16,128]{3,2,1,0:T(8,128)}, f32[16,2,16,128]{3,2,1,0:T(8,128)S(1)}, u32[]{:S(2)}, u32[]{:S(2)}) collective-permute-start(f32[16,2,16,128]{3,2,1,0:T(8,128)} %get-tuple-element.12), channel_id=1, source_target_pairs={{0,1},{1,2},{2,3},{3,4},{4,5},{5,6},{6,7},{7,8},{8,9},{9,10},{10,1... | collective-permute-start | bytes 786440 | tf_op jit(solution)/shard_map/ppermute | solution.py:447
  10.2 19.3 %collective-permute-start.1 = (f32[16,2,16,128]{3,2,1,0:T(8,128)}, f32[16,2,16,128]{3,2,1,0:T(8,128)S(1)}, u32[]{:S(2)}, u32[]{:S(2)}) collective-permute-start(f32[16,2,16,128]{3,2,1,0:T(8,128)} %get-tuple-element.13), channel_id=1, source_target_pairs={{1,0},{2,1},{3,2},{4,3},{5,4},{6,5},{7,6},{8,7},{9,8},{10,9},{11,1... | collective-permute-start | bytes 786440 | tf_op jit(solution)/shard_map/ppermute | solution.py:447
  11.5 18.0 %copy-start.5 = (f32[8,128]{1,0:T(8,128)S(1)}, f32[8,128]{1,0:T(8,128)}, u32[]{:S(2)}) copy-start(f32[8,128]{1,0:T(8,128)} %get-tuple-element.14.ids_ref) | copy-start | bytes 12292
  29.9 27.6 %collective-permute-start.2 = (f32[17,2,32,128]{3,2,1,0:T(8,128)S(1)}, f32[17,2,32,128]{3,2,1,0:T(8,128)S(1)}, u32[]{:S(2)}, u32[]{:S(2)}) collective-permute-start(f32[17,2,32,128]{3,2,1,0:T(8,128)S(1)} %get-tuple-element.16), channel_id=1, source_target_pairs={{0,16},{16,32},{32,48},{48,64},{64,80},{80,96},{96,112},{112,128},... | collective-permute-start | bytes 1671176 | tf_op jit(solution)/shard_map/ppermute | solution.py:447
  32.6 24.9 %collective-permute-start.3 = (f32[17,2,32,128]{3,2,1,0:T(8,128)S(1)}, f32[17,2,32,128]{3,2,1,0:T(8,128)S(1)}, u32[]{:S(2)}, u32[]{:S(2)}) collective-permute-start(f32[17,2,32,128]{3,2,1,0:T(8,128)S(1)} %get-tuple-element.17), channel_id=1, source_target_pairs={{16,0},{32,16},{48,32},{64,48},{80,64},{96,80},{112,96},{128,112},... | collective-permute-start | bytes 1671176 | tf_op jit(solution)/shard_map/ppermute | solution.py:447
  34.5 22.9 %copy-start.3 = (s32[4096]{0:T(1024)S(1)}, s32[4096]{0:T(1024)}, u32[]{:S(2)}) copy-start(s32[4096]{0:T(1024)} %own_ref.1) | copy-start | bytes 49156
  34.6 22.9 %copy-start.4 = (s32[4,2048]{1,0:T(4,128)S(1)}, s32[4,2048]{1,0:T(4,128)}, u32[]{:S(2)}) copy-start(s32[4,2048]{1,0:T(4,128)} %free_ref.1) | copy-start | bytes 98308
  66.4 0.6 copy-start.6

commit v9 on v8

--- a/solution.py
+++ b/solution.py
@@ -18,6 +18,7 @@
 YO = 12
 YR = 56
 LANES = 128
+FOLD = 2
 GROUP = 32
 PIECE = 4
 BATCH = 4
@@ -36,8 +37,17 @@
 CORNER, CORNER_ROWS = corner_pieces()
 
 
-def table_rows(nx):
-    return max(8, nx * GROUP // LANES)
+def lines(nx):
+    return [[4 * y + c for y in range(nx // 4)] for c in range(4)]
+
+
+def sheets(nx, ny):
+    return [[(4 * y + c) * ny + j for c in range(4) for j in range(ny)] for y in range(nx // 4)]
+
+
+def place_of(line, column, ny):
+    y = lax.shift_right_logical(line, 2)
+    return FOLD * ((line & 3) * ny + column) + (y & (FOLD - 1)), lax.div(y, FOLD) * GROUP
 
 
 def first_kernel(
@@ -118,18 +128,14 @@
         ref[LAYERS, 0, cy - 1 : cy, :] = ids_ref[0:1, :]
         ref[LAYERS, 1, cy - 1 : cy, :] = yup_ref[0, 0, LAYERS : LAYERS + 1, :]
         ref[LAYERS + 1, 0, cy - 1 : cy, :] = ydn_ref[0, 0, LAYERS : LAYERS + 1, :]
-    rows = table_rows(nx)
-    if nx < rows:
-        for j in range(ny):
-            tab_ref[j, 0:nx, :] = got_ref[...]
-            tab_ref[j, nx:rows, :] = jnp.zeros((rows - nx, LANES), jnp.float32)
-    else:
-        lane = lax.broadcasted_iota(jnp.int32, (rows, LANES), 1)
-        table = got_ref[0:rows, :]
-        for g in range(1, nx // rows):
-            part = pltpu.roll(got_ref[g * rows : (g + 1) * rows, :], g * GROUP, 1)
-            table = jnp.where(lane < g * GROUP, table, part)
-        tab_ref[...] = jnp.broadcast_to(table[None], tab_ref.shape)
+    lane = lax.broadcasted_iota(jnp.int32, (FOLD, LANES), 1)
+    table = got_ref[0:FOLD, :]
+    for g in range(1, nx // 4 // FOLD):
+        part = pltpu.roll(got_ref[g * FOLD : (g + 1) * FOLD, :], g * GROUP, 1)
+        table = jnp.where(lane < g * GROUP, table, part)
+    table = jnp.concatenate([table] * (8 // FOLD), axis=0)
+    for at in range(0, tab_ref.shape[0], 8):
+        tab_ref[at : at + 8, :] = table
     for copy in copies:
         copy.wait()
 
@@ -237,9 +243,8 @@
     def posted(e):
         place = lax.shift_right_logical(list_s[e], 12)
         owner = lax.shift_right_logical(place, 3)
-        return lax.rem(owner, ny), lax.div(owner, ny), place & 7
-
-    rows = table_rows(nx)
+        at, first = place_of(lax.div(owner, ny), lax.rem(owner, ny), ny)
+        return at, first, place & 7
 
     def pick(batch, carry):
         for j in range(BATCH):
@@ -247,10 +252,9 @@
         return carry
 
     def pick_one(e):
-        column, line, k = posted(e)
-        at = column * rows + lax.rem(line, rows)
+        at, first, k = posted(e)
         pick_v[pl.ds(e, 1), :] = tab_ref[pl.ds(at, 1), :]
-        which_v[pl.ds(e, 1), :] = jnp.broadcast_to(lax.div(line, rows) * GROUP + k, (1, LANES))
+        which_v[pl.ds(e, 1), :] = jnp.broadcast_to(first + k, (1, LANES))
 
     lax.fori_loop(0, batches, pick, 0)
     lanes = lax.broadcasted_iota(jnp.int32, pick_v.shape, 1)
@@ -403,8 +407,8 @@
     sum_v[0] = part
 
     def post(e, carry):
-        column, line, k = posted(e)
-        msg_ref[pl.ds(column * rows + lax.rem(line, rows), 1), :] += sum_v[0, pl.ds(e, 1), :]
+        at, first, k = posted(e)
+        msg_ref[pl.ds(at, 1), :] += sum_v[0, pl.ds(e, 1), :]
         return carry
 
     lax.fori_loop(0, own_total, post, 0)
@@ -413,10 +417,12 @@
 
 
 def sum_kernel(got_ref, out_ref):
-    total = jnp.sum(got_ref[...], axis=0)
-    for at in range(0, out_ref.shape[0], 8):
-        rows = min(8, out_ref.shape[0])
-        out_ref[at : at + rows, :] = pltpu.roll(total, (LANES - GROUP * (at // 8)) % LANES, 1)[0:rows]
+    total = got_ref[0:8, :]
+    for at in range(8, got_ref.shape[0], 8):
+        total = total + got_ref[at : at + 8, :]
+    total = sum(total[at : at + FOLD] for at in range(0, 8, FOLD))
+    for at in range(0, out_ref.shape[0], FOLD):
+        out_ref[at : at + FOLD, :] = pltpu.roll(total, (LANES - GROUP * (at // FOLD)) % LANES, 1)
 
 
 def gradient_kernel(got_ref, flag_ref, out_ref):
@@ -449,7 +455,7 @@
     fields = (checkpoint, diffusivity, terminal_adjoint)
     yup, ydn, ids, row = pl.pallas_call(
         functools.partial(first_kernel, cx, cy),
-        out_shape=[shape(cx, 2, 16, LANES)] * 2 + [shape(8, LANES), shape(nx, LANES)],
+        out_shape=[shape(cx, 2, 16, LANES)] * 2 + [shape(8, LANES), shape(nx // 4, LANES)],
         in_specs=[ANY] * 8,
         out_specs=[VM] * 4,
         scratch_shapes=[
@@ -467,11 +473,12 @@
         name="first",
     )(*fields, owner_map, controls, act_ids, slot_tiles, slot_count)
     yup, ydn = shift(yup, "gy", 1), shift(ydn, "gy", -1)
-    got = lax.all_to_all(row, "gx", 0, 0, tiled=True)
-    rows = table_rows(nx)
+    line, sheet = lines(nx), sheets(nx, ny)
+    rows = 4 * ny * FOLD
+    got = lax.all_to_all(row, "gx", 0, 0, axis_index_groups=line, tiled=True)
     xup, xdn, table = pl.pallas_call(
         functools.partial(second_kernel, cx, cy, nx, ny),
-        out_shape=[shape(LAYERS + 2, 2, cy, LANES)] * 2 + [shape(ny, rows, LANES)],
+        out_shape=[shape(LAYERS + 2, 2, cy, LANES)] * 2 + [shape(rows, LANES)],
         in_specs=[ANY] * 3 + [VM] * 4,
         out_specs=[VM] * 3,
         scratch_shapes=[pltpu.SemaphoreType.DMA((12,))],
@@ -479,12 +486,12 @@
         name="second",
     )(*fields, yup, ydn, ids, got)
     xup, xdn = shift(xup, "gx", 1), shift(xdn, "gx", -1)
-    table = lax.all_to_all(table, "gy", 0, 0, tiled=True).reshape(ny * rows, LANES)
+    table = lax.all_to_all(table, AXES, 0, 0, axis_index_groups=sheet, tiled=True)
 
     ext = pltpu.VMEM((cx + 2 * XO, 2, YR, LANES), f32)
     start_adjoint, message, flags = pl.pallas_call(
         functools.partial(window_kernel, cx, cy, nx, ny),
-        out_shape=[shape(cx, cy, cz), shape(ny * rows, LANES), shape(8, LANES)],
+        out_shape=[shape(cx, cy, cz), shape(rows, LANES), shape(8, LANES)],
         in_specs=[VM] * 11,
         out_specs=[ANY, VM, VM],
         scratch_shapes=[ext] * 11
@@ -504,11 +511,11 @@
         name="window",
     )(*fields, yup, ydn, xup, xdn, ids, table, owner_map.reshape(-1, LANES), free_list)
 
-    got = lax.all_to_all(message.reshape(ny, rows, LANES), "gy", 0, 0, tiled=True)
+    got = lax.all_to_all(message, AXES, 0, 0, axis_index_groups=sheet, tiled=True)
     part = pl.pallas_call(
-        sum_kernel, out_shape=shape(nx, LANES), in_specs=[VM], out_specs=VM, name="partial_sums"
+        sum_kernel, out_shape=shape(nx // 4, LANES), in_specs=[VM], out_specs=VM, name="partial_sums"
     )(got)
-    got = lax.all_to_all(part, "gx", 0, 0, tiled=True)
+    got = lax.all_to_all(part, "gx", 0, 0, axis_index_groups=line, tiled=True)
     gradient = pl.pallas_call(
         gradient_kernel, out_shape=shape(*controls.shape), in_specs=[VM] * 2, out_specs=VM, name="gradient"
     )(got, flags)

time: 99 us -> 96.9 us (0.979)
  blocking collectives: 69.5 us -> 63.7 us
  waiting for transfers between devices: 0.01 us -> 4.2 us
    all_to_all x4, blocking collectives: 69.5 us -> 63.7 us  [the longest x1 22.7 us: shards(): lax.all_to_all(table, AXES, 0, 0, axis_index_groups=sheet, tiled=True)]
    ppermute x4, waiting for transfers between devices: 0.01 us -> 4.2 us  [shift(): return lax.ppermute(value, axis, pairs)]
  transfers between devices with their start and end apart: 4 -> 4, of which waited for: 0 -> 1; matrix products, arithmetic and copies ran while one was open for 0% -> 0% of each run, Pallas kernels for 0% -> 0%
where the time goes in v9:
time: 96.9 us; the launch traced here: 96.2 us
  blocking collectives  63.7 us (66%)
  Pallas kernels  14.2 us (15%)
  starting transfers between devices  12.6 us (13%)
  waiting for transfers between devices  4.2 us (4%)
  between operations  1.43 us (1%)
    all_to_all x1, blocking collectives, shards(): lax.all_to_all(table, AXES, 0, 0, axis_index_groups=sheet, tiled=True)  22.7 us
    all_to_all x1, blocking collectives, shards(): lax.all_to_all(message, AXES, 0, 0, axis_index_groups=sheet, tiled=True)  14.2 us
    all_to_all x1, blocking collectives, shards(): got = lax.all_to_all(part, 'gx', 0, 0, axis_index_groups=line, tiled=True)  13.7 us
    all_to_all x1, blocking collectives, shards(): got = lax.all_to_all(row, 'gx', 0, 0, axis_index_groups=line, tiled=True)  13.1 us
    ppermute x4, starting transfers between devices, shift(): return lax.ppermute(value, axis, pairs)  12.6 us
    pallas_call x1, Pallas kernels, shards(): pl.pallas_call(functools.partial(window_kernel, cx, cy, nx, ny), out_shap...  8.76 us
    ppermute x4, waiting for transfers between devices, shift(): return lax.ppermute(value, axis, pairs)  4.2 us
    pallas_call x1, Pallas kernels, shards(): pl.pallas_call(functools.partial(first_kernel, cx, cy), out_shape=[shape(...  2.27 us
  transfers between devices with their start and end apart: 4, of which 1 were waited for; matrix products, arithmetic and copies ran while one was open for 0% of the time, Pallas kernels for 0%

profile of v9, /device:TPU:1, one launch (start us, length us, event | category | flops | bytes accessed | tf_op | source)
XLA Modules:
  0.0 96.2 jit_solution(8364497971605464602)
XLA Ops:
  1.3 0.0 copy-start
  1.3 0.0 copy-start.1
  1.3 0.0 copy-start.2
  1.3 2.3 %first.1 = (f32[16,2,16,128]{3,2,1,0:T(8,128)}, f32[16,2,16,128]{3,2,1,0:T(8,128)}, f32[8,128]{1,0:T(8,128)}, f32[8,128]{1,0:T(8,128)}) custom-call(f32[16,32,256]{2,1,0:T(8,128)} %ck_ref.5, f32[16,32,256]{2,1,0:T(8,128)} %kp_ref.5, f32[16,32,256]{2,1,0:T(8,128)} %ta_ref.5, s32[4096]{0:T(1024)} %own_ref.1, f32[4,8]{1,0:T(4,128)} %ctl_ref.1, s32[16]{0:T(128)} %act_ref.1, ...), custom_call_target="tpu_custom_call" | custom-call | tf_op jit(solution)/shard_map/first/pallas_call | solution.py:456
  3.6 0.0 copy-start.7
  3.6 6.6 %collective-permute-start = (f32[16,2,16,128]{3,2,1,0:T(8,128)}, f32[16,2,16,128]{3,2,1,0:T(8,128)S(1)}, u32[]{:S(2)}, u32[]{:S(2)}) collective-permute-start(f32[16,2,16,128]{3,2,1,0:T(8,128)} %get-tuple-element.12), channel_id=1, source_target_pairs={{0,1},{1,2},{2,3},{3,4},{4,5},{5,6},{6,7},{7,8},{8,9},{9,10},{10,1... | collective-permute-start | bytes 786440 | tf_op jit(solution)/shard_map/ppermute | solution.py:453
  10.3 1.3 %collective-permute-start.1 = (f32[16,2,16,128]{3,2,1,0:T(8,128)}, f32[16,2,16,128]{3,2,1,0:T(8,128)S(1)}, u32[]{:S(2)}, u32[]{:S(2)}) collective-permute-start(f32[16,2,16,128]{3,2,1,0:T(8,128)} %get-tuple-element.13), channel_id=1, source_target_pairs={{1,0},{2,1},{3,2},{4,3},{5,4},{6,5},{7,6},{8,7},{9,8},{10,9},{11,1... | collective-permute-start | bytes 786440 | tf_op jit(solution)/shard_map/ppermute | solution.py:453
  11.6 0.0 copy-done.7
  11.6 0.0 copy-start.5
  11.6 13.1 %all_to_all.44 = f32[8,1,128]{2,1,0:T(1,128)S(1)} all-to-all(f32[8,1,128]{2,1,0:T(1,128)S(1)} %bitcast.21), channel_id=1, replica_groups={{0,64,128,192,256,320,384,448},{16,80,144,208,272,336,400,464},{32,96,1..., dimensions={0} | all-to-all | bytes 8192 | tf_op jit(solution)/shard_map/all_to_all | solution.py:478
  24.7 0.0 collective-permute-done.yup_ref
  24.7 4.2 %collective-permute-done.1.ydn_ref = f32[16,2,16,128]{3,2,1,0:T(8,128)S(1)} collective-permute-done((f32[16,2,16,128]{3,2,1,0:T(8,128)}, f32[16,2,16,128]{3,2,1,0:T(8,128)S(1)}, u32[]{:S(2)}, u32[]{:S(2)}) %collective-permute-start.1) | collective-permute-done | bytes 262176 | tf_op jit(solution)/shard_map/ppermute | solution.py:453
  28.9 0.0 copy-done
  28.9 0.0 copy-done.1
  28.9 0.0 copy-done.2
  28.9 0.0 copy-done.5
  28.9 0.3 second.1
  29.2 2.1 %collective-permute-start.2 = (f32[17,2,32,128]{3,2,1,0:T(8,128)S(1)}, f32[17,2,32,128]{3,2,1,0:T(8,128)S(1)}, u32[]{:S(2)}, u32[]{:S(2)}) collective-permute-start(f32[17,2,32,128]{3,2,1,0:T(8,128)S(1)} %get-tuple-element.16), channel_id=1, source_target_pairs={{0,16},{16,32},{32,48},{48,64},{64,80},{80,96},{96,112},{112,128},... | collective-permute-start | bytes 1671176 | tf_op jit(solution)/shard_map/ppermute | solution.py:453
  31.3 2.6 %collective-permute-start.3 = (f32[17,2,32,128]{3,2,1,0:T(8,128)S(1)}, f32[17,2,32,128]{3,2,1,0:T(8,128)S(1)}, u32[]{:S(2)}, u32[]{:S(2)}) collective-permute-start(f32[17,2,32,128]{3,2,1,0:T(8,128)S(1)} %get-tuple-element.17), channel_id=1, source_target_pairs={{16,0},{32,16},{48,32},{64,48},{80,64},{96,80},{112,96},{128,112},... | collective-permute-start | bytes 1671176 | tf_op jit(solution)/shard_map/ppermute | solution.py:453
  33.9 0.0 copy-start.3
  33.9 0.0 copy-start.4
  33.9 22.7 %all_to_all.45 = f32[64,2,128]{2,1,0:T(2,128)S(1)} all-to-all(f32[64,2,128]{2,1,0:T(2,128)S(1)} %bitcast.15), channel_id=1, replica_groups={{0,1,2,3,4,5,6,7,8,9,10,11,12,13,14,15,16,17,18,19,20,21,22,23,24,25,26..., dimensions={0} | all-to-all | bytes 131072 | tf_op jit(solution)/shard_map/all_to_all | solution.py:489
  56.6 0.0 collective-permute-done.2.xup_ref
  56.6 0.0 collective-permute-done.3.xdn_ref
  56.6 0.0 copy-done.3
  56.6 0.0 copy-done.4
  56.6 8.8 %window.1 = (f32[16,32,256]{2,1,0:T(8,128)}, f32[128,128]{1,0:T(8,128)S(1)}, f32[8,128]{1,0:T(8,128)S(1)}) custom-call(f32[16,32,256]{2,1,0:T(8,128)S(1)} %copy-done, f32[16,32,256]{2,1,0:T(8,128)S(1)} %copy-done.1, f32[16,32,256]{2,1,0:T(8,128)S(1)} %copy-done.2, f32[16,2,16,128]{3,2,1,0:T(8,128)S(1)} %collective-permute-done.yup_ref, ...), custom_call_target="tpu_custom_call" | custom-call | tf_op jit(solution)/shard_map/window/pallas_call | solution.py:492
  65.4 0.0 copy-start.6
  65.4 14.2 %all_to_all.46 = f32[64,2,128]{2,1,0:T(2,128)} all-to-all(f32[64,2,128]{2,1,0:T(2,128)S(1)} %bitcast.16), channel_id=1, replica_groups={{0,1,2,3,4,5,6,7,8,9,10,11,12,13,14,15,16,17,18,19,20,21,22,23,24,25,26..., dimensions={0} | all-to-all | bytes 131072 | tf_op jit(solution)/shard_map/all_to_all | solution.py:514
  79.6 0.0 copy-done.6
  79.6 1.5 %partial_sums.1 = f32[8,128]{1,0:T(8,128)} custom-call(f32[128,128]{1,0:T(8,128)} %bitcast.18), custom_call_target="tpu_custom_call" | custom-call | tf_op jit(solution)/shard_map/partial_sums/pallas_call | solution.py:515
  81.2 13.7 %all_to_all.47 = f32[8,1,128]{2,1,0:T(1,128)} all-to-all(f32[8,1,128]{2,1,0:T(1,128)} %bitcast.19), channel_id=1, replica_groups={{0,64,128,192,256,320,384,448},{16,80,144,208,272,336,400,464},{32,96,1..., dimensions={0} | all-to-all | bytes 8192 | tf_op jit(solution)/shard_map/all_to_all | solution.py:518
  94.8 1.3 %gradient.1 = f32[4,8]{1,0:T(4,128)} custom-call(f32[8,128]{1,0:T(8,128)} %bitcast.20, f32[8,128]{1,0:T(8,128)} %copy-done.6), custom_call_target="tpu_custom_call" | custom-call | tf_op jit(solution)/shard_map/gradient/pallas_call | solution.py:519
Async XLA Ops:
  1.3 27.7 %copy-start = (f32[16,32,256]{2,1,0:T(8,128)S(1)}, f32[16,32,256]{2,1,0:T(8,128)}, u32[]{:S(2)}) copy-start(f32[16,32,256]{2,1,0:T(8,128)} %ck_ref.5) | copy-start | bytes 1572868
  1.3 27.6 %copy-start.1 = (f32[16,32,256]{2,1,0:T(8,128)S(1)}, f32[16,32,256]{2,1,0:T(8,128)}, u32[]{:S(2)}) copy-start(f32[16,32,256]{2,1,0:T(8,128)} %kp_ref.5) | copy-start | bytes 1572868
  1.3 27.6 %copy-start.2 = (f32[16,32,256]{2,1,0:T(8,128)S(1)}, f32[16,32,256]{2,1,0:T(8,128)}, u32[]{:S(2)}) copy-start(f32[16,32,256]{2,1,0:T(8,128)} %ta_ref.5) | copy-start | bytes 1572868
  3.6 8.0 %copy-start.7 = (f32[8,128]{1,0:T(8,128)S(1)}, f32[8,128]{1,0:T(8,128)}, u32[]{:S(2)}) copy-start(f32[8,128]{1,0:T(8,128)} %get-tuple-element.15) | copy-start | bytes 12292
  3.6 21.1 %collective-permute-start = (f32[16,2,16,128]{3,2,1,0:T(8,128)}, f32[16,2,16,128]{3,2,1,0:T(8,128)S(1)}, u32[]{:S(2)}, u32[]{:S(2)}) collective-permute-start(f32[16,2,16,128]{3,2,1,0:T(8,128)} %get-tuple-element.12), channel_id=1, source_target_pairs={{0,1},{1,2},{2,3},{3,4},{4,5},{5,6},{6,7},{7,8},{8,9},{9,10},{10,1... | collective-permute-start | bytes 786440 | tf_op jit(solution)/shard_map/ppermute | solution.py:453
  10.3 18.7 %collective-permute-start.1 = (f32[16,2,16,128]{3,2,1,0:T(8,128)}, f32[16,2,16,128]{3,2,1,0:T(8,128)S(1)}, u32[]{:S(2)}, u32[]{:S(2)}) collective-permute-start(f32[16,2,16,128]{3,2,1,0:T(8,128)} %get-tuple-element.13), channel_id=1, source_target_pairs={{1,0},{2,1},{3,2},{4,3},{5,4},{6,5},{7,6},{8,7},{9,8},{10,9},{11,1... | collective-permute-start | bytes 786440 | tf_op jit(solution)/shard_map/ppermute | solution.py:453
  11.6 17.4 %copy-start.5 = (f32[8,128]{1,0:T(8,128)S(1)}, f32[8,128]{1,0:T(8,128)}, u32[]{:S(2)}) copy-start(f32[8,128]{1,0:T(8,128)} %get-tuple-element.14.ids_ref) | copy-start | bytes 12292
  29.2 27.4 %collective-permute-start.2 = (f32[17,2,32,128]{3,2,1,0:T(8,128)S(1)}, f32[17,2,32,128]{3,2,1,0:T(8,128)S(1)}, u32[]{:S(2)}, u32[]{:S(2)}) collective-permute-start(f32[17,2,32,128]{3,2,1,0:T(8,128)S(1)} %get-tuple-element.16), channel_id=1, source_target_pairs={{0,16},{16,32},{32,48},{48,64},{64,80},{80,96},{96,112},{112,128},... | collective-permute-start | bytes 1671176 | tf_op jit(solution)/shard_map/ppermute | solution.py:453
  31.3 25.3 %collective-permute-start.3 = (f32[17,2,32,128]{3,2,1,0:T(8,128)S(1)}, f32[17,2,32,128]{3,2,1,0:T(8,128)S(1)}, u32[]{:S(2)}, u32[]{:S(2)}) collective-permute-start(f32[17,2,32,128]{3,2,1,0:T(8,128)S(1)} %get-tuple-element.17), channel_id=1, source_target_pairs={{16,0},{32,16},{48,32},{64,48},{80,64},{96,80},{112,96},{128,112},... | collective-permute-start | bytes 1671176 | tf_op jit(solution)/shard_map/ppermute | solution.py:453
  33.9 22.7 %copy-start.3 = (s32[4096]{0:T(1024)S(1)}, s32[4096]{0:T(1024)}, u32[]{:S(2)}) copy-start(s32[4096]{0:T(1024)} %own_ref.1) | copy-start | bytes 49156
  33.9 22.7 %copy-start.4 = (s32[4,2048]{1,0:T(4,128)S(1)}, s32[4,2048]{1,0:T(4,128)}, u32[]{:S(2)}) copy-start(s32[4,2048]{1,0:T(4,128)} %free_ref.1) | copy-start | bytes 98308
  65.4 14.2 %copy-start.6 = (f32[8,128]{1,0:T(8,128)}, f32[8,128]{1,0:T(8,128)S(1)}, u32[]{:S(2)}) copy-start(f32[8,128]{1,0:T(8,128)S(1)} %get-tuple-element.21.flag_ref) | copy-start | bytes 12292

commit v10 on v9

--- a/solution.py
+++ b/solution.py
@@ -18,7 +18,7 @@
 YO = 12
 YR = 56
 LANES = 128
-FOLD = 2
+LINE = 4
 GROUP = 32
 PIECE = 4
 BATCH = 4
@@ -38,16 +38,11 @@
 
 
 def lines(nx):
-    return [[4 * y + c for y in range(nx // 4)] for c in range(4)]
+    return [[LINE * y + c for c in range(LINE)] for y in range(nx // LINE)]
 
 
 def sheets(nx, ny):
-    return [[(4 * y + c) * ny + j for c in range(4) for j in range(ny)] for y in range(nx // 4)]
-
-
-def place_of(line, column, ny):
-    y = lax.shift_right_logical(line, 2)
-    return FOLD * ((line & 3) * ny + column) + (y & (FOLD - 1)), lax.div(y, FOLD) * GROUP
+    return [[(LINE * y + c) * ny + j for y in range(nx // LINE) for j in range(ny)] for c in range(LINE)]
 
 
 def first_kernel(
@@ -128,12 +123,11 @@
         ref[LAYERS, 0, cy - 1 : cy, :] = ids_ref[0:1, :]
         ref[LAYERS, 1, cy - 1 : cy, :] = yup_ref[0, 0, LAYERS : LAYERS + 1, :]
         ref[LAYERS + 1, 0, cy - 1 : cy, :] = ydn_ref[0, 0, LAYERS : LAYERS + 1, :]
-    lane = lax.broadcasted_iota(jnp.int32, (FOLD, LANES), 1)
-    table = got_ref[0:FOLD, :]
-    for g in range(1, nx // 4 // FOLD):
-        part = pltpu.roll(got_ref[g * FOLD : (g + 1) * FOLD, :], g * GROUP, 1)
-        table = jnp.where(lane < g * GROUP, table, part)
-    table = jnp.concatenate([table] * (8 // FOLD), axis=0)
+    lane = lax.broadcasted_iota(jnp.int32, (8, LANES), 1)
+    table = jnp.broadcast_to(got_ref[0:1, :], (8, LANES))
+    for c in range(1, LINE):
+        part = pltpu.roll(jnp.broadcast_to(got_ref[c : c + 1, :], (8, LANES)), c * GROUP, 1)
+        table = jnp.where(lane < c * GROUP, table, part)
     for at in range(0, tab_ref.shape[0], 8):
         tab_ref[at : at + 8, :] = table
     for copy in copies:
@@ -243,8 +237,8 @@
     def posted(e):
         place = lax.shift_right_logical(list_s[e], 12)
         owner = lax.shift_right_logical(place, 3)
-        at, first = place_of(lax.div(owner, ny), lax.rem(owner, ny), ny)
-        return at, first, place & 7
+        line, column = lax.div(owner, ny), lax.rem(owner, ny)
+        return lax.div(line, LINE) * ny + column, lax.rem(line, LINE) * GROUP, place & 7
 
     def pick(batch, carry):
         for j in range(BATCH):
@@ -420,9 +414,9 @@
     total = got_ref[0:8, :]
     for at in range(8, got_ref.shape[0], 8):
         total = total + got_ref[at : at + 8, :]
-    total = sum(total[at : at + FOLD] for at in range(0, 8, FOLD))
-    for at in range(0, out_ref.shape[0], FOLD):
-        out_ref[at : at + FOLD, :] = pltpu.roll(total, (LANES - GROUP * (at // FOLD)) % LANES, 1)
+    total = jnp.broadcast_to(jnp.sum(total, axis=0, keepdims=True), (8, LANES))
+    for c in range(LINE):
+        out_ref[c : c + 1, :] = pltpu.roll(total, (LANES - GROUP * c) % LANES, 1)[0:1]
 
 
 def gradient_kernel(got_ref, flag_ref, out_ref):
@@ -455,7 +449,7 @@
     fields = (checkpoint, diffusivity, terminal_adjoint)
     yup, ydn, ids, row = pl.pallas_call(
         functools.partial(first_kernel, cx, cy),
-        out_shape=[shape(cx, 2, 16, LANES)] * 2 + [shape(8, LANES), shape(nx // 4, LANES)],
+        out_shape=[shape(cx, 2, 16, LANES)] * 2 + [shape(8, LANES), shape(LINE, LANES)],
         in_specs=[ANY] * 8,
         out_specs=[VM] * 4,
         scratch_shapes=[
@@ -474,7 +468,7 @@
     )(*fields, owner_map, controls, act_ids, slot_tiles, slot_count)
     yup, ydn = shift(yup, "gy", 1), shift(ydn, "gy", -1)
     line, sheet = lines(nx), sheets(nx, ny)
-    rows = 4 * ny * FOLD
+    rows = nx // LINE * ny
     got = lax.all_to_all(row, "gx", 0, 0, axis_index_groups=line, tiled=True)
     xup, xdn, table = pl.pallas_call(
         functools.partial(second_kernel, cx, cy, nx, ny),
@@ -513,7 +507,7 @@
 
     got = lax.all_to_all(message, AXES, 0, 0, axis_index_groups=sheet, tiled=True)
     part = pl.pallas_call(
-        sum_kernel, out_shape=shape(nx // 4, LANES), in_specs=[VM], out_specs=VM, name="partial_sums"
+        sum_kernel, out_shape=shape(LINE, LANES), in_specs=[VM], out_specs=VM, name="partial_sums"
     )(got)
     got = lax.all_to_all(part, "gx", 0, 0, axis_index_groups=line, tiled=True)
     gradient = pl.pallas_call(

time: 96.9 us -> 108 us (1.11)
  waiting for transfers between devices: 4.2 us -> 9.9 us
  blocking collectives: 63.7 us -> 68.9 us
    all_to_all x1, blocking collectives: 22.7 us -> 30.1 us  [shards(): lax.all_to_all(table, AXES, 0, 0, axis_index_groups=sheet, tiled=True)]
    all_to_all x1, blocking collectives: 13.1 us -> 7.46 us  [shards(): got = lax.all_to_all(row, 'gx', 0, 0, axis_index_groups=line, tiled=True)]
    ppermute x4, waiting for transfers between devices: 4.2 us -> 9.9 us  [shift(): return lax.ppermute(value, axis, pairs)]
    all_to_all x1, blocking collectives: 14.2 us -> 19.5 us  [shards(): lax.all_to_all(message, AXES, 0, 0, axis_index_groups=sheet, tiled=True)]
    all_to_all x1, blocking collectives: 13.7 us -> 11.9 us  [shards(): got = lax.all_to_all(part, 'gx', 0, 0, axis_index_groups=line, tiled=True)]
where the time goes in v10:
time: 108 us; the launch traced here: 107 us
  blocking collectives  68.9 us (64%)
  Pallas kernels  14.4 us (13%)
  starting transfers between devices  12.6 us (12%)
  waiting for transfers between devices  9.9 us (9%)
  between operations  1.43 us (1%)
    all_to_all x1, blocking collectives, shards(): lax.all_to_all(table, AXES, 0, 0, axis_index_groups=sheet, tiled=True)  30.1 us
    all_to_all x1, blocking collectives, shards(): lax.all_to_all(message, AXES, 0, 0, axis_index_groups=sheet, tiled=True)  19.5 us
    ppermute x4, starting transfers between devices, shift(): return lax.ppermute(value, axis, pairs)  12.6 us
    all_to_all x1, blocking collectives, shards(): got = lax.all_to_all(part, 'gx', 0, 0, axis_index_groups=line, tiled=True)  11.9 us
    ppermute x4, waiting for transfers between devices, shift(): return lax.ppermute(value, axis, pairs)  9.9 us
    pallas_call x1, Pallas kernels, shards(): pl.pallas_call(functools.partial(window_kernel, cx, cy, nx, ny), out_shap...  8.95 us
    all_to_all x1, blocking collectives, shards(): got = lax.all_to_all(row, 'gx', 0, 0, axis_index_groups=line, tiled=True)  7.46 us
    pallas_call x1, Pallas kernels, shards(): pl.pallas_call(functools.partial(first_kernel, cx, cy), out_shape=[shape(...  2.28 us
  transfers between devices with their start and end apart: 4, of which 1 were waited for; matrix products, arithmetic and copies ran while one was open for 0% of the time, Pallas kernels for 0%

profile of v10, /device:TPU:1, one launch (start us, length us, event | category | flops | bytes accessed | tf_op | source)
XLA Modules:
  0.0 107.3 jit_solution(4366658010134339459)
XLA Ops:
  1.3 0.0 copy-start
  1.3 0.0 copy-start.1
  1.3 0.0 copy-start.2
  1.3 2.3 %first.1 = (f32[16,2,16,128]{3,2,1,0:T(8,128)}, f32[16,2,16,128]{3,2,1,0:T(8,128)}, f32[8,128]{1,0:T(8,128)}, f32[4,128]{1,0:T(4,128)}) custom-call(f32[16,32,256]{2,1,0:T(8,128)} %ck_ref.5, f32[16,32,256]{2,1,0:T(8,128)} %kp_ref.5, f32[16,32,256]{2,1,0:T(8,128)} %ta_ref.5, s32[4096]{0:T(1024)} %own_ref.1, f32[4,8]{1,0:T(4,128)} %ctl_ref.1, s32[16]{0:T(128)} %act_ref.1, ...), custom_call_target="tpu_custom_call" | custom-call | tf_op jit(solution)/shard_map/first/pallas_call | solution.py:450
  3.6 6.6 %collective-permute-start = (f32[16,2,16,128]{3,2,1,0:T(8,128)}, f32[16,2,16,128]{3,2,1,0:T(8,128)S(1)}, u32[]{:S(2)}, u32[]{:S(2)}) collective-permute-start(f32[16,2,16,128]{3,2,1,0:T(8,128)} %get-tuple-element.12), channel_id=1, source_target_pairs={{0,1},{1,2},{2,3},{3,4},{4,5},{5,6},{6,7},{7,8},{8,9},{9,10},{10,1... | collective-permute-start | bytes 786440 | tf_op jit(solution)/shard_map/ppermute | solution.py:447
  10.2 0.0 copy-start.7
  10.3 1.3 %collective-permute-start.1 = (f32[16,2,16,128]{3,2,1,0:T(8,128)}, f32[16,2,16,128]{3,2,1,0:T(8,128)S(1)}, u32[]{:S(2)}, u32[]{:S(2)}) collective-permute-start(f32[16,2,16,128]{3,2,1,0:T(8,128)} %get-tuple-element.13), channel_id=1, source_target_pairs={{1,0},{2,1},{3,2},{4,3},{5,4},{6,5},{7,6},{8,7},{9,8},{10,9},{11,1... | collective-permute-start | bytes 786440 | tf_op jit(solution)/shard_map/ppermute | solution.py:447
  11.6 0.0 copy-done.7
  11.6 0.0 copy-start.5
  11.6 7.5 %all_to_all.44 = f32[4,1,128]{2,1,0:T(1,128)S(1)} all-to-all(f32[4,1,128]{2,1,0:T(1,128)S(1)} %bitcast.25), channel_id=1, replica_groups={{0,16,32,48},{64,80,96,112},{128,144,160,176},{192,208,224,240},{256,27..., dimensions={0} | all-to-all | bytes 4096 | tf_op jit(solution)/shard_map/all_to_all | solution.py:472
  19.0 0.0 collective-permute-done.yup_ref
  19.0 9.9 %collective-permute-done.1.ydn_ref = f32[16,2,16,128]{3,2,1,0:T(8,128)S(1)} collective-permute-done((f32[16,2,16,128]{3,2,1,0:T(8,128)}, f32[16,2,16,128]{3,2,1,0:T(8,128)S(1)}, u32[]{:S(2)}, u32[]{:S(2)}) %collective-permute-start.1) | collective-permute-done | bytes 262176 | tf_op jit(solution)/shard_map/ppermute | solution.py:447
  28.9 0.0 copy-done
  28.9 0.0 copy-done.1
  28.9 0.0 copy-done.2
  28.9 0.0 copy-done.5
  28.9 0.3 second.1
  29.2 1.9 %collective-permute-start.2 = (f32[17,2,32,128]{3,2,1,0:T(8,128)S(1)}, f32[17,2,32,128]{3,2,1,0:T(8,128)S(1)}, u32[]{:S(2)}, u32[]{:S(2)}) collective-permute-start(f32[17,2,32,128]{3,2,1,0:T(8,128)S(1)} %get-tuple-element.16), channel_id=1, source_target_pairs={{0,16},{16,32},{32,48},{48,64},{64,80},{80,96},{96,112},{112,128},... | collective-permute-start | bytes 1671176 | tf_op jit(solution)/shard_map/ppermute | solution.py:447
  31.2 2.7 %collective-permute-start.3 = (f32[17,2,32,128]{3,2,1,0:T(8,128)S(1)}, f32[17,2,32,128]{3,2,1,0:T(8,128)S(1)}, u32[]{:S(2)}, u32[]{:S(2)}) collective-permute-start(f32[17,2,32,128]{3,2,1,0:T(8,128)S(1)} %get-tuple-element.17), channel_id=1, source_target_pairs={{16,0},{32,16},{48,32},{64,48},{80,64},{96,80},{112,96},{128,112},... | collective-permute-start | bytes 1671176 | tf_op jit(solution)/shard_map/ppermute | solution.py:447
  33.9 0.0 copy-start.3
  33.9 0.0 copy-start.4
  33.9 30.1 %all_to_all.45 = f32[128,1,128]{2,1,0:T(1,128)S(1)} all-to-all(f32[128,1,128]{2,1,0:T(1,128)S(1)} %bitcast.19), channel_id=1, replica_groups={{0,1,2,3,4,5,6,7,8,9,10,11,12,13,14,15,64,65,66,67,68,69,70,71,72,73,74..., dimensions={0} | all-to-all | bytes 131072 | tf_op jit(solution)/shard_map/all_to_all | solution.py:483
  64.0 0.0 collective-permute-done.2.xup_ref
  64.0 0.0 collective-permute-done.3.xdn_ref
  64.0 0.0 copy-done.3
  64.0 0.0 copy-done.4
  64.0 8.9 %window.1 = (f32[16,32,256]{2,1,0:T(8,128)}, f32[128,128]{1,0:T(8,128)S(1)}, f32[8,128]{1,0:T(8,128)S(1)}) custom-call(f32[16,32,256]{2,1,0:T(8,128)S(1)} %copy-done, f32[16,32,256]{2,1,0:T(8,128)S(1)} %copy-done.1, f32[16,32,256]{2,1,0:T(8,128)S(1)} %copy-done.2, f32[16,2,16,128]{3,2,1,0:T(8,128)S(1)} %collective-permute-done.yup_ref, ...), custom_call_target="tpu_custom_call" | custom-call | tf_op jit(solution)/shard_map/window/pallas_call | solution.py:486
  73.0 0.0 copy-start.6
  73.0 19.5 %all_to_all.46 = f32[128,1,128]{2,1,0:T(1,128)} all-to-all(f32[128,1,128]{2,1,0:T(1,128)S(1)} %bitcast.20), channel_id=1, replica_groups={{0,1,2,3,4,5,6,7,8,9,10,11,12,13,14,15,64,65,66,67,68,69,70,71,72,73,74..., dimensions={0} | all-to-all | bytes 131072 | tf_op jit(solution)/shard_map/all_to_all | solution.py:508
  92.5 0.0 copy-done.6
  92.5 1.5 %partial_sums.1 = f32[4,128]{1,0:T(4,128)} custom-call(f32[128,128]{1,0:T(8,128)} %bitcast.22), custom_call_target="tpu_custom_call" | custom-call | tf_op jit(solution)/shard_map/partial_sums/pallas_call | solution.py:509
  94.0 11.9 %all_to_all.47 = f32[4,1,128]{2,1,0:T(1,128)} all-to-all(f32[4,1,128]{2,1,0:T(1,128)} %bitcast.23), channel_id=1, replica_groups={{0,16,32,48},{64,80,96,112},{128,144,160,176},{192,208,224,240},{256,27..., dimensions={0} | all-to-all | bytes 4096 | tf_op jit(solution)/shard_map/all_to_all | solution.py:512
  105.9 1.3 %gradient.1 = f32[4,8]{1,0:T(4,128)} custom-call(f32[4,128]{1,0:T(4,128)} %bitcast.24, f32[8,128]{1,0:T(8,128)} %copy-done.6), custom_call_target="tpu_custom_call" | custom-call | tf_op jit(solution)/shard_map/gradient/pallas_call | solution.py:513
Async XLA Ops:
  1.3 27.7 %copy-start = (f32[16,32,256]{2,1,0:T(8,128)S(1)}, f32[16,32,256]{2,1,0:T(8,128)}, u32[]{:S(2)}) copy-start(f32[16,32,256]{2,1,0:T(8,128)} %ck_ref.5) | copy-start | bytes 1572868
  1.3 27.6 %copy-start.1 = (f32[16,32,256]{2,1,0:T(8,128)S(1)}, f32[16,32,256]{2,1,0:T(8,128)}, u32[]{:S(2)}) copy-start(f32[16,32,256]{2,1,0:T(8,128)} %kp_ref.5) | copy-start | bytes 1572868
  1.3 27.6 %copy-start.2 = (f32[16,32,256]{2,1,0:T(8,128)S(1)}, f32[16,32,256]{2,1,0:T(8,128)}, u32[]{:S(2)}) copy-start(f32[16,32,256]{2,1,0:T(8,128)} %ta_ref.5) | copy-start | bytes 1572868
  3.6 15.4 %collective-permute-start = (f32[16,2,16,128]{3,2,1,0:T(8,128)}, f32[16,2,16,128]{3,2,1,0:T(8,128)S(1)}, u32[]{:S(2)}, u32[]{:S(2)}) collective-permute-start(f32[16,2,16,128]{3,2,1,0:T(8,128)} %get-tuple-element.12), channel_id=1, source_target_pairs={{0,1},{1,2},{2,3},{3,4},{4,5},{5,6},{6,7},{7,8},{8,9},{9,10},{10,1... | collective-permute-start | bytes 786440 | tf_op jit(solution)/shard_map/ppermute | solution.py:447
  10.2 1.3 %copy-start.7 = (f32[4,128]{1,0:T(4,128)S(1)}, f32[4,128]{1,0:T(4,128)}, u32[]{:S(2)}) copy-start(f32[4,128]{1,0:T(4,128)} %get-tuple-element.15) | copy-start | bytes 6148
  10.3 18.7 %collective-permute-start.1 = (f32[16,2,16,128]{3,2,1,0:T(8,128)}, f32[16,2,16,128]{3,2,1,0:T(8,128)S(1)}, u32[]{:S(2)}, u32[]{:S(2)}) collective-permute-start(f32[16,2,16,128]{3,2,1,0:T(8,128)} %get-tuple-element.13), channel_id=1, source_target_pairs={{1,0},{2,1},{3,2},{4,3},{5,4},{6,5},{7,6},{8,7},{9,8},{10,9},{11,1... | collective-permute-start | bytes 786440 | tf_op jit(solution)/shard_map/ppermute | solution.py:447
  11.6 17.4 %copy-start.5 = (f32[8,128]{1,0:T(8,128)S(1)}, f32[8,128]{1,0:T(8,128)}, u32[]{:S(2)}) copy-start(f32[8,128]{1,0:T(8,128)} %get-tuple-element.14.ids_ref) | copy-start | bytes 12292
  29.2 34.8 %collective-permute-start.2 = (f32[17,2,32,128]{3,2,1,0:T(8,128)S(1)}, f32[17,2,32,128]{3,2,1,0:T(8,128)S(1)}, u32[]{:S(2)}, u32[]{:S(2)}) collective-permute-start(f32[17,2,32,128]{3,2,1,0:T(8,128)S(1)} %get-tuple-element.16), channel_id=1, source_target_pairs={{0,16},{16,32},{32,48},{48,64},{64,80},{80,96},{96,112},{112,128},... | collective-permute-start | bytes 1671176 | tf_op jit(solution)/shard_map/ppermute | solution.py:447
  31.2 32.8 %collective-permute-start.3 = (f32[17,2,32,128]{3,2,1,0:T(8,128)S(1)}, f32[17,2,32,128]{3,2,1,0:T(8,128)S(1)}, u32[]{:S(2)}, u32[]{:S(2)}) collective-permute-start(f32[17,2,32,128]{3,2,1,0:T(8,128)S(1)} %get-tuple-element.17), channel_id=1, source_target_pairs={{16,0},{32,16},{48,32},{64,48},{80,64},{96,80},{112,96},{128,112},... | collective-permute-start | bytes 1671176 | tf_op jit(solution)/shard_map/ppermute | solution.py:447
  33.9 30.1 %copy-start.3 = (s32[4096]{0:T(1024)S(1)}, s32[4096]{0:T(1024)}, u32[]{:S(2)}) copy-start(s32[4096]{0:T(1024)} %own_ref.1) | copy-start | bytes 49156
  33.9 30.1 %copy-start.4 = (s32[4,2048]{1,0:T(4,128)S(1)}, s32[4,2048]{1,0:T(4,128)}, u32[]{:S(2)}) copy-start(s32[4,2048]{1,0:T(4,128)} %free_ref.1) | copy-start | bytes 98308
  73.0 19.5 %copy-start.6 = (f32[8,128]{1,0:T(8,128)}, f32[8,128]{1,0:T(8,128)S(1)}, u32[]{:S(2)}) copy-start(f32[8,128]{1,0:T(8,128)S(1)} %get-tuple-element.21.flag_ref) | copy-start | bytes 12292

commit v11 on v9

--- a/solution.py
+++ b/solution.py
@@ -397,6 +397,8 @@
         x, h, y = locate(e)
         for n, adj in enumerate((a1, a2, a3, a4)):
             sum_v[n, pl.ds(e, 1), :] = adj[x, h, pl.ds(y, 1), :]
+        at, first, k = posted(e)
+        which_v[pl.ds(e, 1), :] = jnp.broadcast_to(k, (1, LANES))
         return carry
 
     lax.fori_loop(0, own_total, foot, 0)
@@ -407,22 +409,13 @@
     sum_v[0] = part
 
     def post(e, carry):
-        at, first, k = posted(e)
-        msg_ref[pl.ds(at, 1), :] += sum_v[0, pl.ds(e, 1), :]
+        owner = lax.shift_right_logical(list_s[e], 15)
+        msg_ref[pl.ds(owner, 1), :] += sum_v[0, pl.ds(e, 1), :]
         return carry
 
     lax.fori_loop(0, own_total, post, 0)
     for write in writes:
         write.wait()
-
-
-def sum_kernel(got_ref, out_ref):
-    total = got_ref[0:8, :]
-    for at in range(8, got_ref.shape[0], 8):
-        total = total + got_ref[at : at + 8, :]
-    total = sum(total[at : at + FOLD] for at in range(0, 8, FOLD))
-    for at in range(0, out_ref.shape[0], FOLD):
-        out_ref[at : at + FOLD, :] = pltpu.roll(total, (LANES - GROUP * (at // FOLD)) % LANES, 1)
 
 
 def gradient_kernel(got_ref, flag_ref, out_ref):
@@ -491,7 +484,7 @@
     ext = pltpu.VMEM((cx + 2 * XO, 2, YR, LANES), f32)
     start_adjoint, message, flags = pl.pallas_call(
         functools.partial(window_kernel, cx, cy, nx, ny),
-        out_shape=[shape(cx, cy, cz), shape(rows, LANES), shape(8, LANES)],
+        out_shape=[shape(cx, cy, cz), shape(nx * ny, LANES), shape(8, LANES)],
         in_specs=[VM] * 11,
         out_specs=[ANY, VM, VM],
         scratch_shapes=[ext] * 11
@@ -511,11 +504,7 @@
         name="window",
     )(*fields, yup, ydn, xup, xdn, ids, table, owner_map.reshape(-1, LANES), free_list)
 
-    got = lax.all_to_all(message, AXES, 0, 0, axis_index_groups=sheet, tiled=True)
-    part = pl.pallas_call(
-        sum_kernel, out_shape=shape(nx // 4, LANES), in_specs=[VM], out_specs=VM, name="partial_sums"
-    )(got)
-    got = lax.all_to_all(part, "gx", 0, 0, axis_index_groups=line, tiled=True)
+    got = lax.all_to_all(message, AXES, 0, 0, tiled=True)
     gradient = pl.pallas_call(
         gradient_kernel, out_shape=shape(*controls.shape), in_specs=[VM] * 2, out_specs=VM, name="gradient"
     )(got, flags)

time: 96.9 us -> 97.5 us (level)
  blocking collectives: 63.7 us -> 65.7 us
  Pallas kernels: 14.2 us -> 13.1 us
    all_to_all x2 -> x1, blocking collectives: 27.9 us -> 29.8 us  [shards(): got = lax.all_to_all(message, AXES, 0, 0, tiled=True)]
    pallas_call x1 -> x0, Pallas kernels: 1.52 us -> none  [shards(): pl.pallas_call(sum_kernel, out_shape=shape(nx // 4, LANES), in_specs=[VM]...]
where the time goes in v11:
time: 97.5 us; the launch traced here: 97 us
  blocking collectives  65.7 us (67%)
  Pallas kernels  13.1 us (13%)
  starting transfers between devices  12.6 us (13%)
  waiting for transfers between devices  4.2 us (4%)
  between operations  1.43 us (1%)
    all_to_all x1, blocking collectives, shards(): got = lax.all_to_all(message, AXES, 0, 0, tiled=True)  29.8 us
    all_to_all x1, blocking collectives, shards(): lax.all_to_all(table, AXES, 0, 0, axis_index_groups=sheet, tiled=True)  22.7 us
    all_to_all x1, blocking collectives, shards(): got = lax.all_to_all(row, 'gx', 0, 0, axis_index_groups=line, tiled=True)  13.1 us
    ppermute x4, starting transfers between devices, shift(): return lax.ppermute(value, axis, pairs)  12.6 us
    pallas_call x1, Pallas kernels, shards(): pl.pallas_call(functools.partial(window_kernel, cx, cy, nx, ny), out_shap...  8.85 us
    ppermute x4, waiting for transfers between devices, shift(): return lax.ppermute(value, axis, pairs)  4.2 us
    pallas_call x1, Pallas kernels, shards(): pl.pallas_call(functools.partial(first_kernel, cx, cy), out_shape=[shape(...  2.27 us
  transfers between devices with their start and end apart: 4, of which 1 were waited for; matrix products, arithmetic and copies ran while one was open for 0% of the time, Pallas kernels for 0%

profile of v11, /device:TPU:1, one launch (start us, length us, event | category | flops | bytes accessed | tf_op | source)
XLA Modules:
  0.0 97.0 jit_solution(972468267721531030)
XLA Ops:
  1.3 0.0 copy-start
  1.3 0.0 copy-start.1
  1.3 0.0 copy-start.2
  1.3 2.3 %first.1 = (f32[16,2,16,128]{3,2,1,0:T(8,128)}, f32[16,2,16,128]{3,2,1,0:T(8,128)}, f32[8,128]{1,0:T(8,128)}, f32[8,128]{1,0:T(8,128)}) custom-call(f32[16,32,256]{2,1,0:T(8,128)} %ck_ref.5, f32[16,32,256]{2,1,0:T(8,128)} %kp_ref.5, f32[16,32,256]{2,1,0:T(8,128)} %ta_ref.5, s32[4096]{0:T(1024)} %own_ref.1, f32[4,8]{1,0:T(4,128)} %ctl_ref.1, s32[16]{0:T(128)} %act_ref.1, ...), custom_call_target="tpu_custom_call" | custom-call | tf_op jit(solution)/shard_map/first/pallas_call | solution.py:449
  3.6 0.0 copy-start.7
  3.6 6.6 %collective-permute-start = (f32[16,2,16,128]{3,2,1,0:T(8,128)}, f32[16,2,16,128]{3,2,1,0:T(8,128)S(1)}, u32[]{:S(2)}, u32[]{:S(2)}) collective-permute-start(f32[16,2,16,128]{3,2,1,0:T(8,128)} %get-tuple-element.12), channel_id=1, source_target_pairs={{0,1},{1,2},{2,3},{3,4},{4,5},{5,6},{6,7},{7,8},{8,9},{9,10},{10,1... | collective-permute-start | bytes 786440 | tf_op jit(solution)/shard_map/ppermute | solution.py:446
  10.3 1.3 %collective-permute-start.1 = (f32[16,2,16,128]{3,2,1,0:T(8,128)}, f32[16,2,16,128]{3,2,1,0:T(8,128)S(1)}, u32[]{:S(2)}, u32[]{:S(2)}) collective-permute-start(f32[16,2,16,128]{3,2,1,0:T(8,128)} %get-tuple-element.13), channel_id=1, source_target_pairs={{1,0},{2,1},{3,2},{4,3},{5,4},{6,5},{7,6},{8,7},{9,8},{10,9},{11,1... | collective-permute-start | bytes 786440 | tf_op jit(solution)/shard_map/ppermute | solution.py:446
  11.6 0.0 copy-done.7
  11.6 0.0 copy-start.5
  11.6 13.1 %all_to_all.33 = f32[8,1,128]{2,1,0:T(1,128)S(1)} all-to-all(f32[8,1,128]{2,1,0:T(1,128)S(1)} %bitcast.17), channel_id=1, replica_groups={{0,64,128,192,256,320,384,448},{16,80,144,208,272,336,400,464},{32,96,1..., dimensions={0} | all-to-all | bytes 8192 | tf_op jit(solution)/shard_map/all_to_all | solution.py:471
  24.7 0.0 collective-permute-done.yup_ref
  24.7 4.2 %collective-permute-done.1.ydn_ref = f32[16,2,16,128]{3,2,1,0:T(8,128)S(1)} collective-permute-done((f32[16,2,16,128]{3,2,1,0:T(8,128)}, f32[16,2,16,128]{3,2,1,0:T(8,128)S(1)}, u32[]{:S(2)}, u32[]{:S(2)}) %collective-permute-start.1) | collective-permute-done | bytes 262176 | tf_op jit(solution)/shard_map/ppermute | solution.py:446
  28.9 0.0 copy-done
  28.9 0.0 copy-done.1
  28.9 0.0 copy-done.2
  28.9 0.0 copy-done.5
  28.9 0.3 second.1
  29.2 2.1 %collective-permute-start.2 = (f32[17,2,32,128]{3,2,1,0:T(8,128)S(1)}, f32[17,2,32,128]{3,2,1,0:T(8,128)S(1)}, u32[]{:S(2)}, u32[]{:S(2)}) collective-permute-start(f32[17,2,32,128]{3,2,1,0:T(8,128)S(1)} %get-tuple-element.16), channel_id=1, source_target_pairs={{0,16},{16,32},{32,48},{48,64},{64,80},{80,96},{96,112},{112,128},... | collective-permute-start | bytes 1671176 | tf_op jit(solution)/shard_map/ppermute | solution.py:446
  31.3 2.6 %collective-permute-start.3 = (f32[17,2,32,128]{3,2,1,0:T(8,128)S(1)}, f32[17,2,32,128]{3,2,1,0:T(8,128)S(1)}, u32[]{:S(2)}, u32[]{:S(2)}) collective-permute-start(f32[17,2,32,128]{3,2,1,0:T(8,128)S(1)} %get-tuple-element.17), channel_id=1, source_target_pairs={{16,0},{32,16},{48,32},{64,48},{80,64},{96,80},{112,96},{128,112},... | collective-permute-start | bytes 1671176 | tf_op jit(solution)/shard_map/ppermute | solution.py:446
  33.9 0.0 copy-start.3
  33.9 0.0 copy-start.4
  33.9 22.7 %all_to_all.34 = f32[64,2,128]{2,1,0:T(2,128)S(1)} all-to-all(f32[64,2,128]{2,1,0:T(2,128)S(1)} %bitcast.14), channel_id=1, replica_groups={{0,1,2,3,4,5,6,7,8,9,10,11,12,13,14,15,16,17,18,19,20,21,22,23,24,25,26..., dimensions={0} | all-to-all | bytes 131072 | tf_op jit(solution)/shard_map/all_to_all | solution.py:482
  56.6 0.0 collective-permute-done.2.xup_ref
  56.6 0.0 collective-permute-done.3.xdn_ref
  56.6 0.0 copy-done.3
  56.6 0.0 copy-done.4
  56.6 8.8 %window.1 = (f32[16,32,256]{2,1,0:T(8,128)}, f32[512,128]{1,0:T(8,128)S(1)}, f32[8,128]{1,0:T(8,128)S(1)}) custom-call(f32[16,32,256]{2,1,0:T(8,128)S(1)} %copy-done, f32[16,32,256]{2,1,0:T(8,128)S(1)} %copy-done.1, f32[16,32,256]{2,1,0:T(8,128)S(1)} %copy-done.2, f32[16,2,16,128]{3,2,1,0:T(8,128)S(1)} %collective-permute-done.yup_ref, ...), custom_call_target="tpu_custom_call" | custom-call | tf_op jit(solution)/shard_map/window/pallas_call | solution.py:485
  65.5 0.0 copy-start.6
  65.5 29.8 %all_to_all.35 = f32[512,1,128]{2,1,0:T(1,128)} all-to-all(f32[512,1,128]{2,1,0:T(1,128)S(1)} %bitcast.12), channel_id=1, replica_groups=mesh['gx'=32,'gy'=16] {'gx','gy'}, dimensions={0} | all-to-all | bytes 524288 | tf_op jit(solution)/shard_map/all_to_all | solution.py:507
  95.3 0.0 copy-done.6
  95.3 1.7 %gradient.1 = f32[4,8]{1,0:T(4,128)} custom-call(f32[512,128]{1,0:T(8,128)} %bitcast.16, f32[8,128]{1,0:T(8,128)} %copy-done.6), custom_call_target="tpu_custom_call" | custom-call | tf_op jit(solution)/shard_map/gradient/pallas_call | solution.py:508
Async XLA Ops:
  1.3 27.7 %copy-start = (f32[16,32,256]{2,1,0:T(8,128)S(1)}, f32[16,32,256]{2,1,0:T(8,128)}, u32[]{:S(2)}) copy-start(f32[16,32,256]{2,1,0:T(8,128)} %ck_ref.5) | copy-start | bytes 1572868
  1.3 27.6 %copy-start.1 = (f32[16,32,256]{2,1,0:T(8,128)S(1)}, f32[16,32,256]{2,1,0:T(8,128)}, u32[]{:S(2)}) copy-start(f32[16,32,256]{2,1,0:T(8,128)} %kp_ref.5) | copy-start | bytes 1572868
  1.3 27.6 %copy-start.2 = (f32[16,32,256]{2,1,0:T(8,128)S(1)}, f32[16,32,256]{2,1,0:T(8,128)}, u32[]{:S(2)}) copy-start(f32[16,32,256]{2,1,0:T(8,128)} %ta_ref.5) | copy-start | bytes 1572868
  3.6 8.0 %copy-start.7 = (f32[8,128]{1,0:T(8,128)S(1)}, f32[8,128]{1,0:T(8,128)}, u32[]{:S(2)}) copy-start(f32[8,128]{1,0:T(8,128)} %get-tuple-element.15) | copy-start | bytes 12292
  3.6 21.1 %collective-permute-start = (f32[16,2,16,128]{3,2,1,0:T(8,128)}, f32[16,2,16,128]{3,2,1,0:T(8,128)S(1)}, u32[]{:S(2)}, u32[]{:S(2)}) collective-permute-start(f32[16,2,16,128]{3,2,1,0:T(8,128)} %get-tuple-element.12), channel_id=1, source_target_pairs={{0,1},{1,2},{2,3},{3,4},{4,5},{5,6},{6,7},{7,8},{8,9},{9,10},{10,1... | collective-permute-start | bytes 786440 | tf_op jit(solution)/shard_map/ppermute | solution.py:446
  10.3 18.7 %collective-permute-start.1 = (f32[16,2,16,128]{3,2,1,0:T(8,128)}, f32[16,2,16,128]{3,2,1,0:T(8,128)S(1)}, u32[]{:S(2)}, u32[]{:S(2)}) collective-permute-start(f32[16,2,16,128]{3,2,1,0:T(8,128)} %get-tuple-element.13), channel_id=1, source_target_pairs={{1,0},{2,1},{3,2},{4,3},{5,4},{6,5},{7,6},{8,7},{9,8},{10,9},{11,1... | collective-permute-start | bytes 786440 | tf_op jit(solution)/shard_map/ppermute | solution.py:446
  11.6 17.4 %copy-start.5 = (f32[8,128]{1,0:T(8,128)S(1)}, f32[8,128]{1,0:T(8,128)}, u32[]{:S(2)}) copy-start(f32[8,128]{1,0:T(8,128)} %get-tuple-element.14.ids_ref) | copy-start | bytes 12292
  29.2 27.4 %collective-permute-start.2 = (f32[17,2,32,128]{3,2,1,0:T(8,128)S(1)}, f32[17,2,32,128]{3,2,1,0:T(8,128)S(1)}, u32[]{:S(2)}, u32[]{:S(2)}) collective-permute-start(f32[17,2,32,128]{3,2,1,0:T(8,128)S(1)} %get-tuple-element.16), channel_id=1, source_target_pairs={{0,16},{16,32},{32,48},{48,64},{64,80},{80,96},{96,112},{112,128},... | collective-permute-start | bytes 1671176 | tf_op jit(solution)/shard_map/ppermute | solution.py:446
  31.3 25.3 %collective-permute-start.3 = (f32[17,2,32,128]{3,2,1,0:T(8,128)S(1)}, f32[17,2,32,128]{3,2,1,0:T(8,128)S(1)}, u32[]{:S(2)}, u32[]{:S(2)}) collective-permute-start(f32[17,2,32,128]{3,2,1,0:T(8,128)S(1)} %get-tuple-element.17), channel_id=1, source_target_pairs={{16,0},{32,16},{48,32},{64,48},{80,64},{96,80},{112,96},{128,112},... | collective-permute-start | bytes 1671176 | tf_op jit(solution)/shard_map/ppermute | solution.py:446
  33.9 22.7 %copy-start.3 = (s32[4096]{0:T(1024)S(1)}, s32[4096]{0:T(1024)}, u32[]{:S(2)}) copy-start(s32[4096]{0:T(1024)} %own_ref.1) | copy-start | bytes 49156
  33.9 22.7 %copy-start.4 = (s32[4,2048]{1,0:T(4,128)S(1)}, s32[4,2048]{1,0:T(4,128)}, u32[]{:S(2)}) copy-start(s32[4,2048]{1,0:T(4,128)} %free_ref.1) | copy-start | bytes 98308
  65.5 29.9 %copy-start.6 = (f32[8,128]{1,0:T(8,128)}, f32[8,128]{1,0:T(8,128)S(1)}, u32[]{:S(2)}) copy-start(f32[8,128]{1,0:T(8,128)S(1)} %get-tuple-element.21.flag_ref) | copy-start | bytes 12292
